TPU v7x, 32 devices: a whole 2x2x4 slice. The times are simulated.
32 devices in a mesh: coh: 4 (over z), lat: 4 (over x, core), lon: 2 (over y).
Axes of the slice: x: 2, y: 2, z: 4, core: 2. Of those that a mesh axis runs over, the one named last changes fastest.
Arguments:
- saved_period_abundance: bfloat16 [2, 128, 256, 512], P(None, 'coh', 'lat', 'lon'), may hold values from 0.099609375 to 2
- final_abundance_sensitivity: bfloat16 [128, 256, 512], P('coh', 'lat', 'lon'), may hold values from -6 to 6
- prey_biomass: float32 [2, 256, 512], P(None, 'lat', 'lon'), may hold values from 0.2 to 2
- water_heat_field: float32 [2, 256, 512], P(None, 'lat', 'lon'), may hold values from 10 to 30
- marine_indicator: int32 [256, 512], P('lat', 'lon'), may hold values 0 or 1
- fishing_pressure: float32 [256, 512], P('lat', 'lon'), may hold values from 0.1 to 2
- offspring_yield: float32 [256, 512], P('lat', 'lon'), may hold values from 2 to 20
- death_fraction: float32 [128], P('coh'), may hold values from 0.01 to 0.5
- gear_vulnerability: float32 [128], P('coh'), may hold values from 0.05 to 0.5
- spreading_coefficient: float32 [128], P('coh'), may hold values from 0.02 to 0.12
- directed_drift_rate: float32 [128], P('coh'), may hold values from 0.01 to 0.06
- favoured_thermal_level: float32 [128], P('coh'), may hold values from 12 to 28
- breeding_contribution: float32 [128], P('coh'), may hold values from 0.005 to 0.03
- landing_error_sensitivity: float32 [256, 2, 128], P(('lat', 'lon'), None, 'coh'), may hold values from -6 to 6
- fleet_east_piece: int32 [256, 1], P(('lat', 'lon')), may hold values from 0 to 1; in each aligned block of 32 rows (0 to 31, 32 to 63, ...) at most 16 rows name the same one
- fleet_north_piece: int32 [256], P(('lat', 'lon')), may hold values from 0 to 3
- fleet_area_patch: int32 [256], P(('lat', 'lon')), may hold values from 0 to 31
- fleet_age_bounds: int32 [256, 2], P(('lat', 'lon')), may hold values from 0 to 128, as said below
Outputs:
- density_grad: float32 [128, 256, 512], P('coh', 'lat', 'lon')
- recruit_grad: float32 [256, 512], P('lat', 'lon')
Inputs may be any that keep to these rules, and one draw needn't show every extreme that they name: `fleet_east_piece`: among the rows of one device, at most 16 name the same longitude tile, and some longitude tile is named by exactly 16 of them. `fleet_age_bounds`: in every row the first entry is below the second.
All inputs are finite; a program needn't handle non-finite values. No bound on the sum of `marine_indicator` on one device may be relied on, other than what follows from the above.
Results may differ from a plain program's by a relative error of at most 0.0003.
Values sent between devices are 32-bit elements; how exact they have to be, the bound alone decides.
No kernel may reach another device: no remote copies, remote signals or barrier semaphores. Data moves between devices by JAX's collectives and lax.ppermute only.
A program may use at most 64 MiB of HBM per device.

v0:
```python
import jax
import jax.numpy as jnp
from jax import lax
from jax.sharding import PartitionSpec as P

BY = 16
BX = 32


thermal_tolerance_spread = 4.0
highest = lax.Precision.HIGHEST


def from_root(value, axis, source):
    kept = jnp.where(lax.axis_index(axis) == source, value, 0).astype(value.dtype)
    return lax.psum(kept, axis)


def shifted(block, axis, distance):
    devices = range(lax.axis_size(axis))
    route = [(i - distance, i) for i in devices if i - distance in devices]
    return lax.ppermute(block, axis, route)


def with_halo(x, sides, width):
    for axis, dim in sides:
        devices, length = (lax.axis_size(axis), x.shape[dim])
        up = [(i, (i + 1) % devices) for i in range(devices - 1)]
        down = [(j, i) for i, j in up]
        last = lax.slice_in_dim(x, length - width, length, axis=dim)
        first = lax.slice_in_dim(x, 0, width, axis=dim)
        before = lax.ppermute(last, axis, up)
        after = lax.ppermute(first, axis, down)
        x = jnp.concatenate([before, x, after], axis=dim)
    return x


def views(rimmed):
    return (
        rimmed[..., :-2, 1:-1],
        rimmed[..., 2:, 1:-1],
        rimmed[..., 1:-1, 2:],
        rimmed[..., 1:-1, :-2],
    )


def fold_rows(base, nblocks, pieces):
    values, targets = pieces
    wanted = (base + jnp.arange(nblocks)).astype(jnp.float32)
    onehot = (targets[None, :] == wanted[:, None]).astype(jnp.float32)
    return jnp.dot(onehot, values, precision=highest)


def shards(
    saved_period_abundance,
    final_abundance_sensitivity,
    prey_biomass,
    water_heat_field,
    marine_indicator,
    fishing_pressure,
    offspring_yield,
    death_fraction,
    gear_vulnerability,
    spreading_coefficient,
    directed_drift_rate,
    favoured_thermal_level,
    breeding_contribution,
    landing_error_sensitivity,
    fleet_east_piece,
    fleet_north_piece,
    fleet_area_patch,
    fleet_age_bounds,
):
    months, ages_here, rows_y, rows_x = saved_period_abundance.shape
    coh_pos = lax.axis_index("coh")
    lat_pos = lax.axis_index("lat")
    lon_pos = lax.axis_index("lon")
    lon_count = lax.axis_size("lon")
    total_ages = ages_here * lax.axis_size("coh")
    cohort_age = coh_pos * ages_here + jnp.arange(ages_here)
    maturity = (cohort_age + 1).astype(jnp.float32) / total_ages * breeding_contribution
    sea_field = marine_indicator.astype(jnp.float32)
    row_count = landing_error_sensitivity.shape[0]
    blocks_y = rows_y // BY
    blocks_x = rows_x // BX
    nblocks = blocks_y * blocks_x
    inside = (cohort_age[None, :] >= fleet_age_bounds[:, 0:1]) & (
        cohort_age[None, :] < fleet_age_bounds[:, 1:2]
    )
    masked = (landing_error_sensitivity * inside[:, None, :].astype(jnp.float32)).reshape(
        row_count, months * ages_here
    )
    place_id = (
        (fleet_north_piece * lon_count + fleet_east_piece[:, 0]) * nblocks + fleet_area_patch
    ).astype(jnp.float32)
    block_values = fold_rows(
        (lat_pos * lon_count + lon_pos) * nblocks,
        nblocks,
        (
            lax.all_gather(masked, ("lat", "lon"), axis=0, tiled=True),
            lax.all_gather(place_id, ("lat", "lon"), axis=0, tiled=True),
        ),
    )
    partial_spawn = jnp.stack(
        [
            jnp.tensordot(
                maturity,
                saved_period_abundance[period_counter].astype(jnp.float32),
                axes=1,
                precision=highest,
            )
            for period_counter in range(months)
        ]
    )
    survive = jnp.exp(
        -death_fraction[:, None, None] - gear_vulnerability[:, None, None] * fishing_pressure[None]
    )
    adjoint = final_abundance_sensitivity.astype(jnp.float32)
    grad_recruit = jnp.zeros((rows_y, rows_x), jnp.float32)
    spawn_total = lax.psum(partial_spawn, "coh")
    for period_counter in range(months - 1, -1, -1):
        spawning = spawn_total[period_counter]
        first_plane = from_root(adjoint[0], "coh", 0)
        next_plane = shifted(adjoint[0], "coh", -1)
        extended = jnp.concatenate(
            [
                adjoint[1:],
                next_plane[None],
                prey_biomass[period_counter][None],
                water_heat_field[period_counter][None],
                sea_field[None],
            ],
            axis=0,
        )
        rimmed = with_halo(extended, (("lat", 1), ("lon", 2)), 1)
        later_rim = rimmed[:ages_here]
        forage_rim = rimmed[ages_here]
        thermal_halo_border = rimmed[ages_here + 1]
        sea_rim = rimmed[ages_here + 2]
        thermal_departure = (
            thermal_halo_border[None] - favoured_thermal_level[:, None, None]
        ) / thermal_tolerance_spread
        habitat = sea_rim * forage_rim / (1.0 + thermal_departure * thermal_departure)
        later = later_rim[:, 1:-1, 1:-1]
        habitat_here = habitat[:, 1:-1, 1:-1]
        outflow = jnp.zeros_like(later)
        for sea_next, hab_next, adj_next in zip(views(sea_rim), views(habitat), views(later_rim)):
            flow_rate = (
                sea_field
                * sea_next
                * (
                    spreading_coefficient[:, None, None]
                    + jnp.maximum(
                        directed_drift_rate[:, None, None] * (hab_next - habitat_here), 0.0
                    )
                )
            )
            outflow = outflow + flow_rate * (later - adj_next)
        after_move = later - outflow
        ratio = 1.0 / (1.0 + spawning)
        recruit_term = first_plane * sea_field * offspring_yield * ratio * ratio
        month_values = block_values[
            :, period_counter * ages_here : (period_counter + 1) * ages_here
        ]
        block_grid = month_values.reshape(blocks_y, blocks_x, ages_here).transpose(2, 0, 1)
        spread = jnp.broadcast_to(
            block_grid[:, :, None, :, None], (ages_here, blocks_y, BY, blocks_x, BX)
        )
        adjoint = (
            survive * after_move
            + recruit_term[None] * maturity[:, None, None]
            + gear_vulnerability[:, None, None]
            * fishing_pressure[None]
            * spread.reshape(ages_here, rows_y, rows_x)
        )
        grad_recruit = grad_recruit + first_plane * sea_field * spawning * ratio
    return (adjoint, grad_recruit)


def solution(mesh):
    in_specs = (
        P(None, "coh", "lat", "lon"),
        P("coh", "lat", "lon"),
        P(None, "lat", "lon"),
        P(None, "lat", "lon"),
        P("lat", "lon"),
        P("lat", "lon"),
        P("lat", "lon"),
        P("coh"),
        P("coh"),
        P("coh"),
        P("coh"),
        P("coh"),
        P("coh"),
        P(("lat", "lon"), None, "coh"),
        P(("lat", "lon"), None),
        P(("lat", "lon")),
        P(("lat", "lon")),
        P(("lat", "lon"), None),
    )
    out_specs = (P("coh", "lat", "lon"), P("lat", "lon"))
    return jax.shard_map(shards, mesh=mesh, in_specs=in_specs, out_specs=out_specs, check_vma=False)
```

profile of v0, /device:TPU:1, one launch (start us, length us, event | category | flops | bytes accessed | tf_op | source)
XLA Modules:
  0.0 194.8 jit_solution(5677409577969922918)
XLA Ops:
  10.6 1.7 slice_bitcast_fusion.1
  15.2 1.8 constant_dynamic-update-slice_fusion.1
  17.2 18.0 %all_gather.7 = f32[256,64]{1,0:T(8,128)S(1)} all-gather(f32[32,64]{1,0:T(8,128)S(1)} %reshape.100), channel_id=1, replica_groups=mesh['coh'=4,'lat'=4,'lon'=2] {'lat','lon'}, dimensions={0}, use_global_device_ids=true | all-gather | bytes 73728 | tf_op jit(solution)/shard_map/all_gather | solution.py:100
  36.6 13.3 %all-reduce = f32[256]{0:T(256)S(1)} all-reduce(f32[256]{0:T(256)S(1)} %convert_dynamic-update-slice_fusion), channel_id=1, replica_groups=mesh['coh'=4,'lat'=4,'lon'=2] {'lat','lon'}, use_global_device_ids=true, to_apply=%add | all-reduce | flops 256 | bytes 2048
  50.1 2.2 %collective-permute-start.2 = (f32[35,1,256]{2,1,0:T(1,128)S(1)}, f32[35,1,256]{2,1,0:T(1,128)S(1)}, u32[]{:S(2)}, u32[]{:S(2)}) collective-permute-start(f32[35,1,256]{2,1,0:T(1,128)S(1)} %get-tuple-element.17), channel_id=1, source_target_pairs={{2,0},{4,2},{6,4},{3,1},{5,3},{7,5},{10,8},{12,10},{14,12},{11,9},... | collective-permute-start | bytes 107528 | tf_op jit(solution)/shard_map/ppermute | solution.py:33
  52.4 3.3 %collective-permute-start.1 = (f32[35,1,256]{2,1,0:T(1,128)S(1)}, f32[35,1,256]{2,1,0:T(1,128)S(1)}, u32[]{:S(2)}, u32[]{:S(2)}) collective-permute-start(f32[35,1,256]{2,1,0:T(1,128)S(1)} %get-tuple-element.16), channel_id=1, source_target_pairs={{0,2},{2,4},{4,6},{1,3},{3,5},{5,7},{8,10},{10,12},{12,14},{9,11},... | collective-permute-start | bytes 107528 | tf_op jit(solution)/shard_map/ppermute | solution.py:32
  57.1 1.9 fusion.82
  59.0 1.9 copy.35
  60.9 1.6 collective-permute-start.3
  62.5 1.8 copy.36
  65.8 1.6 slice.258
  67.5 3.9 %broadcast_in_dim.18 = f32[32,4,16,8,32]{4,3,2,1,0:T(8,128)} broadcast(f32[32,4,8]{2,1,0:T(4,128)S(1)} %copy.41), dimensions={0,1,3} | broadcast | bytes 2101248 | tf_op jit(solution)/shard_map/broadcast_in_dim | solution.py:166
  71.5 7.0 %reshape.102 = f32[32,64,256]{2,1,0:T(8,128)} reshape(f32[32,4,16,8,32]{4,3,2,1,0:T(8,128)} %broadcast_in_dim.18) | data formatting | bytes 4194304 | tf_op jit(solution)/shard_map/reshape | solution.py:174
  79.1 1.6 copy.37
  80.7 1.6 copy.38
  86.9 13.5 %fusion.4 = f32[32,64,256]{2,1,0:T(8,128)S(1)} fusion(f32[32,64,256]{2,1,0:T(8,128)} %reshape.102, f32[35,66,1]{2,1,0:T(8,128)} %copy.37, f32[35,1,256]{2,1,0:T(1,128)} %copy-done.12, f32[35,64,256]{2,1,0:T(8,128)} %copy-done, f32[35,1,256]{2,1,0:T(1,128)} %copy-done.14, f32[32,66,258]{2,1,0:T(8,128)S(1)} %add_divide_fusion.1, f32[35,66,1]{2,1,0:T(8,128)} %copy.38, ...), kind=kLoop, calls=%fused_computation.11 | loop fusion | flops 25165824 | bytes 19554992 | tf_op jit(solution)/shard_map/add | solution.py:170
  101.9 1.8 fusion.85
  103.7 3.8 %collective-permute-done.5 = f32[64,256]{1,0:T(8,128)S(1)} collective-permute-done((f32[64,256]{1,0:T(8,128)S(1)}, f32[64,256]{1,0:T(8,128)S(1)}, u32[]{:S(2)}, u32[]{:S(2)}) %collective-permute-start.5) | collective-permute-done | bytes 65568 | tf_op jit(solution)/shard_map/ppermute | solution.py:22
  107.6 2.3 %collective-permute-start.7 = (f32[35,1,256]{2,1,0:T(1,128)S(1)}, f32[35,1,256]{2,1,0:T(1,128)S(1)}, u32[]{:S(2)}, u32[]{:S(2)}) collective-permute-start(f32[35,1,256]{2,1,0:T(1,128)S(1)} %get-tuple-element.15), channel_id=1, source_target_pairs={{2,0},{4,2},{6,4},{3,1},{5,3},{7,5},{10,8},{12,10},{14,12},{11,9},... | collective-permute-start | bytes 107528 | tf_op jit(solution)/shard_map/ppermute | solution.py:33
  109.9 4.6 %collective-permute-start.6 = (f32[35,1,256]{2,1,0:T(1,128)S(1)}, f32[35,1,256]{2,1,0:T(1,128)S(1)}, u32[]{:S(2)}, u32[]{:S(2)}) collective-permute-start(f32[35,1,256]{2,1,0:T(1,128)S(1)} %get-tuple-element.14), channel_id=1, source_target_pairs={{0,2},{2,4},{4,6},{1,3},{3,5},{5,7},{8,10},{10,12},{12,14},{9,11},... | collective-permute-start | bytes 107528 | tf_op jit(solution)/shard_map/ppermute | solution.py:32
  114.6 3.9 %broadcast_in_dim.20 = f32[32,4,16,8,32]{4,3,2,1,0:T(8,128)} broadcast(f32[32,4,8]{2,1,0:T(4,128)S(1)} %copy.48), dimensions={0,1,3} | broadcast | bytes 2101248 | tf_op jit(solution)/shard_map/broadcast_in_dim | solution.py:166
  118.5 7.0 %reshape.104 = f32[32,64,256]{2,1,0:T(8,128)} reshape(f32[32,4,16,8,32]{4,3,2,1,0:T(8,128)} %broadcast_in_dim.20) | data formatting | bytes 4194304 | tf_op jit(solution)/shard_map/reshape | solution.py:174
  125.9 1.9 fusion.81
  127.8 1.8 copy.42
  129.6 4.3 %collective-permute-start.8 = (f32[35,66,1]{1,2,0:T(1,128)S(1)}, f32[35,66,1]{1,2,0:T(1,128)S(1)}, u32[]{:S(2)}, u32[]{:S(2)}) collective-permute-start(f32[35,66,1]{1,2,0:T(1,128)S(1)} %copy.42), channel_id=1, source_target_pairs={{0,1},{2,3},{4,5},{6,7},{8,9},{10,11},{12,13},{14,15},{16,17},{18,... | collective-permute-start | bytes 27728 | tf_op jit(solution)/shard_map/ppermute | solution.py:32
  133.8 1.8 copy.43
  135.6 1.5 collective-permute-start.9
  138.7 1.6 copy.44
  140.3 1.6 copy.45
  145.2 26.1 %all-reduce.5.cloned.1.call-done = f32[64,256]{1,0:T(8,128)} async-done(((f32[64,256]{1,0:T(8,128)}), f32[64,256]{1,0:T(8,128)}) %all-reduce.5.cloned.1.call-update) | async-done | bytes 65552 | tf_op jit(solution)/shard_map/psum | solution.py:16
  171.3 1.9 multiply_add_fusion
  173.3 14.7 %fusion.6 = f32[32,64,256]{2,1,0:T(8,128)} fusion(f32[32,64,256]{2,1,0:T(8,128)} %reshape.104, f32[35,66,1]{2,1,0:T(8,128)} %copy.44, f32[35,1,256]{2,1,0:T(1,128)} %copy-done.11, f32[35,64,256]{2,1,0:T(8,128)} %copy-done.1, f32[35,1,256]{2,1,0:T(1,128)} %copy-done.13, f32[32,66,258]{2,1,0:T(8,128)S(1)} %add_divide_fusion, f32[35,66,1]{2,1,0:T(8,128)} %copy.45, ...), kind=kLoop, calls=%fused_computation.13 | loop fusion | flops 25165824 | bytes 19554992 | tf_op jit(solution)/shard_map/add | solution.py:170
  (133 shorter events, 22.0 us)
Async XLA Ops:
  7.2 78.4 %all-reduce.7.cloned.1.call-start = ((), (), s32[]{:S(2)}) async-start(), calls=%async_computation.1 | async-start | bytes 393216 | tf_op jit(solution)/shard_map/psum | solution.py:16
  8.7 41.2 %collective-permute-start = (f32[64,256]{1,0:T(8,128)S(1)}, f32[64,256]{1,0:T(8,128)S(1)}, u32[]{:S(2)}, u32[]{:S(2)}) collective-permute-start(f32[64,256]{1,0:T(8,128)S(1)} %slice_bitcast_fusion.5), channel_id=1, source_target_pairs={{8,0},{16,8},{24,16},{9,1},{17,9},{25,17},{10,2},{18,10},{26,18},{... | collective-permute-start | bytes 196616 | tf_op jit(solution)/shard_map/ppermute | solution.py:22
  15.0 156.3 %all-reduce.5.cloned.1.call-start = ((), (), s32[]{:S(2)}) async-start(), calls=%async_computation | async-start | bytes 131072 | tf_op jit(solution)/shard_map/psum | solution.py:16
  15.1 20.1 %copy-start.35 = (u32[32]{0:T(128)S(1)}, u32[32]{0:T(128)}, u32[]{:S(2)}) copy-start(u32[32]{0:T(128)} %constant.36) | copy-start | bytes 388
  15.1 21.3 %copy-start.30 = (s32[32]{0:T(128)S(1)}, s32[32]{0:T(128)}, u32[]{:S(2)}) copy-start(s32[32]{0:T(128)} %param.34) | copy-start | bytes 388
  15.1 21.3 %copy-start.31 = (s32[32,1]{0,1:T(1,128)S(1)}, s32[32,1]{0,1:T(1,128)}, u32[]{:S(2)}) copy-start(s32[32,1]{0,1:T(1,128)} %param.32) | copy-start | bytes 388
  15.1 21.3 %copy-start.32 = (s32[32]{0:T(128)S(1)}, s32[32]{0:T(128)}, u32[]{:S(2)}) copy-start(s32[32]{0:T(128)} %param.33) | copy-start | bytes 388
  15.2 34.8 %copy-start.17 = (f32[2,64,256]{2,1,0:T(8,128)S(1)}, f32[2,64,256]{2,1,0:T(8,128)}, u32[]{:S(2)}) copy-start(f32[2,64,256]{2,1,0:T(8,128)} %param.20) | copy-start | bytes 393220
  15.2 34.8 %copy-start.19 = (f32[2,64,256]{2,1,0:T(8,128)S(1)}, f32[2,64,256]{2,1,0:T(8,128)}, u32[]{:S(2)}) copy-start(f32[2,64,256]{2,1,0:T(8,128)} %param.21) | copy-start | bytes 393220
  15.2 34.9 %copy-start.9 = (s32[64,256]{1,0:T(8,128)S(1)}, s32[64,256]{1,0:T(8,128)}, u32[]{:S(2)}) copy-start(s32[64,256]{1,0:T(8,128)} %param.22) | copy-start | bytes 196612
  50.0 7.1 %copy-start.15 = (f32[64,256]{1,0:T(8,128)}, f32[64,256]{1,0:T(8,128)S(1)}, u32[]{:S(2)}) copy-start(f32[64,256]{1,0:T(8,128)S(1)} %collective-permute-done) | copy-start | bytes 196612
  50.1 33.3 %copy-start = (f32[35,64,256]{2,1,0:T(8,128)}, f32[35,64,256]{2,1,0:T(8,128)S(1)}, u32[]{:S(2)}) copy-start(f32[35,64,256]{2,1,0:T(8,128)S(1)} %bitcast_dynamic-update-slice_fusion.1) | copy-start | bytes 6881284
  50.1 5.8 %collective-permute-start.2 = (f32[35,1,256]{2,1,0:T(1,128)S(1)}, f32[35,1,256]{2,1,0:T(1,128)S(1)}, u32[]{:S(2)}, u32[]{:S(2)}) collective-permute-start(f32[35,1,256]{2,1,0:T(1,128)S(1)} %get-tuple-element.17), channel_id=1, source_target_pairs={{2,0},{4,2},{6,4},{3,1},{5,3},{7,5},{10,8},{12,10},{14,12},{11,9},... | collective-permute-start | bytes 107528 | tf_op jit(solution)/shard_map/ppermute | solution.py:33
  52.4 4.4 %collective-permute-start.1 = (f32[35,1,256]{2,1,0:T(1,128)S(1)}, f32[35,1,256]{2,1,0:T(1,128)S(1)}, u32[]{:S(2)}, u32[]{:S(2)}) collective-permute-start(f32[35,1,256]{2,1,0:T(1,128)S(1)} %get-tuple-element.16), channel_id=1, source_target_pairs={{0,2},{2,4},{4,6},{1,3},{3,5},{5,7},{8,10},{10,12},{12,14},{9,11},... | collective-permute-start | bytes 107528 | tf_op jit(solution)/shard_map/ppermute | solution.py:32
  55.9 27.4 %copy-start.12 = (f32[35,1,256]{2,1,0:T(1,128)}, f32[35,1,256]{2,1,0:T(1,128)S(1)}, u32[]{:S(2)}) copy-start(f32[35,1,256]{2,1,0:T(1,128)S(1)} %collective-permute-done.2) | copy-start | bytes 107524
  56.7 26.6 %copy-start.14 = (f32[35,1,256]{2,1,0:T(1,128)}, f32[35,1,256]{2,1,0:T(1,128)S(1)}, u32[]{:S(2)}) copy-start(f32[35,1,256]{2,1,0:T(1,128)S(1)} %collective-permute-done.1) | copy-start | bytes 107524
  60.9 18.2 %collective-permute-start.3 = (f32[35,66,1]{1,2,0:T(1,128)S(1)}, f32[35,66,1]{1,2,0:T(1,128)S(1)}, u32[]{:S(2)}, u32[]{:S(2)}) collective-permute-start(f32[35,66,1]{1,2,0:T(1,128)S(1)} %copy.35), channel_id=1, source_target_pairs={{0,1},{2,3},{4,5},{6,7},{8,9},{10,11},{12,13},{14,15},{16,17},{18,... | collective-permute-start | bytes 27728 | tf_op jit(solution)/shard_map/ppermute | solution.py:32
  64.2 16.5 %collective-permute-start.4 = (f32[35,66,1]{1,2,0:T(1,128)S(1)}, f32[35,66,1]{1,2,0:T(1,128)S(1)}, u32[]{:S(2)}, u32[]{:S(2)}) collective-permute-start(f32[35,66,1]{1,2,0:T(1,128)S(1)} %copy.36), channel_id=1, source_target_pairs={{1,0},{3,2},{5,4},{7,6},{9,8},{11,10},{13,12},{15,14},{17,16},{19,... | collective-permute-start | bytes 27728 | tf_op jit(solution)/shard_map/ppermute | solution.py:33
  100.4 7.1 %copy-start.10 = (s32[64,256]{1,0:T(8,128)S(1)}, s32[64,256]{1,0:T(8,128)}, u32[]{:S(2)}) copy-start(s32[64,256]{1,0:T(8,128)} %param.22) | copy-start | bytes 196612
  100.4 7.0 %collective-permute-start.5 = (f32[64,256]{1,0:T(8,128)S(1)}, f32[64,256]{1,0:T(8,128)S(1)}, u32[]{:S(2)}, u32[]{:S(2)}) collective-permute-start(f32[64,256]{1,0:T(8,128)S(1)} %slice_bitcast_fusion.3), channel_id=1, source_target_pairs={{8,0},{16,8},{24,16},{9,1},{17,9},{25,17},{10,2},{18,10},{26,18},{... | collective-permute-start | bytes 196616 | tf_op jit(solution)/shard_map/ppermute | solution.py:22
  107.4 7.1 %copy-start.16 = (f32[64,256]{1,0:T(8,128)}, f32[64,256]{1,0:T(8,128)S(1)}, u32[]{:S(2)}) copy-start(f32[64,256]{1,0:T(8,128)S(1)} %collective-permute-done.5) | copy-start | bytes 196612
  107.5 35.4 %copy-start.1 = (f32[35,64,256]{2,1,0:T(8,128)}, f32[35,64,256]{2,1,0:T(8,128)S(1)}, u32[]{:S(2)}) copy-start(f32[35,64,256]{2,1,0:T(8,128)S(1)} %bitcast_dynamic-update-slice_fusion) | copy-start | bytes 6881284
  107.6 18.0 %collective-permute-start.7 = (f32[35,1,256]{2,1,0:T(1,128)S(1)}, f32[35,1,256]{2,1,0:T(1,128)S(1)}, u32[]{:S(2)}, u32[]{:S(2)}) collective-permute-start(f32[35,1,256]{2,1,0:T(1,128)S(1)} %get-tuple-element.15), channel_id=1, source_target_pairs={{2,0},{4,2},{6,4},{3,1},{5,3},{7,5},{10,8},{12,10},{14,12},{11,9},... | collective-permute-start | bytes 107528 | tf_op jit(solution)/shard_map/ppermute | solution.py:33
  109.9 15.7 %collective-permute-start.6 = (f32[35,1,256]{2,1,0:T(1,128)S(1)}, f32[35,1,256]{2,1,0:T(1,128)S(1)}, u32[]{:S(2)}, u32[]{:S(2)}) collective-permute-start(f32[35,1,256]{2,1,0:T(1,128)S(1)} %get-tuple-element.14), channel_id=1, source_target_pairs={{0,2},{2,4},{4,6},{1,3},{3,5},{5,7},{8,10},{10,12},{12,14},{9,11},... | collective-permute-start | bytes 107528 | tf_op jit(solution)/shard_map/ppermute | solution.py:32
  125.6 17.4 %copy-start.11 = (f32[35,1,256]{2,1,0:T(1,128)}, f32[35,1,256]{2,1,0:T(1,128)S(1)}, u32[]{:S(2)}) copy-start(f32[35,1,256]{2,1,0:T(1,128)S(1)} %collective-permute-done.7) | copy-start | bytes 107524
  125.6 17.4 %copy-start.13 = (f32[35,1,256]{2,1,0:T(1,128)}, f32[35,1,256]{2,1,0:T(1,128)S(1)}, u32[]{:S(2)}) copy-start(f32[35,1,256]{2,1,0:T(1,128)S(1)} %collective-permute-done.6) | copy-start | bytes 107524
  129.6 9.1 %collective-permute-start.8 = (f32[35,66,1]{1,2,0:T(1,128)S(1)}, f32[35,66,1]{1,2,0:T(1,128)S(1)}, u32[]{:S(2)}, u32[]{:S(2)}) collective-permute-start(f32[35,66,1]{1,2,0:T(1,128)S(1)} %copy.42), channel_id=1, source_target_pairs={{0,1},{2,3},{4,5},{6,7},{8,9},{10,11},{12,13},{14,15},{16,17},{18,... | collective-permute-start | bytes 27728 | tf_op jit(solution)/shard_map/ppermute | solution.py:32
  135.6 4.6 %collective-permute-start.9 = (f32[35,66,1]{1,2,0:T(1,128)S(1)}, f32[35,66,1]{1,2,0:T(1,128)S(1)}, u32[]{:S(2)}, u32[]{:S(2)}) collective-permute-start(f32[35,66,1]{1,2,0:T(1,128)S(1)} %copy.43), channel_id=1, source_target_pairs={{1,0},{3,2},{5,4},{7,6},{9,8},{11,10},{13,12},{15,14},{17,16},{19,... | collective-permute-start | bytes 27728 | tf_op jit(solution)/shard_map/ppermute | solution.py:33
  144.4 28.8 %copy-start.23 = (f32[32]{0:T(128)S(1)}, f32[32]{0:T(128)}, u32[]{:S(2)}) copy-start(f32[32]{0:T(128)} %copy-done.22) | copy-start | bytes 388
  144.4 28.8 %copy-start.24 = (f32[32]{0:T(128)S(1)}, f32[32]{0:T(128)}, u32[]{:S(2)}) copy-start(f32[32]{0:T(128)} %param.28) | copy-start | bytes 388
  144.4 28.9 %copy-start.25 = (f32[32]{0:T(128)S(1)}, f32[32]{0:T(128)}, u32[]{:S(2)}) copy-start(f32[32]{0:T(128)} %param.27) | copy-start | bytes 388
  144.4 28.9 %copy-start.26 = (f32[32]{0:T(128)S(1)}, f32[32]{0:T(128)}, u32[]{:S(2)}) copy-start(f32[32]{0:T(128)} %param.26) | copy-start | bytes 388
  (16 other events, 51.2 us)
Sparse Core Ops, SparseCore 0:
  15.1 36.2 all-reduce.6
  138.8 32.5 all-reduce.4
where the time goes:
time: 198 us; the launch traced here: 195 us
  local copies, waits for them, and re-layouts  48.7 us (25%)
  other arithmetic  42.2 us (21%)
  blocking collectives  31.3 us (16%)
  waiting for transfers between devices  30.8 us (16%)
  starting transfers between devices  24.2 us (12%)
  between operations  15.4 us (8%)
  matrix products  2.12 us (1%)
    add x2, other arithmetic, shards(): survive * after_move + recruit_term[None] * maturity[:, None, None]  28.1 us
    psum x2, waiting for transfers between devices, from_root(): return lax.psum(kept, axis)  26.2 us
    all_gather x1, blocking collectives, shards(): lax.all_gather(masked, ('lat', 'lon'), axis=0, tiled=True)  18 us
    reshape x2, local copies, waits for them, and re-layouts, shards(): spread.reshape(ages_here, rows_y, rows_x)  14.1 us
    ppermute x4, starting transfers between devices, with_halo(): before = lax.ppermute(last, axis, up)  13.8 us
    unnamed x1, blocking collectives  13.3 us
    broadcast_in_dim x2, local copies, waits for them, and re-layouts, shards(): jnp.broadcast_to(block_grid[:, :, None, :, None], (ages_here, blocks_y, B...  7.83 us
    ppermute x4, starting transfers between devices, with_halo(): after = lax.ppermute(first, axis, down)  7.55 us
  transfers between devices with their start and end apart: 12, of which 3 were waited for; matrix products, arithmetic and copies ran while one was open for 28% of the time, Pallas kernels for 0%

commit v1 on v0

v1 whole, which is shorter than its diff:
```python
import functools
import math

import jax
import jax.numpy as jnp
from jax import lax
from jax.experimental import pallas as pl
from jax.experimental.pallas import tpu as pltpu
from jax.sharding import PartitionSpec as P

BY = 16
BX = 32
LANES = 128
SUB = 8
GROUP = 8

f32 = jnp.float32
VMEM = pltpu.MemorySpace.VMEM
SMEM = pltpu.MemorySpace.SMEM
LOG2E = math.log2(math.e)

DEATH, GEAR2, KAPPA, TAU, IDEAL, MAT, GEAR = range(7)


def up_to(value, step):
    return -(-value // step) * step


def whole(memory=VMEM):
    return pl.BlockSpec(memory_space=memory)


def params_of(limit=48):
    return pltpu.CompilerParams(vmem_limit_bytes=limit * 2**20)


def shift(x, axis, distance):
    n = lax.axis_size(axis)
    return lax.ppermute(x, axis, [(i, (i + distance) % n) for i in range(n)])


def swap_edges(ahead, back, both, axis):
    n = lax.axis_size(axis)
    if n == 1:
        return ahead, back
    if n == 2:
        got = shift(both, axis, 1)
        return got, got
    return shift(ahead, axis, 1), shift(back, axis, -1)


def spawn_kernel(months, ages, pos_ref, par_ref, saved_ref, first_ref, out_ref):
    for t in range(months):
        total = saved_ref[t, 0].astype(f32) * par_ref[MAT, 0]
        for a in range(1, ages):
            total = total + saved_ref[t, a].astype(f32) * par_ref[MAT, a]
        out_ref[t] = total
    youngest = (pos_ref[0] == 0).astype(f32)
    out_ref[months] = first_ref[...] * youngest


def spawn_parts(pos, par, saved, first):
    months, ages, rows, cols = saved.shape
    step = 16
    return pl.pallas_call(
        functools.partial(spawn_kernel, months, ages),
        grid=(rows // step,),
        in_specs=[
            whole(SMEM),
            whole(SMEM),
            pl.BlockSpec((months, ages, step, cols), lambda i: (0, 0, i, 0)),
            pl.BlockSpec((step, cols), lambda i: (i, 0)),
        ],
        out_specs=pl.BlockSpec((months + 1, step, cols), lambda i: (0, i, 0)),
        out_shape=jax.ShapeDtypeStruct((months + 1, rows, cols), f32),
        compiler_params=params_of(24),
        name="spawn_parts",
    )(pos, par, saved, first)


def sum_over(x, axis):
    n = lax.axis_size(axis)
    if n & (n - 1):
        return [x] + [shift(x, axis, d) for d in range(1, n)]
    terms = [x]
    reach = 1
    while reach < n:
        mine = functools.reduce(jnp.add, terms)
        terms = [mine, lax.ppermute(mine, axis, [(i, i ^ reach) for i in range(n)])]
        reach *= 2
    return terms


def pack_kernel(months, ages, sizes, fleets, *refs):
    pos_ref, fin_ref, next_ref, sea_ref, prey_ref, heat_ref = refs[:6]
    fleet_refs = refs[6 : 6 + fleets]
    ahead_ref, back_ref, east_ref, west_ref, both_ref, fleet_out, later_ref = refs[6 + fleets :]
    n_coh, n_lat, n_lon = sizes
    rows, cols = next_ref.shape
    keep = (pos_ref[0] < n_coh - 1).astype(f32)
    last = next_ref[...] * keep
    later_ref[...] = last

    count = fleet_refs[0].shape[0]
    half = count * fleets // 2
    for k, ref in enumerate(fleet_refs):
        at = k * count
        if count <= half:
            side, line = divmod(at, half)
            fleet_out[line : line + count, side * LANES : (side + 1) * LANES] = ref[...]
        else:
            fleet_out[0:half, 0:LANES] = ref[0:half, :]
            fleet_out[0:half, LANES : 2 * LANES] = ref[half:, :]

    band = 16
    for a in range(ages):
        if a + 1 < ages:
            top = fin_ref[a + 1, 0:band, :].astype(f32)[0:1]
            bottom = fin_ref[a + 1, rows - band : rows, :].astype(f32)[band - 1 : band]
        else:
            top, bottom = last[0:1], last[rows - 1 : rows]
        back_ref[a : a + 1, :] = top
        ahead_ref[a : a + 1, :] = bottom
    fields = [sea_ref[...].astype(f32)]
    for t in range(months):
        fields += [prey_ref[t], heat_ref[t]]
    for k, field in enumerate(fields):
        back_ref[ages + k : ages + k + 1, :] = field[0:1]
        ahead_ref[ages + k : ages + k + 1, :] = field[rows - 1 : rows]
    blank = jnp.zeros((1, cols), f32)
    start = up_to(ages + len(fields), SUB)
    for k in range(ages + len(fields), start):
        back_ref[k : k + 1, :] = blank
        ahead_ref[k : k + 1, :] = blank
    back_ref[start:, 0 : 2 * LANES] = fleet_out[...]
    ahead_ref[start:, 0 : 2 * LANES] = fleet_out[...]

    lane = lax.broadcasted_iota(jnp.int32, (rows, LANES), 1)
    east = jnp.zeros((rows, LANES), f32)
    west = jnp.zeros((rows, LANES), f32)
    for k in range(ages + len(fields)):
        if k + 1 < ages:
            left = fin_ref[k + 1, :, 0:LANES].astype(f32)
            right = fin_ref[k + 1, :, cols - LANES : cols].astype(f32)
        else:
            plane = last if k + 1 == ages else fields[k - ages]
            left, right = plane[:, 0:LANES], plane[:, cols - LANES : cols]
        west = jnp.where(lane == k, pltpu.roll(left, k, 1) if k else left, west)
        east = jnp.where(lane == k, pltpu.roll(right, k + 1, 1), east)
    east_ref[...] = east
    west_ref[...] = west
    both_ref[...] = jnp.where(pos_ref[2] == 0, east, west)


def pack_edges(sizes, pos, fin, nxt, sea, prey, heat, fleet_blocks):
    ages, rows, cols = fin.shape
    months = prey.shape[0]
    half = len(fleet_blocks) * fleet_blocks[0].shape[0] // 2
    tall = up_to(ages + 1 + 2 * months, SUB) + half
    line = jax.ShapeDtypeStruct((tall, cols), f32)
    column = jax.ShapeDtypeStruct((rows, LANES), f32)
    return pl.pallas_call(
        functools.partial(pack_kernel, months, ages, sizes, len(fleet_blocks)),
        in_specs=[whole(SMEM)] + [whole()] * (5 + len(fleet_blocks)),
        out_specs=[whole()] * 7,
        out_shape=[
            line,
            line,
            column,
            column,
            column,
            jax.ShapeDtypeStruct((half, 2 * LANES), f32),
            jax.ShapeDtypeStruct((rows, cols), f32),
        ],
        compiler_params=params_of(16),
        name="pack_edges",
    )(pos, fin, nxt, sea, prey, heat, *fleet_blocks)


def recruit_kernel(months, month, ages, sizes, terms, *refs):
    pos_ref, parv_ref, sea_ref, yield_ref, nxt_ref = refs[:5]
    term_refs = refs[5 : 5 + terms]
    rest = refs[5 + terms :]
    top_ref, bottom_ref, west_ref, east_ref = rest[:4]
    ahead_out, back_out, east_out, west_out, both_out, recruit_out, last_out = rest[4:]
    n_coh = sizes[0]
    rows, cols = sea_ref.shape
    keep = (pos_ref[0] < n_coh - 1).astype(f32)
    spawning = functools.reduce(jnp.add, [r[month] for r in term_refs])
    first = functools.reduce(jnp.add, [r[months] for r in term_refs])
    ratio = 1.0 / (1.0 + spawning)
    recruit = first * sea_ref[...].astype(f32) * yield_ref[...] * ratio * ratio
    recruit_out[...] = recruit
    mat_next = nxt_ref[rows : rows + 1, :]
    last = (nxt_ref[0:rows, :] + recruit * mat_next) * keep
    last_out[...] = last

    mat_row = parv_ref[MAT : MAT + 1, :]
    down = lax.broadcasted_iota(jnp.int32, (ages, LANES), 0)
    across = lax.broadcasted_iota(jnp.int32, (ages, LANES), 1)
    mat_col = jnp.sum(
        jnp.where(down == across, jnp.broadcast_to(mat_row, (ages, LANES)), 0.0), axis=1, keepdims=True
    )
    for src, dst, row in ((top_ref, back_out, 0), (bottom_ref, ahead_out, rows - 1)):
        full = jnp.concatenate([src[j] for j in range(src.shape[0])], axis=1)
        full = full + recruit[row : row + 1, :] * mat_col
        up = pltpu.roll(full, ages - 1, 0)
        place = lax.broadcasted_iota(jnp.int32, (ages, cols), 0)
        dst[...] = jnp.where(place == ages - 1, last[row : row + 1, :], up)
    lane = lax.broadcasted_iota(jnp.int32, (rows, LANES), 1)
    sides = []
    for src, dst, col in ((west_ref, west_out, 0), (east_ref, east_out, cols - 1)):
        full = src[...] + recruit[:, col : col + 1] * mat_row
        up = pltpu.roll(full, LANES - 1, 1)
        sides.append(jnp.where(lane == ages - 1, last[:, col : col + 1], up))
        dst[...] = sides[-1]
    both_out[...] = jnp.where(pos_ref[2] == 0, sides[1], sides[0])


def recruit_edges(sizes, month, pos, parv, sea, yields, nxt, terms, edges):
    rows, cols = sea.shape
    ages = edges[0].shape[1]
    months = terms[0].shape[0] - 1
    line = jax.ShapeDtypeStruct((ages, cols), f32)
    column = jax.ShapeDtypeStruct((rows, LANES), f32)
    return pl.pallas_call(
        functools.partial(recruit_kernel, months, month, ages, sizes, len(terms)),
        in_specs=[whole(SMEM)] + [whole()] * (4 + len(terms) + 4),
        out_specs=[whole()] * 7,
        out_shape=[line, line, column, column, column] + [jax.ShapeDtypeStruct((rows, cols), f32)] * 2,
        compiler_params=params_of(8),
        name="recruit_edges",
    )(pos, parv, sea, yields, nxt, *terms, *edges)


def habitat_of(forage, heat, ideal, tau):
    off = heat - ideal
    return forage * (tau / (1.0 + off * off))


def month_kernel(cfg, *refs):
    (months, month, ages, sizes, count, later_bf16, with_recruit, last_month, n_fleet, n_terms, n_bcast, edges_out) = cfg
    refs = list(refs)

    def take(n):
        out = refs[:n]
        del refs[:n]
        return out

    pos_ref, par_ref, parv_ref = take(3)
    later_ref, next_ref = take(2)
    own_ahead, own_back, own_east, own_west = take(4)
    from_before, from_after, from_west, from_east = take(4)
    if with_recruit:
        msg_before, msg_after, msg_west, msg_east = take(4)
        (recruit_ref,) = take(1)
    else:
        msg_before, msg_after, msg_west, msg_east = from_before, from_after, from_west, from_east
    sea_ref, prey_ref, heat_ref, fish_ref = take(4)
    fleet_refs = take(n_fleet)
    if last_month:
        (yield_ref,) = take(1)
        term_refs = take(n_terms)
        bcast_refs = take(n_bcast)
        out_ref, grad_ref = take(2)
    elif edges_out:
        out_ref, top_out, bottom_out, west_out, east_out = take(5)
    else:
        (out_ref,) = take(1)
    openv, openh, forage, heat4, rowc, colw, cole, catch = take(8)
    if last_month:
        (final_recruit,) = take(1)

    n_coh, n_lat, n_lon = sizes
    rows, cols = sea_ref.shape
    n_i, n_j = rows // SUB, cols // LANES
    blocks_y, blocks_x = rows // BY, cols // BX
    sea_line, prey_line, heat_line = ages, ages + 1 + 2 * month, ages + 2 + 2 * month
    step = pl.program_id(0)

    @pl.when(step == 0)
    def _():
        sea = sea_ref[...].astype(f32)
        line = lax.broadcasted_iota(jnp.int32, (rows, cols), 0)
        column = lax.broadcasted_iota(jnp.int32, (rows, cols), 1)
        openv[...] = jnp.where(line == rows - 1, 0.0, sea * pltpu.roll(sea, rows - 1, 0))
        openh[...] = jnp.where(column == cols - 1, 0.0, sea * pltpu.roll(sea, cols - 1, 1))
        heat_q = heat_ref[0] * 0.25
        heat4[...] = heat_q
        fields = sea * prey_ref[0]
        forage[...] = fields

        down = lax.broadcasted_iota(jnp.int32, (ages, LANES), 0)
        across = lax.broadcasted_iota(jnp.int32, (ages, LANES), 1)

        def as_column(k):
            row = jnp.broadcast_to(parv_ref[k : k + 1, :], (ages, LANES))
            return jnp.sum(jnp.where(down == across, row, 0.0), axis=1, keepdims=True)

        kappa, tau, ideal = as_column(KAPPA), as_column(TAU), as_column(IDEAL)
        has = [
            (pos_ref[1] > 0).astype(f32),
            (pos_ref[1] < n_lat - 1).astype(f32),
            (pos_ref[2] > 0).astype(f32),
            (pos_ref[2] < n_lon - 1).astype(f32),
        ]
        for k, (row, own, got, msg) in enumerate(
            ((0, own_back, from_before, msg_before), (rows - 1, own_ahead, from_after, msg_after))
        ):
            here = habitat_of(fields[row : row + 1], heat_q[row : row + 1], ideal, tau)
            sea_there = msg[sea_line : sea_line + 1, :]
            there = habitat_of(
                sea_there * msg[prey_line : prey_line + 1, :], msg[heat_line : heat_line + 1, :] * 0.25, ideal, tau
            )
            rate = (sea[row : row + 1] * sea_there * has[k]) * (kappa + jnp.maximum(there - here, 0.0))
            flux = rate * (own[0:ages, :] - got[0:ages, :])
            for j in range(n_j):
                rowc[k, j] = flux[:, j * LANES : (j + 1) * LANES]
        kappa, tau, ideal = parv_ref[KAPPA : KAPPA + 1], parv_ref[TAU : TAU + 1], parv_ref[IDEAL : IDEAL + 1]
        for k, (col, own, got, msg, dst) in enumerate(
            ((0, own_west, from_west, msg_west, colw), (cols - 1, own_east, from_east, msg_east, cole))
        ):
            here = habitat_of(fields[:, col : col + 1], heat_q[:, col : col + 1], ideal, tau)
            sea_there = msg[:, sea_line : sea_line + 1]
            there = habitat_of(
                sea_there * msg[:, prey_line : prey_line + 1], msg[:, heat_line : heat_line + 1] * 0.25, ideal, tau
            )
            rate = (sea[:, col : col + 1] * sea_there * has[2 + k]) * (kappa + jnp.maximum(there - here, 0.0))
            dst[...] = rate * (own[...] - got[...])

        flat = []
        for ref in fleet_refs:
            flat += [ref[:, 0:LANES], ref[:, LANES : 2 * LANES]]
        flat = jnp.concatenate(flat, axis=0)
        names = flat[:, 2 * ages : 2 * ages + 1] if months == 2 else flat[:, months * ages : months * ages + 1]
        turned = flat.T[month * ages : (month + 1) * ages]
        base = ((pos_ref[1] * n_lon + pos_ref[2]) * (blocks_y * blocks_x)).astype(f32)
        block_col = (lax.broadcasted_iota(jnp.int32, (flat.shape[0], cols), 1) // BX).astype(f32)
        gear = as_column(GEAR)
        for by in range(blocks_y):
            named = (block_col == names - (base + by * blocks_x)).astype(f32)
            sums = gear * jnp.dot(turned, named, precision=lax.Precision.HIGHEST, preferred_element_type=f32)
            for j in range(n_j):
                catch[by, j] = sums[:, j * LANES : (j + 1) * LANES]

        if last_month:
            totals = [functools.reduce(jnp.add, [r[t] for r in term_refs]) for t in range(months + 1)]
            own = bcast_refs[0][...]
            wrapped = bcast_refs[1][...]
            first = own * (pos_ref[0] == 0).astype(f32) + wrapped * (pos_ref[0] == n_coh - 1).astype(f32)
            for ref in bcast_refs[2:]:
                first = first + ref[...]
            first = first[0:rows] + recruit_ref[...] * first[rows : rows + 1]
            ratios = [1.0 / (1.0 + totals[t]) for t in range(months)]
            grad_ref[...] = (totals[months] * totals[1] * ratios[1] + first * totals[0] * ratios[0]) * sea
            final_recruit[...] = first * sea * yield_ref[...] * ratios[0] * ratios[0]

    lane = lax.broadcasted_iota(jnp.int32, (SUB, LANES), 1)
    sub = lax.broadcasted_iota(jnp.int32, (SUB, LANES), 0)

    def tile(i, j):
        return slice(i * SUB, (i + 1) * SUB), slice(j * LANES, (j + 1) * LANES)

    def cohort(k, load):
        a = step * count + k
        kappa, tau, ideal = par_ref[KAPPA, a], par_ref[TAU, a], par_ref[IDEAL, a]
        death, gear2 = par_ref[DEATH, a], par_ref[GEAR2, a]
        if last_month:
            mat = par_ref[MAT, a]
        if with_recruit:
            mat_later = par_ref[MAT, a + 1]

        def strip(i):
            adj, hab = [], []
            for j in range(n_j):
                at = tile(i, j)
                value = load(*at)
                if with_recruit and load is not load_next:
                    value = value + recruit_ref[at] * mat_later
                adj.append(value)
                off = heat4[at] - ideal
                hab.append(forage[at] * tau * pl.reciprocal(1.0 + off * off, approx=False))
            return adj, hab, [pltpu.roll(v, SUB - 1, 0) for v in adj], [pltpu.roll(v, SUB - 1, 0) for v in hab]

        now = strip(0)
        above = [jnp.broadcast_to(-rowc[0, j, pl.ds(a, 1), :], (SUB, LANES)) for j in range(n_j)]
        below = [jnp.broadcast_to(rowc[1, j, pl.ds(a, 1), :], (SUB, LANES)) for j in range(n_j)]
        for i in range(n_i):
            after = strip(i + 1) if i + 1 < n_i else now
            adj, hab, adj_up, hab_up = now
            out = [None] * n_j
            for j in range(n_j):
                at = tile(i, j)
                adj_d = jnp.where(sub == SUB - 1, after[2][j], adj_up[j])
                hab_d = jnp.where(sub == SUB - 1, after[3][j], hab_up[j])
                g = hab_d - hab[j]
                d = openv[at] * (adj[j] - adj_d)
                p = jnp.maximum(g, 0.0) + kappa
                f = p * d
                if i == n_i - 1:
                    f = jnp.where(sub == SUB - 1, below[j], f)
                turned = pltpu.roll((p - g) * d, 1, 0)
                out[j] = f - jnp.where(sub == 0, above[j], turned)
                above[j] = turned
            adj_l = [pltpu.roll(v, LANES - 1, 1) for v in adj]
            hab_l = [pltpu.roll(v, LANES - 1, 1) for v in hab]
            flows, backs = [], []
            for j in range(n_j):
                at = tile(i, j)
                if j + 1 < n_j:
                    adj_d = jnp.where(lane == LANES - 1, adj_l[j + 1], adj_l[j])
                    hab_d = jnp.where(lane == LANES - 1, hab_l[j + 1], hab_l[j])
                else:
                    adj_d, hab_d = adj_l[j], hab_l[j]
                g = hab_d - hab[j]
                d = openh[at] * (adj[j] - adj_d)
                p = jnp.maximum(g, 0.0) + kappa
                flows.append(p * d)
                backs.append(pltpu.roll((p - g) * d, 1, 1))
            rs = slice(i * SUB, (i + 1) * SUB)
            edge_e = pltpu.roll(cole[rs, :], (2 * LANES - 1) - a, 1)
            edge_w = pltpu.roll(-colw[rs, :], LANES - a, 1)
            flows[-1] = jnp.where(lane == LANES - 1, edge_e, flows[-1])
            for j in range(n_j):
                at = tile(i, j)
                came = jnp.where(lane == 0, backs[j - 1] if j else edge_w, backs[j])
                moved = adj[j] - (out[j] + flows[j] - came)
                fish = fish_ref[at]
                survive = jnp.exp2(death - gear2 * fish)
                caught = catch[i * SUB // BY, j, pl.ds(a, 1), :]
                value = survive * moved + fish * caught
                if last_month:
                    value = value + final_recruit[at] * mat
                out_ref[(k,) + at] = value
                if edges_out:
                    if i == 0:
                        top_out[j, pl.ds(a, 1), :] = value[0:1]
                    if i == n_i - 1:
                        bottom_out[j, pl.ds(a, 1), :] = value[SUB - 1 : SUB]
                    if j == 0:
                        west_out[rs, :] = jnp.where(lane == a, pltpu.roll(value, a, 1), west_out[rs, :])
                    if j == n_j - 1:
                        east_out[rs, :] = jnp.where(lane == a, pltpu.roll(value, a + 1, 1), east_out[rs, :])
            now = after

    def load_next(ys, xs):
        return next_ref[ys, xs]

    def loader(a):
        def load(ys, xs):
            if later_bf16:
                low = ys.start // 16 * 16
                wide = later_ref[a + 1, low : low + 16, xs].astype(f32)
                return wide[ys.start - low : ys.stop - low]
            return later_ref[a + 1, ys, xs]

        return load

    if count == 1:
        cohort(0, loader(0))
    else:
        if edges_out:
            @pl.when(step == 0)
            def _():
                west_out[...] = jnp.zeros_like(west_out)
                east_out[...] = jnp.zeros_like(east_out)

        final_step = step == ages // count - 1

        def body(k, carry):
            cohort(k, loader(step * count + k))
            return carry

        lax.fori_loop(0, jnp.where(final_step, count - 1, count), body, 0)

        @pl.when(final_step)
        def _():
            cohort(count - 1, load_next)


def month_step(
    sizes, month, months, pos, par, parv, later, nxt, own, got, first_got, recruit, sea, prey, heat, fish,
    fleet_blocks, first_only=False, final=None
):
    ages, rows, cols = later.shape
    later_bf16 = later.dtype == jnp.bfloat16
    with_recruit = recruit is not None
    count = 1 if first_only else GROUP
    last_month = final is not None
    edges_out = not last_month and not first_only
    line = jax.ShapeDtypeStruct((cols // LANES, ages, LANES), f32)
    column = jax.ShapeDtypeStruct((rows, LANES), f32)
    fleet_specs = []
    fleet_args = []
    for block, start in fleet_blocks:
        size = block.shape[0] - start
        fleet_args.append(block)
        fleet_specs.append((start, size))
    operands = [pos, par, parv, later, nxt, *own, *got]
    if with_recruit:
        operands += [*first_got, recruit]
    specs = [whole(SMEM), whole(SMEM)] + [whole()] * (len(operands) - 2)
    operands += [sea, prey, heat, fish]
    one = pl.BlockSpec((1, rows, cols), lambda i: (month, 0, 0))
    specs += [whole(), one, one, whole()]
    operands += fleet_args
    specs += [whole()] * len(fleet_args)
    n_terms = n_bcast = 0
    if last_month:
        yields, terms, bcasts = final
        operands += [yields, *terms, *bcasts]
        specs += [whole()] * (1 + len(terms) + len(bcasts))
        n_terms, n_bcast = len(terms), len(bcasts)
    if first_only:
        out_shape = [jax.ShapeDtypeStruct((1, rows, cols), f32)]
        out_specs = [pl.BlockSpec((1, rows, cols), lambda i: (0, 0, 0))]
        grid = (1,)
    else:
        out_shape = [jax.ShapeDtypeStruct((ages, rows, cols), f32)]
        out_specs = [pl.BlockSpec((count, rows, cols), lambda i: (i, 0, 0))]
        grid = (ages // count,)
    if last_month:
        out_shape.append(jax.ShapeDtypeStruct((rows, cols), f32))
        out_specs.append(whole())
    elif edges_out:
        out_shape += [line, line, column, column]
        out_specs += [whole()] * 4
    scratch = [
        pltpu.VMEM((rows, cols), f32),
        pltpu.VMEM((rows, cols), f32),
        pltpu.VMEM((rows, cols), f32),
        pltpu.VMEM((rows, cols), f32),
        pltpu.VMEM((2, cols // LANES, ages, LANES), f32),
        pltpu.VMEM((rows, LANES), f32),
        pltpu.VMEM((rows, LANES), f32),
        pltpu.VMEM((rows // BY, cols // LANES, ages, LANES), f32),
    ]
    if last_month:
        scratch.append(pltpu.VMEM((rows, cols), f32))
    cfg = (
        months, month, ages, sizes, count, later_bf16, with_recruit, last_month, len(fleet_args), n_terms, n_bcast,
        edges_out,
    )

    def kernel(*refs):
        refs = list(refs)
        at = len(operands) - (0 if not last_month else 1 + n_terms + n_bcast) - len(fleet_args)
        for k, (start, size) in enumerate(fleet_specs):
            if start:
                refs[at + k] = refs[at + k].at[start : start + size]
        month_kernel(cfg, *refs)

    cells = (1 if first_only else ages) * rows * cols
    return pl.pallas_call(
        kernel,
        grid=grid,
        in_specs=specs,
        out_specs=out_specs,
        out_shape=out_shape,
        scratch_shapes=scratch,
        cost_estimate=pl.CostEstimate(flops=60 * cells, bytes_accessed=8 * cells, transcendentals=2 * cells),
        compiler_params=params_of(24),
        name="month_first" if first_only else "month_step",
    )(*operands)


def shards(
    saved,
    fin,
    prey,
    heat,
    sea,
    fish,
    yields,
    death,
    gear,
    kappa,
    tau,
    ideal,
    breeding,
    landing,
    east_piece,
    north_piece,
    patch,
    bounds,
):
    months, ages, rows, cols = saved.shape
    n_coh, n_lat, n_lon = sizes = tuple(lax.axis_size(axis) for axis in ("coh", "lat", "lon"))
    at_coh, at_lat, at_lon = (lax.axis_index(axis) for axis in ("coh", "lat", "lon"))
    pos = jnp.stack([at_coh, at_lat, at_lon]).astype(jnp.int32)
    cohort_age = at_coh * ages + jnp.arange(ages)
    maturity = (cohort_age + 1).astype(f32) / (ages * n_coh) * breeding
    table = jnp.stack([death * -LOG2E, gear * LOG2E, kappa, tau, ideal * 0.25, maturity, gear, gear])
    par = jnp.pad(table, ((0, 0), (0, LANES - ages)))

    nblocks = (rows // BY) * (cols // BX)
    inside = (cohort_age[None, :] >= bounds[:, 0:1]) & (cohort_age[None, :] < bounds[:, 1:2])
    masked = (landing * inside[:, None, :].astype(f32)).reshape(landing.shape[0], months * ages)
    names = ((north_piece * n_lon + east_piece[:, 0]) * nblocks + patch).astype(f32)
    fleet = jnp.concatenate([masked, names[:, None]], axis=1)
    fleet = jnp.pad(fleet, ((0, 0), (0, LANES - fleet.shape[1])))

    first = fin[0].astype(f32)
    nxt = shift(first, "coh", -1)
    fleet_lon = [fleet] + [shift(fleet, "lon", d) for d in range(1, n_lon)]
    terms = sum_over(spawn_parts(pos, par, saved, first), "coh")

    ahead, back, east, west, both, fleet_pack, later_last = pack_edges(
        sizes, pos, fin, nxt, sea, prey, heat, fleet_lon
    )
    from_west, from_east = swap_edges(east, west, both, "lon")
    from_before, from_after = shift(ahead, "lat", 1), shift(back, "lat", -1)
    start = ahead.shape[0] - fleet_pack.shape[0]
    fleet_blocks = [(ahead, start), (from_before, start)]
    if n_lat > 2:
        fleet_blocks.append((from_after, start))
    fleet_blocks += [(shift(fleet_pack, "lat", d), 0) for d in range(2, n_lat - 1)]

    own = (ahead, back, east, west)
    got = first_got = (from_before, from_after, from_west, from_east)
    later, nxt, recruit = fin, later_last, None
    for month in range(months - 1, 0, -1):
        common = (sizes, month, months, pos, par, par, later, nxt, own, got, first_got, recruit, sea, prey, heat, fish)
        (plane,) = month_step(*common, fleet_blocks, first_only=True)
        mat_rows = jnp.broadcast_to(maturity[0], (SUB, cols))
        plane = jnp.concatenate([plane[0], mat_rows], axis=0)
        down = shift(plane, "coh", -1)
        bcasts = [plane, down] + [lax.ppermute(plane, "coh", [(0, j)]) for j in range(1, n_coh - 1)]
        later, *edges = month_step(*common, fleet_blocks)
        ahead, back, east, west, both, recruit, nxt = recruit_edges(
            sizes, month, pos, par, sea, yields, down, terms, edges
        )
        own = (ahead, back, east, west)
        got = (
            shift(ahead, "lat", 1),
            shift(back, "lat", -1),
            *swap_edges(east, west, both, "lon"),
        )
    return tuple(month_step(
        sizes, 0, months, pos, par, par, later, nxt, own, got, first_got, recruit, sea, prey, heat, fish,
        fleet_blocks, final=(yields, terms, bcasts)
    ))


def solution(mesh):
    in_specs = (
        P(None, "coh", "lat", "lon"),
        P("coh", "lat", "lon"),
        P(None, "lat", "lon"),
        P(None, "lat", "lon"),
        P("lat", "lon"),
        P("lat", "lon"),
        P("lat", "lon"),
        P("coh"),
        P("coh"),
        P("coh"),
        P("coh"),
        P("coh"),
        P("coh"),
        P(("lat", "lon"), None, "coh"),
        P(("lat", "lon"), None),
        P(("lat", "lon")),
        P(("lat", "lon")),
        P(("lat", "lon"), None),
    )
    out_specs = (P("coh", "lat", "lon"), P("lat", "lon"))

    return jax.shard_map(shards, mesh=mesh, in_specs=in_specs, out_specs=out_specs, check_vma=False)
```

time: 198 us -> 57.9 us (0.29); the launches traced: 195 us -> 57.7 us
  local copies, waits for them, and re-layouts: 48.7 us -> 2.63 us
  other arithmetic: 42.2 us -> 3.14 us
  blocking collectives: 31.3 us -> 0 us
  waiting for transfers between devices: 30.8 us -> 6.78 us
  Pallas kernels: 0 us -> 23.8 us
  between operations: 15.4 us -> 0.91 us
  starting transfers between devices: 24.2 us -> 20.4 us
  matrix products: 2.12 us -> 0 us
    add x4 -> x2, other arithmetic: 30.1 us -> 0.03 us  [the longest x1 0.02 us: sum_over(): mine = functools.reduce(jnp.add, terms)]
    psum x2 -> x0, waiting for transfers between devices: 26.2 us -> none  [from_root(): return lax.psum(kept, axis)]
    pallas_call x0 -> x6, Pallas kernels: none -> 23.8 us  [the longest x3 20.7 us: month_step(): pl.pallas_call(kernel, grid=grid, in_specs=specs, out_specs=out_specs, ou...]
    all_gather x1 -> x0, blocking collectives: 18 us -> none  [shards(): lax.all_gather(masked, ('lat', 'lon'), axis=0, tiled=True)]
    slice x10 -> x0, local copies, waits for them, and re-layouts: 14.5 us -> none  [the longest x4 7.34 us: with_halo(): first = lax.slice_in_dim(x, 0, width, axis=dim)]
    reshape x3 -> x1, local copies, waits for them, and re-layouts: 14.2 us -> 0.09 us  [shards(): (landing * inside[:, None, :].astype(f32)).reshape(landing.shape[0], mont...]
    unnamed x1 -> x0, blocking collectives: 13.3 us -> none
    broadcast_in_dim x2 -> x1, local copies, waits for them, and re-layouts: 7.83 us -> 0.09 us  [shards(): fleet = jnp.concatenate([masked, names[:, None]], axis=1)]
  transfers between devices with their start and end apart: 12 -> 14, of which waited for: 3 -> 5; matrix products, arithmetic and copies ran while one was open for 28% -> 6% of each run, Pallas kernels for 0% -> 26%
where the time goes in v1:
time: 57.9 us; the launch traced here: 57.7 us
  Pallas kernels  23.8 us (41%)
  starting transfers between devices  20.4 us (35%)
  waiting for transfers between devices  6.78 us (12%)
  other arithmetic  3.14 us (5%)
  local copies, waits for them, and re-layouts  2.63 us (5%)
  between operations  0.91 us (2%)
    pallas_call x3, Pallas kernels, month_step(): pl.pallas_call(kernel, grid=grid, in_specs=specs, out_specs=out_specs, ou...  20.7 us
    ppermute x10, starting transfers between devices, shift(): return lax.ppermute(x, axis, [(i, (i + distance) % n) for i in range(n)])  14.6 us
    ppermute x10, waiting for transfers between devices, shift(): return lax.ppermute(x, axis, [(i, (i + distance) % n) for i in range(n)])  6.77 us
    ppermute x2, starting transfers between devices, shards(): lax.ppermute(plane, 'coh', [(0, j)])  5.04 us
    another operation x3, other arithmetic, shards(): jnp.stack([death * -LOG2E, gear * LOG2E, kappa, tau, ideal * 0.25, maturi...  1.99 us
    unnamed x26, local copies, waits for them, and re-layouts  1.65 us
    pallas_call x1, Pallas kernels, spawn_parts(): pl.pallas_call(functools.partial(spawn_kernel, months, ages), grid=(rows...  1.31 us
  transfers between devices with their start and end apart: 14, of which 5 were waited for; matrix products, arithmetic and copies ran while one was open for 6% of the time, Pallas kernels for 26%

profile of v1, /device:TPU:1, one launch (start us, length us, event | category | flops | bytes accessed | tf_op | source)
XLA Modules:
  0.0 57.7 jit_solution(17722164902412790495)
XLA Ops:
  0.6 0.9 %bitcast_convert_fusion.first_ref = f32[64,256]{1,0:T(8,128)S(1)} fusion(bf16[32,64,256]{2,1,0:T(8,128)(2,1)} %refs_3_.6), kind=kLoop, calls=%fused_computation | loop fusion | flops 16384 | bytes 98304 | tf_op jit(solution)/shard_map/convert_element_type | solution.py:603
  1.5 4.2 %collective-permute-start = (f32[64,256]{1,0:T(8,128)S(1)}, f32[64,256]{1,0:T(8,128)S(1)}, u32[]{:S(2)}, u32[]{:S(2)}) collective-permute-start(f32[64,256]{1,0:T(8,128)S(1)} %bitcast_convert_fusion.first_ref), channel_id=1, source_target_pairs={{0,24},{8,0},{16,8},{24,16},{1,25},{9,1},{17,9},{25,17},{2,26},{10... | collective-permute-start | bytes 196616 | tf_op jit(solution)/shard_map/ppermute | solution.py:39
  5.6 0.7 %multiply_bitcast_fusion.2 = f32[1,32]{1,0:T(1,128)S(1)} fusion(f32[32]{0:T(128)} %param.25), kind=kLoop, calls=%fused_computation.16 | loop fusion | flops 32 | bytes 256 | tf_op jit(solution)/shard_map/stack | solution.py:593
  6.3 0.7 %fusion.2 = f32[1,32]{1,0:T(1,128)S(1)} fusion(f32[32]{0:T(128)} %param.30, s32[]{:T(128)S(6)} %mul.50), kind=kLoop, calls=%fused_computation.17 | loop fusion | flops 160 | bytes 260 | tf_op jit(solution)/shard_map/stack | solution.py:593
  7.0 0.7 %multiply_bitcast_fusion = (f32[1,32]{1,0:T(1,128)S(1)}, f32[1,32]{1,0:T(1,128)S(1)}) fusion(f32[32]{0:T(128)} %param.29, f32[32]{0:T(128)} %param.26), kind=kLoop, calls=%fused_computation.14 | loop fusion | flops 64 | bytes 512 | tf_op jit(solution)/shard_map/stack | solution.py:593
  7.6 0.8 %stack.48 = f32[8,32]{1,0:T(8,128)S(1)} concatenate(f32[1,32]{1,0:T(1,128)S(1)} %multiply_bitcast_fusion.2, f32[1,32]{1,0:T(1,128)S(1)} %get-tuple-element.43, f32[1,32]{1,0:T(1,128)} %bitcast.38, f32[1,32]{1,0:T(1,128)} %bitcast.39, f32[1,32]{1,0:T(1,128)S(1)} %get-tuple-element.42, f32[1,32]{1,0:T(1,128)S(1)} %fusion.2, f32[1,32]{1,0:T(1,128)} %bitcast.35, f32[1,32]{1,0:T(1,128)} %bitcast.36), dimensions={0} | concatenate | bytes 2048 | tf_op jit(solution)/shard_map/stack | solution.py:593
  8.4 0.1 pad_add_fusion.refs_0_.pos_ref
  8.5 1.6 %copy-done.1 = bf16[2,32,64,256]{3,2,1,0:T(8,128)(2,1)S(1)} copy-done((bf16[2,32,64,256]{3,2,1,0:T(8,128)(2,1)S(1)}, bf16[2,32,64,256]{3,2,1,0:T(8,128)(2,1)}, u32[]{:S(2)}) %copy-start.1) | copy-done | bytes 2097176
  10.2 1.3 %spawn_parts.1 = f32[3,64,256]{2,1,0:T(8,128)S(1)} custom-call(s32[3]{0:T(128)S(1)} %pad_add_fusion.refs_0_.pos_ref, f32[8,128]{1,0:T(8,128)S(1)} %pad.9.refs_1_.refs_2_.par_ref, bf16[2,32,64,256]{3,2,1,0:T(8,128)(2,1)S(1)} %copy-done.1, f32[64,256]{1,0:T(8,128)S(1)} %bitcast_convert_fusion.first_ref), custom_call_target="tpu_custom_call" | custom-call | tf_op jit(solution)/shard_map/spawn_parts/pallas_call | solution.py:65
  11.7 0.1 copy.20
  11.8 0.1 reshape.64
  12.0 1.2 %collective-permute-start.1 = (f32[32,128]{1,0:T(8,128)S(1)}, f32[32,128]{1,0:T(8,128)S(1)}, u32[]{:S(2)}, u32[]{:S(2)}) collective-permute-start(f32[32,128]{1,0:T(8,128)S(1)} %select_maximum_fusion.refs_6_), channel_id=1, source_target_pairs={{0,1},{1,0},{2,3},{3,2},{4,5},{5,4},{6,7},{7,6},{8,9},{9,8},{10,11... | collective-permute-start | bytes 49160 | tf_op jit(solution)/shard_map/ppermute | solution.py:39
  13.2 1.3 %collective-permute-done.1.refs_7_ = f32[32,128]{1,0:T(8,128)S(1)} collective-permute-done((f32[32,128]{1,0:T(8,128)S(1)}, f32[32,128]{1,0:T(8,128)S(1)}, u32[]{:S(2)}, u32[]{:S(2)}) %collective-permute-start.1) | collective-permute-done | bytes 16416 | tf_op jit(solution)/shard_map/ppermute | solution.py:39
  14.6 1.0 %pack_edges.1 = (f32[72,256]{1,0:T(8,128)S(1)}, f32[72,256]{1,0:T(8,128)S(1)}, f32[64,128]{1,0:T(8,128)S(1)}, f32[64,128]{1,0:T(8,128)S(1)}, f32[64,128]{1,0:T(8...) custom-call(s32[3]{0:T(128)S(1)} %pad_add_fusion.refs_0_.pos_ref, bf16[32,64,256]{2,1,0:T(8,128)(2,1)S(1)} %copy-done, ...), custom_call_target="tpu_custom_call" | custom-call | tf_op jit(solution)/shard_map/pack_edges/pallas_call | solution.py:162
  15.6 1.3 %collective-permute-start.4 = (f32[64,128]{1,0:T(8,128)S(1)}, f32[64,128]{1,0:T(8,128)S(1)}, u32[]{:S(2)}, u32[]{:S(2)}) collective-permute-start(f32[64,128]{1,0:T(8,128)S(1)} %get-tuple-element.26), channel_id=1, source_target_pairs={{0,1},{1,0},{2,3},{3,2},{4,5},{5,4},{6,7},{7,6},{8,9},{9,8},{10,11... | collective-permute-start | bytes 98312 | tf_op jit(solution)/shard_map/ppermute | solution.py:39
  16.9 1.2 %collective-permute-start.5 = (f32[32,256]{1,0:T(8,128)S(1)}, f32[32,256]{1,0:T(8,128)S(1)}, u32[]{:S(2)}, u32[]{:S(2)}) collective-permute-start(f32[32,256]{1,0:T(8,128)S(1)} %get-tuple-element.27), channel_id=1, source_target_pairs={{0,4},{2,6},{4,0},{6,2},{1,5},{3,7},{5,1},{7,3},{8,12},{10,14},{12... | collective-permute-start | bytes 98312 | tf_op jit(solution)/shard_map/ppermute | solution.py:39
  18.1 2.7 %collective-permute-start.3 = (f32[72,256]{1,0:T(8,128)S(1)}, f32[72,256]{1,0:T(8,128)S(1)}, u32[]{:S(2)}, u32[]{:S(2)}) collective-permute-start(f32[72,256]{1,0:T(8,128)S(1)} %get-tuple-element.23.refs_6_), channel_id=1, source_target_pairs={{0,6},{2,0},{4,2},{6,4},{1,7},{3,1},{5,3},{7,5},{8,14},{10,8},{12,... | collective-permute-start | bytes 221192 | tf_op jit(solution)/shard_map/ppermute | solution.py:39
  20.8 0.1 collective-permute-start.2
  21.0 0.8 %collective-permute-start.8 = (f32[3,64,256]{2,1,0:T(8,128)S(1)}, f32[3,64,256]{2,1,0:T(8,128)S(1)}, u32[]{:S(2)}, u32[]{:S(2)}) collective-permute-start(f32[3,64,256]{2,1,0:T(8,128)S(1)} %add.37.refs_5_.refs_27_), channel_id=1, source_target_pairs={{0,16},{8,24},{16,0},{24,8},{1,17},{9,25},{17,1},{25,9},{2,18},{10... | collective-permute-start | bytes 589832 | tf_op jit(solution)/shard_map/ppermute | solution.py:89
  21.8 2.1 %collective-permute-done.3.refs_10_.refs_19_.refs_14_.refs_24_ = f32[72,256]{1,0:T(8,128)S(1)} collective-permute-done((f32[72,256]{1,0:T(8,128)S(1)}, f32[72,256]{1,0:T(8,128)S(1)}, u32[]{:S(2)}, u32[]{:S(2)}) %collective-permute-start.3) | collective-permute-done | bytes 73760 | tf_op jit(solution)/shard_map/ppermute | solution.py:39
  23.9 1.6 %month_first.1 = f32[1,64,256]{2,1,0:T(8,128)S(1)} custom-call(s32[3]{0:T(128)S(1)} %pad_add_fusion.refs_0_.pos_ref, f32[8,128]{1,0:T(8,128)S(1)} %pad.9.refs_1_.refs_2_.par_ref, f32[8,128]{1,0:T(8,128)S(1)} %pad.9.refs_1_.refs_2_.par_ref, bf16[32,64,256]{2,1,0:T(8,128)(2,1)S(1)} %copy-done, f32[64,256]{1,0:T(8,128)S(1)} %get-tuple-element.21.refs_4_, ...), custom_call_target="tpu_custom_call" | custom-call | flops 983040 | bytes 131072 | tf_op jit(solution)/shard_map/month_first/pallas_call | solution.py:554
  25.5 1.1 %collective-permute-start.6 = (f32[72,256]{1,0:T(8,128)S(1)}, f32[72,256]{1,0:T(8,128)S(1)}, u32[]{:S(2)}, u32[]{:S(2)}) collective-permute-start(f32[72,256]{1,0:T(8,128)S(1)} %concatenate.7.refs_29_), channel_id=1, source_target_pairs={{0,24},{8,0},{16,8},{24,16},{1,25},{9,1},{17,9},{25,17},{2,26},{10... | collective-permute-start | bytes 221192 | tf_op jit(solution)/shard_map/ppermute | solution.py:39
  26.6 3.7 %collective-permute-start.13 = (f32[72,256]{1,0:T(8,128)S(1)}, f32[72,256]{1,0:T(8,128)S(1)}, u32[]{:S(2)}, u32[]{:S(2)}) collective-permute-start(f32[72,256]{1,0:T(8,128)S(1)} %concatenate.7.refs_29_), channel_id=1, source_target_pairs={{0,16},{1,17},{2,18},{3,19},{4,20},{5,21},{6,22},{7,23}} | collective-permute-start | bytes 221192 | tf_op jit(solution)/shard_map/ppermute | solution.py:628
  30.3 1.3 %collective-permute-start.12 = (f32[72,256]{1,0:T(8,128)S(1)}, f32[72,256]{1,0:T(8,128)S(1)}, u32[]{:S(2)}, u32[]{:S(2)}) collective-permute-start(f32[72,256]{1,0:T(8,128)S(1)} %concatenate.7.refs_29_), channel_id=1, source_target_pairs={{0,8},{1,9},{2,10},{3,11},{4,12},{5,13},{6,14},{7,15}} | collective-permute-start | bytes 221192 | tf_op jit(solution)/shard_map/ppermute | solution.py:628
  31.6 10.2 %month_step.2 = (f32[32,64,256]{2,1,0:T(8,128)S(1)}, f32[2,32,128]{2,1,0:T(8,128)S(1)}, f32[2,32,128]{2,1,0:T(8,128)S(1)}, f32[64,128]{1,0:T(8,128)S(1)}, f32[64,128]{1,0:T(8,128)S(1)}) custom-call(s32[3]{0:T(128)S(1)} %pad_add_fusion.refs_0_.pos_ref, f32[8,128]{1,0:T(8,128)S(1)} %pad.9.refs_1_.refs_2_.par_ref, f32[8,128]{1,0:T(8,128)S(1)} %pad.9.refs_1_.refs_2_.par_ref, ...), custom_call_target="tpu_custom_call" | custom-call | flops 31457280 | bytes 4194304 | tf_op jit(solution)/shard_map/month_step/pallas_call | solution.py:554
  41.9 0.8 %recruit_edges.1 = (f32[32,256]{1,0:T(8,128)S(1)}, f32[32,256]{1,0:T(8,128)S(1)}, f32[64,128]{1,0:T(8,128)S(1)}, f32[64,128]{1,0:T(8,128)S(1)}, f32[64,128]{1,0:...) custom-call(s32[3]{0:T(128)S(1)} %pad_add_fusion.refs_0_.pos_ref, f32[8,128]{1,0:T(8,128)S(1)} %pad.9.refs_1_.refs_2_.par_ref, ...), custom_call_target="tpu_custom_call" | custom-call | tf_op jit(solution)/shard_map/recruit_edges/pallas_call | solution.py:226
  42.7 0.3 collective-permute-start.11
  43.0 2.4 %collective-permute-start.9 = (f32[32,256]{1,0:T(8,128)S(1)}, f32[32,256]{1,0:T(8,128)S(1)}, u32[]{:S(2)}, u32[]{:S(2)}) collective-permute-start(f32[32,256]{1,0:T(8,128)S(1)} %get-tuple-element.34.refs_5_), channel_id=1, source_target_pairs={{0,2},{2,4},{4,6},{6,0},{1,3},{3,5},{5,7},{7,1},{8,10},{10,12},{12... | collective-permute-start | bytes 98312 | tf_op jit(solution)/shard_map/ppermute | solution.py:39
  45.4 0.1 collective-permute-done.11.refs_11_.refs_12_
  45.5 0.9 %collective-permute-done.9.refs_9_ = f32[32,256]{1,0:T(8,128)S(1)} collective-permute-done((f32[32,256]{1,0:T(8,128)S(1)}, f32[32,256]{1,0:T(8,128)S(1)}, u32[]{:S(2)}, u32[]{:S(2)}) %collective-permute-start.9) | collective-permute-done | bytes 32800 | tf_op jit(solution)/shard_map/ppermute | solution.py:39
  46.4 2.3 %collective-permute-done.10.refs_10_ = f32[32,256]{1,0:T(8,128)S(1)} collective-permute-done((f32[32,256]{1,0:T(8,128)S(1)}, f32[32,256]{1,0:T(8,128)S(1)}, u32[]{:S(2)}, u32[]{:S(2)}) %collective-permute-start.10) | collective-permute-done | bytes 32800 | tf_op jit(solution)/shard_map/ppermute | solution.py:39
  48.7 8.9 %month_step.3 = (f32[32,64,256]{2,1,0:T(8,128)}, f32[64,256]{1,0:T(8,128)}) custom-call(s32[3]{0:T(128)S(1)} %pad_add_fusion.refs_0_.pos_ref, f32[8,128]{1,0:T(8,128)S(1)} %pad.9.refs_1_.refs_2_.par_ref, f32[8,128]{1,0:T(8,128)S(1)} %pad.9.refs_1_.refs_2_.par_ref, f32[32,64,256]{2,1,0:T(8,128)S(1)} %get-tuple-element.28.refs_3_, ...), custom_call_target="tpu_custom_call" | custom-call | flops 31457280 | bytes 4194304 | tf_op jit(solution)/shard_map/month_step/pallas_call | solution.py:554
  (46 shorter events, 0.4 us)
Async XLA Ops:
  0.6 14.0 %copy-start = (bf16[32,64,256]{2,1,0:T(8,128)(2,1)S(1)}, bf16[32,64,256]{2,1,0:T(8,128)(2,1)}, u32[]{:S(2)}) copy-start(bf16[32,64,256]{2,1,0:T(8,128)(2,1)} %refs_3_.6) | copy-start | bytes 3145732
  1.5 13.1 %collective-permute-start = (f32[64,256]{1,0:T(8,128)S(1)}, f32[64,256]{1,0:T(8,128)S(1)}, u32[]{:S(2)}, u32[]{:S(2)}) collective-permute-start(f32[64,256]{1,0:T(8,128)S(1)} %bitcast_convert_fusion.first_ref), channel_id=1, source_target_pairs={{0,24},{8,0},{16,8},{24,16},{1,25},{9,1},{17,9},{25,17},{2,26},{10... | collective-permute-start | bytes 196616 | tf_op jit(solution)/shard_map/ppermute | solution.py:39
  8.5 1.6 %copy-start.1 = (bf16[2,32,64,256]{3,2,1,0:T(8,128)(2,1)S(1)}, bf16[2,32,64,256]{3,2,1,0:T(8,128)(2,1)}, u32[]{:S(2)}) copy-start(bf16[2,32,64,256]{3,2,1,0:T(8,128)(2,1)} %saved_ref.1) | copy-start | bytes 6291460
  10.1 1.5 %copy-start.8 = (s32[32,2]{0,1:T(2,128)S(1)}, s32[32,2]{0,1:T(2,128)}, u32[]{:S(2)}) copy-start(s32[32,2]{0,1:T(2,128)} %param.35) | copy-start | bytes 772
  10.1 1.6 %copy-start.7 = (f32[32,2,32]{2,1,0:T(2,128)S(1)}, f32[32,2,32]{2,1,0:T(2,128)}, u32[]{:S(2)}) copy-start(f32[32,2,32]{2,1,0:T(2,128)} %param.31) | copy-start | bytes 24580
  10.1 1.6 %copy-start.9 = (s32[32]{0:T(128)S(1)}, s32[32]{0:T(128)}, u32[]{:S(2)}) copy-start(s32[32]{0:T(128)} %param.34) | copy-start | bytes 388
  10.1 1.6 %copy-start.10 = (s32[32,1]{0,1:T(1,128)S(1)}, s32[32,1]{0,1:T(1,128)}, u32[]{:S(2)}) copy-start(s32[32,1]{0,1:T(1,128)} %param.32) | copy-start | bytes 388
  10.1 1.6 %copy-start.11 = (s32[32]{0:T(128)S(1)}, s32[32]{0:T(128)}, u32[]{:S(2)}) copy-start(s32[32]{0:T(128)} %param.33) | copy-start | bytes 388
  10.1 4.5 %copy-start.2 = (f32[2,64,256]{2,1,0:T(8,128)S(1)}, f32[2,64,256]{2,1,0:T(8,128)}, u32[]{:S(2)}) copy-start(f32[2,64,256]{2,1,0:T(8,128)} %refs_19_.1) | copy-start | bytes 393220
  10.1 4.5 %copy-start.3 = (f32[2,64,256]{2,1,0:T(8,128)S(1)}, f32[2,64,256]{2,1,0:T(8,128)}, u32[]{:S(2)}) copy-start(f32[2,64,256]{2,1,0:T(8,128)} %refs_20_.1) | copy-start | bytes 393220
  10.1 4.5 %copy-start.4 = (s32[64,256]{1,0:T(8,128)S(1)}, s32[64,256]{1,0:T(8,128)}, u32[]{:S(2)}) copy-start(s32[64,256]{1,0:T(8,128)} %refs_18_.1) | copy-start | bytes 196612
  10.1 11.6 %copy-start.12 = (f32[32]{0:T(128)S(1)}, f32[32]{0:T(128)}, u32[]{:S(2)}) copy-start(f32[32]{0:T(128)} %param.30) | copy-start | bytes 388
  10.1 13.7 %copy-start.5 = (f32[64,256]{1,0:T(8,128)S(1)}, f32[64,256]{1,0:T(8,128)}, u32[]{:S(2)}) copy-start(f32[64,256]{1,0:T(8,128)} %refs_21_.1) | copy-start | bytes 196612
  11.5 9.5 %collective-permute-start.7 = (f32[3,64,256]{2,1,0:T(8,128)S(1)}, f32[3,64,256]{2,1,0:T(8,128)S(1)}, u32[]{:S(2)}, u32[]{:S(2)}) collective-permute-start(f32[3,64,256]{2,1,0:T(8,128)S(1)} %spawn_parts.1), channel_id=1, source_target_pairs={{0,8},{8,0},{16,24},{24,16},{1,9},{9,1},{17,25},{25,17},{2,10},{10... | collective-permute-start | bytes 589832 | tf_op jit(solution)/shard_map/ppermute | solution.py:89
  12.0 2.6 %collective-permute-start.1 = (f32[32,128]{1,0:T(8,128)S(1)}, f32[32,128]{1,0:T(8,128)S(1)}, u32[]{:S(2)}, u32[]{:S(2)}) collective-permute-start(f32[32,128]{1,0:T(8,128)S(1)} %select_maximum_fusion.refs_6_), channel_id=1, source_target_pairs={{0,1},{1,0},{2,3},{3,2},{4,5},{5,4},{6,7},{7,6},{8,9},{9,8},{10,11... | collective-permute-start | bytes 49160 | tf_op jit(solution)/shard_map/ppermute | solution.py:39
  15.6 6.1 %collective-permute-start.4 = (f32[64,128]{1,0:T(8,128)S(1)}, f32[64,128]{1,0:T(8,128)S(1)}, u32[]{:S(2)}, u32[]{:S(2)}) collective-permute-start(f32[64,128]{1,0:T(8,128)S(1)} %get-tuple-element.26), channel_id=1, source_target_pairs={{0,1},{1,0},{2,3},{3,2},{4,5},{5,4},{6,7},{7,6},{8,9},{9,8},{10,11... | collective-permute-start | bytes 98312 | tf_op jit(solution)/shard_map/ppermute | solution.py:39
  16.9 4.8 %collective-permute-start.5 = (f32[32,256]{1,0:T(8,128)S(1)}, f32[32,256]{1,0:T(8,128)S(1)}, u32[]{:S(2)}, u32[]{:S(2)}) collective-permute-start(f32[32,256]{1,0:T(8,128)S(1)} %get-tuple-element.27), channel_id=1, source_target_pairs={{0,4},{2,6},{4,0},{6,2},{1,5},{3,7},{5,1},{7,3},{8,12},{10,14},{12... | collective-permute-start | bytes 98312 | tf_op jit(solution)/shard_map/ppermute | solution.py:39
  18.1 5.7 %collective-permute-start.3 = (f32[72,256]{1,0:T(8,128)S(1)}, f32[72,256]{1,0:T(8,128)S(1)}, u32[]{:S(2)}, u32[]{:S(2)}) collective-permute-start(f32[72,256]{1,0:T(8,128)S(1)} %get-tuple-element.23.refs_6_), channel_id=1, source_target_pairs={{0,6},{2,0},{4,2},{6,4},{1,7},{3,1},{5,3},{7,5},{8,14},{10,8},{12,... | collective-permute-start | bytes 221192 | tf_op jit(solution)/shard_map/ppermute | solution.py:39
  20.8 3.1 %collective-permute-start.2 = (f32[72,256]{1,0:T(8,128)S(1)}, f32[72,256]{1,0:T(8,128)S(1)}, u32[]{:S(2)}, u32[]{:S(2)}) collective-permute-start(f32[72,256]{1,0:T(8,128)S(1)} %get-tuple-element.22.refs_5_.refs_17_.refs_22_), channel_id=1, source_target_pairs={{0,2},{2,4},{4,6},{6,0},{1,3},{3,5},{5,7},{7,1},{8,10},{10,12},{12... | collective-permute-start | bytes 221192 | tf_op jit(solution)/shard_map/ppermute | solution.py:39
  21.0 20.9 %collective-permute-start.8 = (f32[3,64,256]{2,1,0:T(8,128)S(1)}, f32[3,64,256]{2,1,0:T(8,128)S(1)}, u32[]{:S(2)}, u32[]{:S(2)}) collective-permute-start(f32[3,64,256]{2,1,0:T(8,128)S(1)} %add.37.refs_5_.refs_27_), channel_id=1, source_target_pairs={{0,16},{8,24},{16,0},{24,8},{1,17},{9,25},{17,1},{25,9},{2,18},{10... | collective-permute-start | bytes 589832 | tf_op jit(solution)/shard_map/ppermute | solution.py:89
  23.9 18.0 %copy-start.6 = (f32[64,256]{1,0:T(8,128)S(1)}, f32[64,256]{1,0:T(8,128)}, u32[]{:S(2)}) copy-start(f32[64,256]{1,0:T(8,128)} %refs_26_.1) | copy-start | bytes 196612
  25.5 16.4 %collective-permute-start.6 = (f32[72,256]{1,0:T(8,128)S(1)}, f32[72,256]{1,0:T(8,128)S(1)}, u32[]{:S(2)}, u32[]{:S(2)}) collective-permute-start(f32[72,256]{1,0:T(8,128)S(1)} %concatenate.7.refs_29_), channel_id=1, source_target_pairs={{0,24},{8,0},{16,8},{24,16},{1,25},{9,1},{17,9},{25,17},{2,26},{10... | collective-permute-start | bytes 221192 | tf_op jit(solution)/shard_map/ppermute | solution.py:39
  26.6 18.8 %collective-permute-start.13 = (f32[72,256]{1,0:T(8,128)S(1)}, f32[72,256]{1,0:T(8,128)S(1)}, u32[]{:S(2)}, u32[]{:S(2)}) collective-permute-start(f32[72,256]{1,0:T(8,128)S(1)} %concatenate.7.refs_29_), channel_id=1, source_target_pairs={{0,16},{1,17},{2,18},{3,19},{4,20},{5,21},{6,22},{7,23}} | collective-permute-start | bytes 221192 | tf_op jit(solution)/shard_map/ppermute | solution.py:628
  30.3 15.1 %collective-permute-start.12 = (f32[72,256]{1,0:T(8,128)S(1)}, f32[72,256]{1,0:T(8,128)S(1)}, u32[]{:S(2)}, u32[]{:S(2)}) collective-permute-start(f32[72,256]{1,0:T(8,128)S(1)} %concatenate.7.refs_29_), channel_id=1, source_target_pairs={{0,8},{1,9},{2,10},{3,11},{4,12},{5,13},{6,14},{7,15}} | collective-permute-start | bytes 221192 | tf_op jit(solution)/shard_map/ppermute | solution.py:628
  42.7 2.8 %collective-permute-start.11 = (f32[64,128]{1,0:T(8,128)S(1)}, f32[64,128]{1,0:T(8,128)S(1)}, u32[]{:S(2)}, u32[]{:S(2)}) collective-permute-start(f32[64,128]{1,0:T(8,128)S(1)} %get-tuple-element.38), channel_id=1, source_target_pairs={{0,1},{1,0},{2,3},{3,2},{4,5},{5,4},{6,7},{7,6},{8,9},{9,8},{10,11... | collective-permute-start | bytes 98312 | tf_op jit(solution)/shard_map/ppermute | solution.py:39
  43.0 3.5 %collective-permute-start.9 = (f32[32,256]{1,0:T(8,128)S(1)}, f32[32,256]{1,0:T(8,128)S(1)}, u32[]{:S(2)}, u32[]{:S(2)}) collective-permute-start(f32[32,256]{1,0:T(8,128)S(1)} %get-tuple-element.34.refs_5_), channel_id=1, source_target_pairs={{0,2},{2,4},{4,6},{6,0},{1,3},{3,5},{5,7},{7,1},{8,10},{10,12},{12... | collective-permute-start | bytes 98312 | tf_op jit(solution)/shard_map/ppermute | solution.py:39
  45.4 3.3 %collective-permute-start.10 = (f32[32,256]{1,0:T(8,128)S(1)}, f32[32,256]{1,0:T(8,128)S(1)}, u32[]{:S(2)}, u32[]{:S(2)}) collective-permute-start(f32[32,256]{1,0:T(8,128)S(1)} %get-tuple-element.35.refs_6_), channel_id=1, source_target_pairs={{0,6},{2,0},{4,2},{6,4},{1,7},{3,1},{5,3},{7,5},{8,14},{10,8},{12,... | collective-permute-start | bytes 98312 | tf_op jit(solution)/shard_map/ppermute | solution.py:39

commit v2 on v1

v2 whole, which is shorter than its diff:
```python
import functools
import math

import jax
import jax.numpy as jnp
from jax import lax
from jax.experimental import pallas as pl
from jax.experimental.pallas import tpu as pltpu
from jax.sharding import PartitionSpec as P

BY = 16
BX = 32
LANES = 128
SUB = 8
GROUP = 8
PAIR = 2
SPAWN_MB = 24

f32 = jnp.float32
VMEM = pltpu.MemorySpace.VMEM
SMEM = pltpu.MemorySpace.SMEM
LOG2E = math.log2(math.e)

DEATH, GEAR2, KAPPA, TAU, IDEAL, MAT, GEAR = range(7)


def up_to(value, step):
    return -(-value // step) * step


def whole(memory=VMEM):
    return pl.BlockSpec(memory_space=memory)


def params_of(limit=48):
    return pltpu.CompilerParams(vmem_limit_bytes=limit * 2**20)


def shift(x, axis, distance):
    n = lax.axis_size(axis)
    return lax.ppermute(x, axis, [(i, (i + distance) % n) for i in range(n)])


def swap_edges(ahead, back, both, axis):
    n = lax.axis_size(axis)
    if n == 1:
        return ahead, back
    if n == 2:
        got = shift(both, axis, 1)
        return got, got
    return shift(ahead, axis, 1), shift(back, axis, -1)


def spawn_kernel(months, ages, total_ages, pos_ref, breed_ref, saved_ref, first_ref, _, out_ref):
    mat = [(pos_ref[0] * ages + (a + 1)).astype(f32) / total_ages * breed_ref[a] for a in range(ages)]
    for t in range(months):
        total = saved_ref[t, 0].astype(f32) * mat[0]
        for a in range(1, ages):
            total = total + saved_ref[t, a].astype(f32) * mat[a]
        out_ref[t] = total
    youngest = (pos_ref[0] == 0).astype(f32)
    out_ref[months] = first_ref[...] * youngest


def spawn_parts(pos, breeding, total_ages, saved, first, ahead_of):
    months, ages, rows, cols = saved.shape
    step = 16
    return pl.pallas_call(
        functools.partial(spawn_kernel, months, ages, total_ages),
        grid=(rows // step,),
        in_specs=[
            whole(SMEM),
            whole(SMEM),
            pl.BlockSpec((months, ages, step, cols), lambda i: (0, 0, i, 0)),
            pl.BlockSpec((step, cols), lambda i: (i, 0)),
            pl.BlockSpec(memory_space=pl.ANY),
        ],
        out_specs=pl.BlockSpec((months + 1, step, cols), lambda i: (0, i, 0)),
        out_shape=jax.ShapeDtypeStruct((months + 1, rows, cols), f32),
        compiler_params=params_of(SPAWN_MB),
        name="spawn_parts",
    )(pos, breeding, saved, first, ahead_of)


def add_kernel(a_ref, b_ref, _, out_ref):
    out_ref[...] = a_ref[...] + b_ref[...]


def add_after(a, b, ahead_of):
    return pl.pallas_call(
        add_kernel,
        in_specs=[whole(), whole(), pl.BlockSpec(memory_space=pl.ANY)],
        out_specs=whole(),
        out_shape=jax.ShapeDtypeStruct(a.shape, a.dtype),
        compiler_params=params_of(8),
        name="add_after",
    )(a, b, ahead_of)


def flipped(x, axis, reach):
    return lax.ppermute(x, axis, [(i, i ^ reach) for i in range(lax.axis_size(axis))])


def first_terms(x, axis):
    n = lax.axis_size(axis)
    if n & (n - 1):
        return [x] + [shift(x, axis, d) for d in range(1, n)]
    return [x, flipped(x, axis, 1)] if n > 1 else [x]


def other_terms(terms, axis, ahead_of):
    n = lax.axis_size(axis)
    if n & (n - 1):
        return terms
    reach = 2
    while reach < n:
        mine = add_after(*terms, ahead_of)
        terms = [mine, flipped(mine, axis, reach)]
        reach *= 2
    return terms


def pack_kernel(months, ages, sizes, fleets, *refs):
    pos_ref, fin_ref, next_ref, sea_ref, prey_ref, heat_ref = refs[:6]
    fleet_refs = refs[6 : 6 + fleets]
    death_ref, gear_ref, kappa_ref, tau_ref, ideal_ref, breed_ref = refs[6 + fleets : 12 + fleets]
    ahead_ref, back_ref, east_ref, west_ref, both_ref, fleet_out, later_ref, table_ref = refs[12 + fleets :]
    n_coh, n_lat, n_lon = sizes
    age = lax.broadcasted_iota(jnp.int32, (1, ages), 1) + (pos_ref[0] * ages + 1)
    table_ref[...] = jnp.zeros_like(table_ref)
    table_ref[DEATH : DEATH + 1, 0:ages] = death_ref[...] * -LOG2E
    table_ref[GEAR2 : GEAR2 + 1, 0:ages] = gear_ref[...] * LOG2E
    table_ref[KAPPA : KAPPA + 1, 0:ages] = kappa_ref[...]
    table_ref[TAU : TAU + 1, 0:ages] = tau_ref[...]
    table_ref[IDEAL : IDEAL + 1, 0:ages] = ideal_ref[...] * 0.25
    table_ref[MAT : MAT + 1, 0:ages] = age.astype(f32) / (ages * n_coh) * breed_ref[...]
    table_ref[GEAR : GEAR + 1, 0:ages] = gear_ref[...]
    rows, cols = next_ref.shape
    keep = (pos_ref[0] < n_coh - 1).astype(f32)
    last = next_ref[...] * keep
    later_ref[...] = last

    count = fleet_refs[0].shape[0]
    half = count * fleets // 2
    for k, ref in enumerate(fleet_refs):
        at = k * count
        if count <= half:
            side, line = divmod(at, half)
            fleet_out[line : line + count, side * LANES : (side + 1) * LANES] = ref[...]
        else:
            fleet_out[0:half, 0:LANES] = ref[0:half, :]
            fleet_out[0:half, LANES : 2 * LANES] = ref[half:, :]

    band = 16
    for a in range(ages):
        if a + 1 < ages:
            top = fin_ref[a + 1, 0:band, :].astype(f32)[0:1]
            bottom = fin_ref[a + 1, rows - band : rows, :].astype(f32)[band - 1 : band]
        else:
            top, bottom = last[0:1], last[rows - 1 : rows]
        back_ref[a : a + 1, :] = top
        ahead_ref[a : a + 1, :] = bottom
    fields = [sea_ref[...].astype(f32)]
    for t in range(months):
        fields += [prey_ref[t], heat_ref[t]]
    for k, field in enumerate(fields):
        back_ref[ages + k : ages + k + 1, :] = field[0:1]
        ahead_ref[ages + k : ages + k + 1, :] = field[rows - 1 : rows]
    blank = jnp.zeros((1, cols), f32)
    start = up_to(ages + len(fields), SUB)
    for k in range(ages + len(fields), start):
        back_ref[k : k + 1, :] = blank
        ahead_ref[k : k + 1, :] = blank
    back_ref[start:, 0 : 2 * LANES] = fleet_out[...]
    ahead_ref[start:, 0 : 2 * LANES] = fleet_out[...]

    lane = lax.broadcasted_iota(jnp.int32, (rows, LANES), 1)
    east = jnp.zeros((rows, LANES), f32)
    west = jnp.zeros((rows, LANES), f32)
    for k in range(ages + len(fields)):
        if k + 1 < ages:
            left = fin_ref[k + 1, :, 0:LANES].astype(f32)
            right = fin_ref[k + 1, :, cols - LANES : cols].astype(f32)
        else:
            plane = last if k + 1 == ages else fields[k - ages]
            left, right = plane[:, 0:LANES], plane[:, cols - LANES : cols]
        west = jnp.where(lane == k, pltpu.roll(left, k, 1) if k else left, west)
        east = jnp.where(lane == k, pltpu.roll(right, k + 1, 1), east)
    east_ref[...] = east
    west_ref[...] = west
    both_ref[...] = jnp.where(pos_ref[2] == 0, east, west)


def pack_edges(sizes, pos, fin, nxt, sea, prey, heat, fleet_blocks, rates):
    ages, rows, cols = fin.shape
    months = prey.shape[0]
    half = len(fleet_blocks) * fleet_blocks[0].shape[0] // 2
    tall = up_to(ages + 1 + 2 * months, SUB) + half
    line = jax.ShapeDtypeStruct((tall, cols), f32)
    column = jax.ShapeDtypeStruct((rows, LANES), f32)
    return pl.pallas_call(
        functools.partial(pack_kernel, months, ages, sizes, len(fleet_blocks)),
        in_specs=[whole(SMEM)] + [whole()] * (5 + len(fleet_blocks) + len(rates)),
        out_specs=[whole()] * 8,
        out_shape=[
            line,
            line,
            column,
            column,
            column,
            jax.ShapeDtypeStruct((half, 2 * LANES), f32),
            jax.ShapeDtypeStruct((rows, cols), f32),
            jax.ShapeDtypeStruct((SUB, LANES), f32),
        ],
        compiler_params=params_of(16),
        name="pack_edges",
    )(pos, fin, nxt, sea, prey, heat, *fleet_blocks, *[rate.reshape(1, ages) for rate in rates])


def recruit_kernel(months, month, ages, sizes, terms, *refs):
    pos_ref, parv_ref, sea_ref, yield_ref, nxt_ref = refs[:5]
    term_refs = refs[5 : 5 + terms]
    rest = refs[5 + terms :]
    top_ref, bottom_ref, west_ref, east_ref = rest[:4]
    ahead_out, back_out, east_out, west_out, both_out, recruit_out, last_out = rest[4:]
    n_coh = sizes[0]
    rows, cols = sea_ref.shape
    keep = (pos_ref[0] < n_coh - 1).astype(f32)
    spawning = functools.reduce(jnp.add, [r[month] for r in term_refs])
    first = functools.reduce(jnp.add, [r[months] for r in term_refs])
    ratio = 1.0 / (1.0 + spawning)
    recruit = first * sea_ref[...].astype(f32) * yield_ref[...] * ratio * ratio
    recruit_out[...] = recruit
    mat_next = nxt_ref[rows : rows + 1, :]
    last = (nxt_ref[0:rows, :] + recruit * mat_next) * keep
    last_out[...] = last

    mat_row = parv_ref[MAT : MAT + 1, :]
    down = lax.broadcasted_iota(jnp.int32, (ages, LANES), 0)
    across = lax.broadcasted_iota(jnp.int32, (ages, LANES), 1)
    mat_col = jnp.sum(
        jnp.where(down == across, jnp.broadcast_to(mat_row, (ages, LANES)), 0.0), axis=1, keepdims=True
    )
    for src, dst, row in ((top_ref, back_out, 0), (bottom_ref, ahead_out, rows - 1)):
        full = jnp.concatenate([src[j] for j in range(src.shape[0])], axis=1)
        full = full + recruit[row : row + 1, :] * mat_col
        up = pltpu.roll(full, ages - 1, 0)
        place = lax.broadcasted_iota(jnp.int32, (ages, cols), 0)
        dst[...] = jnp.where(place == ages - 1, last[row : row + 1, :], up)
    lane = lax.broadcasted_iota(jnp.int32, (rows, LANES), 1)
    sides = []
    for src, dst, col in ((west_ref, west_out, 0), (east_ref, east_out, cols - 1)):
        full = src[...] + recruit[:, col : col + 1] * mat_row
        up = pltpu.roll(full, LANES - 1, 1)
        sides.append(jnp.where(lane == ages - 1, last[:, col : col + 1], up))
        dst[...] = sides[-1]
    both_out[...] = jnp.where(pos_ref[2] == 0, sides[1], sides[0])


def recruit_edges(sizes, month, pos, parv, sea, yields, nxt, terms, edges):
    rows, cols = sea.shape
    ages = edges[0].shape[1]
    months = terms[0].shape[0] - 1
    line = jax.ShapeDtypeStruct((ages, cols), f32)
    column = jax.ShapeDtypeStruct((rows, LANES), f32)
    return pl.pallas_call(
        functools.partial(recruit_kernel, months, month, ages, sizes, len(terms)),
        in_specs=[whole(SMEM)] + [whole()] * (4 + len(terms) + 4),
        out_specs=[whole()] * 7,
        out_shape=[line, line, column, column, column] + [jax.ShapeDtypeStruct((rows, cols), f32)] * 2,
        compiler_params=params_of(8),
        name="recruit_edges",
    )(pos, parv, sea, yields, nxt, *terms, *edges)


class Cfg:
    def __init__(self, **kw):
        self.__dict__.update(kw)


def column_of(par_ref, k, ages):
    down = lax.broadcasted_iota(jnp.int32, (ages, LANES), 0)
    across = lax.broadcasted_iota(jnp.int32, (ages, LANES), 1)
    row = jnp.broadcast_to(par_ref[k : k + 1, :], (ages, LANES))
    return jnp.sum(jnp.where(down == across, row, 0.0), axis=1, keepdims=True)


def edge_flux(c, pos_ref, parv_ref, sea_ref, forage_ref, heat4_ref, own, got, msgs, rowc, colw, cole):
    rows, cols, ages = c.rows, c.cols, c.ages
    n_coh, n_lat, n_lon = c.sizes
    own_ahead, own_back, own_east, own_west = own
    from_before, from_after, from_west, from_east = got
    msg_before, msg_after, msg_west, msg_east = msgs
    sea_line, prey_line, heat_line = ages, ages + 1 + 2 * c.month, ages + 2 + 2 * c.month
    kappa, tau, ideal = (column_of(parv_ref, k, ages) for k in (KAPPA, TAU, IDEAL))
    has = [
        (pos_ref[1] > 0).astype(f32),
        (pos_ref[1] < n_lat - 1).astype(f32),
        (pos_ref[2] > 0).astype(f32),
        (pos_ref[2] < n_lon - 1).astype(f32),
    ]
    for k, (row, own, got, msg) in enumerate(
        ((0, own_back, from_before, msg_before), (rows - 1, own_ahead, from_after, msg_after))
    ):
        here = habitat_of(forage_ref[row : row + 1, :], heat4_ref[row : row + 1, :], ideal, tau)
        sea_there = msg[sea_line : sea_line + 1, :]
        there = habitat_of(
            sea_there * msg[prey_line : prey_line + 1, :], msg[heat_line : heat_line + 1, :] * 0.25, ideal, tau
        )
        both = sea_ref[row : row + 1, :].astype(f32) * sea_there * has[k]
        flux = both * (kappa + jnp.maximum(there - here, 0.0)) * (own[0:ages, :] - got[0:ages, :])
        for j in range(cols // LANES):
            rowc[k, j] = flux[:, j * LANES : (j + 1) * LANES]
    kappa, tau, ideal = (parv_ref[k : k + 1, :] for k in (KAPPA, TAU, IDEAL))
    for k, (col, own, got, msg, dst) in enumerate(
        ((0, own_west, from_west, msg_west, colw), (cols - 1, own_east, from_east, msg_east, cole))
    ):
        here = habitat_of(forage_ref[:, col : col + 1], heat4_ref[:, col : col + 1], ideal, tau)
        sea_there = msg[:, sea_line : sea_line + 1]
        there = habitat_of(
            sea_there * msg[:, prey_line : prey_line + 1], msg[:, heat_line : heat_line + 1] * 0.25, ideal, tau
        )
        both = sea_ref[:, col : col + 1].astype(f32) * sea_there * has[2 + k]
        dst[...] = both * (kappa + jnp.maximum(there - here, 0.0)) * (own[...] - got[...])


def advance(c, k, a, par_ref, load, tables, out_ref, recruit=None, lines=None):
    openv, openh, forage, heat4, fish_ref, rowc, colw, cole, catch = tables
    n_i, n_j = c.rows // SUB, c.cols // LANES
    lane = lax.broadcasted_iota(jnp.int32, (SUB, LANES), 1)
    sub = lax.broadcasted_iota(jnp.int32, (SUB, LANES), 0)
    kappa, tau, ideal = par_ref[KAPPA, a], par_ref[TAU, a], par_ref[IDEAL, a]
    death, gear2 = par_ref[DEATH, a], par_ref[GEAR2, a]
    if recruit is not None:
        mat = par_ref[MAT, a]

    def tile(i, j):
        return slice(i * SUB, (i + 1) * SUB), slice(j * LANES, (j + 1) * LANES)

    def strip(i):
        adj, hab = [], []
        for j in range(n_j):
            at = tile(i, j)
            adj.append(load(*at))
            off = heat4[at] - ideal
            hab.append(forage[at] * tau * pl.reciprocal(1.0 + off * off, approx=False))
        return adj, hab, [pltpu.roll(v, SUB - 1, 0) for v in adj], [pltpu.roll(v, SUB - 1, 0) for v in hab]

    now = strip(0)
    above = [jnp.broadcast_to(-rowc[0, j, pl.ds(a, 1), :], (SUB, LANES)) for j in range(n_j)]
    below = [jnp.broadcast_to(rowc[1, j, pl.ds(a, 1), :], (SUB, LANES)) for j in range(n_j)]
    for i in range(n_i):
        after = strip(i + 1) if i + 1 < n_i else now
        adj, hab, adj_up, hab_up = now
        out = [None] * n_j
        for j in range(n_j):
            at = tile(i, j)
            adj_d = jnp.where(sub == SUB - 1, after[2][j], adj_up[j])
            hab_d = jnp.where(sub == SUB - 1, after[3][j], hab_up[j])
            g = hab_d - hab[j]
            d = openv[at] * (adj[j] - adj_d)
            p = jnp.maximum(g, 0.0) + kappa
            f = p * d
            if i == n_i - 1:
                f = jnp.where(sub == SUB - 1, below[j], f)
            turned = pltpu.roll((p - g) * d, 1, 0)
            out[j] = f - jnp.where(sub == 0, above[j], turned)
            above[j] = turned
        adj_l = [pltpu.roll(v, LANES - 1, 1) for v in adj]
        hab_l = [pltpu.roll(v, LANES - 1, 1) for v in hab]
        flows, backs = [], []
        for j in range(n_j):
            at = tile(i, j)
            if j + 1 < n_j:
                adj_d = jnp.where(lane == LANES - 1, adj_l[j + 1], adj_l[j])
                hab_d = jnp.where(lane == LANES - 1, hab_l[j + 1], hab_l[j])
            else:
                adj_d, hab_d = adj_l[j], hab_l[j]
            g = hab_d - hab[j]
            d = openh[at] * (adj[j] - adj_d)
            p = jnp.maximum(g, 0.0) + kappa
            flows.append(p * d)
            backs.append(pltpu.roll((p - g) * d, 1, 1))
        rs = slice(i * SUB, (i + 1) * SUB)
        edge_e = pltpu.roll(cole[rs, :], (2 * LANES - 1) - a, 1)
        edge_w = pltpu.roll(-colw[rs, :], LANES - a, 1)
        flows[-1] = jnp.where(lane == LANES - 1, edge_e, flows[-1])
        for j in range(n_j):
            at = tile(i, j)
            came = jnp.where(lane == 0, backs[j - 1] if j else edge_w, backs[j])
            moved = adj[j] - (out[j] + flows[j] - came)
            fish = fish_ref[at]
            survive = jnp.exp2(death - gear2 * fish)
            caught = catch[i * SUB // BY, j, pl.ds(a, 1), :]
            value = survive * moved + fish * caught
            if recruit is not None:
                value = value + recruit[at] * mat
            out_ref[(k,) + at] = value
            if lines is not None and i == 0:
                lines[0][j, pl.ds(a, 1), :] = value[0:1]
            if lines is not None and i == n_i - 1:
                lines[1][j, pl.ds(a, 1), :] = value[SUB - 1 : SUB]
        now = after


def read_plane(ref, k, ys, xs):
    if ref.dtype == f32:
        return ref[k, ys, xs]
    low = ys.start // 16 * 16
    wide = ref[k, low : low + 16, xs].astype(f32)
    return wide[ys.start - low : ys.stop - low]


def all_cohorts(c, step, count, par_ref, later_ref, next_ref, recruit_ref, go):
    def loader(a):
        def load(ys, xs):
            value = read_plane(later_ref, a + 1, ys, xs)
            if recruit_ref is not None:
                value = value + recruit_ref[ys, xs] * par_ref[MAT, a + 1]
            return value

        return load

    def body(h, carry):
        for k in range(PAIR):
            go(h * PAIR + k, step * count + h * PAIR + k, loader(step * count + h * PAIR + k))
        return carry

    final = step == c.ages // count - 1
    turns = count // PAIR
    lax.fori_loop(0, jnp.where(final, turns - 1, turns) if c.ages > count else turns - 1, body, 0)

    def rest():
        for k in range(count - PAIR, count):
            a = c.ages - count + k
            go(k, a, loader(a) if a + 1 < c.ages else lambda ys, xs: next_ref[ys, xs])

    if c.ages > count:
        pl.when(final)(rest)
    else:
        rest()


def first_kernel(c, *refs):
    refs = list(refs)

    def take(n):
        out = refs[:n]
        del refs[:n]
        return out

    pos_ref, par_ref, parv_ref, later_ref = take(4)
    own, got = take(4), take(4)
    sea_ref, prey_ref, heat_ref, fish_ref = take(4)
    fleet_refs = take(c.n_fleet)
    plane_out, openv, openh, forage, heat4, rowc, colw, cole, catch = take(9)
    rows, cols, ages, months = c.rows, c.cols, c.ages, c.months
    blocks_y, blocks_x = rows // BY, cols // BX
    sea = sea_ref[...].astype(f32)
    line = lax.broadcasted_iota(jnp.int32, (rows, cols), 0)
    column = lax.broadcasted_iota(jnp.int32, (rows, cols), 1)
    openv[...] = jnp.where(line == rows - 1, 0.0, sea * pltpu.roll(sea, rows - 1, 0))
    openh[...] = jnp.where(column == cols - 1, 0.0, sea * pltpu.roll(sea, cols - 1, 1))
    for t in range(months):
        heat4[t] = heat_ref[t] * 0.25
        forage[t] = sea * prey_ref[t]
    edge_flux(c, pos_ref, parv_ref, sea_ref, forage.at[c.month], heat4.at[c.month], own, got, got, rowc, colw, cole)

    flat = []
    for ref in fleet_refs:
        flat += [ref[:, 0:LANES], ref[:, LANES : 2 * LANES]]
    flat = jnp.concatenate(flat, axis=0)
    names = flat[:, months * ages : months * ages + 1]
    turned = flat.T[0 : months * ages]
    base = ((pos_ref[1] * c.sizes[2] + pos_ref[2]) * (blocks_y * blocks_x)).astype(f32)
    block_col = (lax.broadcasted_iota(jnp.int32, (flat.shape[0], cols), 1) // BX).astype(f32)
    gear = column_of(parv_ref, GEAR, ages)
    for by in range(blocks_y):
        named = (block_col == names - (base + by * blocks_x)).astype(f32)
        sums = jnp.dot(turned, named, precision=lax.Precision.HIGHEST, preferred_element_type=f32)
        for t in range(months):
            for j in range(cols // LANES):
                catch[t, by, j] = gear * sums[t * ages : (t + 1) * ages, j * LANES : (j + 1) * LANES]

    tables = (openv, openh, forage.at[c.month], heat4.at[c.month], fish_ref, rowc, colw, cole, catch.at[c.month])
    advance(c, 0, 0, par_ref, lambda ys, xs: read_plane(later_ref, 1, ys, xs), tables, plane_out)
    plane_out[0, rows : rows + SUB, :] = jnp.broadcast_to(
        jnp.broadcast_to(parv_ref[MAT : MAT + 1, 0:1], (1, cols)), (SUB, cols)
    )


def month_kernel(c, *refs):
    refs = list(refs)

    def take(n):
        out = refs[:n]
        del refs[:n]
        return out

    par_ref, later_ref, next_ref, fish_ref = take(4)
    openv, openh, forage, heat4, rowc, colw, cole, catch = take(8)
    out_ref, top_out, bottom_out, west_out, east_out = take(5)
    tables = (openv, openh, forage.at[c.month], heat4.at[c.month], fish_ref, rowc, colw, cole, catch.at[c.month])

    def go(k, a, load):
        advance(c, k, a, par_ref, load, tables, out_ref, lines=(top_out, bottom_out))

    all_cohorts(c, 0, c.ages, par_ref, later_ref, next_ref, None, go)
    lane = lax.broadcasted_iota(jnp.int32, (SUB, LANES), 1)
    for i in range(c.rows // SUB):
        rs = slice(i * SUB, (i + 1) * SUB)
        for dst, lo, by in ((west_out, 0, 0), (east_out, c.cols - LANES, 1)):
            found = jnp.zeros((SUB, LANES), f32)
            for k in range(c.ages):
                value = out_ref[k, rs, lo : lo + LANES]
                found = jnp.where(lane == k, pltpu.roll(value, k + by, 1) if k + by else value, found)
            dst[rs, :] = found


def last_kernel(c, *refs):
    refs = list(refs)

    def take(n):
        out = refs[:n]
        del refs[:n]
        return out

    pos_ref, par_ref, parv_ref, later_ref, next_ref, recruit_ref, sea_ref, fish_ref, yield_ref = take(9)
    openv, openh, forage, heat4, catch = take(5)
    own, got, msgs = take(4), take(4), take(4)
    term_refs = take(c.n_terms)
    bcast_refs = take(c.n_bcast)
    out_ref, grad_ref = take(2)
    rowc, colw, cole, final_recruit = take(4)
    rows, months = c.rows, c.months
    step = pl.program_id(0)

    @pl.when(step == 0)
    def _():
        edge_flux(
            c, pos_ref, parv_ref, sea_ref, forage.at[c.month], heat4.at[c.month], own, got, msgs, rowc, colw, cole
        )
        sea = sea_ref[...].astype(f32)
        totals = [functools.reduce(jnp.add, [r[t] for r in term_refs]) for t in range(months + 1)]
        first = bcast_refs[0][...] * (pos_ref[0] == 0).astype(f32)
        first = first + bcast_refs[1][...] * (pos_ref[0] == c.sizes[0] - 1).astype(f32)
        for ref in bcast_refs[2:]:
            first = first + ref[...]
        first = first[0:rows] + recruit_ref[...] * first[rows : rows + 1]
        ratios = [1.0 / (1.0 + totals[t]) for t in range(months)]
        grad_ref[...] = (totals[months] * totals[1] * ratios[1] + first * totals[0] * ratios[0]) * sea
        final_recruit[...] = first * sea * yield_ref[...] * ratios[0] * ratios[0]

    tables = (openv, openh, forage.at[c.month], heat4.at[c.month], fish_ref, rowc, colw, cole, catch.at[c.month])

    def go(k, a, load):
        advance(c, k, a, par_ref, load, tables, out_ref, recruit=final_recruit)

    all_cohorts(c, step, GROUP, par_ref, later_ref, next_ref, recruit_ref, go)


def cost(planes, rows, cols):
    cells = planes * rows * cols
    return pl.CostEstimate(flops=60 * cells, bytes_accessed=8 * cells, transcendentals=2 * cells)


def edge_shapes(ages, rows, cols):
    return [
        jax.ShapeDtypeStruct((2, cols // LANES, ages, LANES), f32),
        jax.ShapeDtypeStruct((rows, LANES), f32),
        jax.ShapeDtypeStruct((rows, LANES), f32),
    ]


def first_cohort(sizes, pos, par, fin, own, got, sea, prey, heat, fish, fleet_blocks):
    ages, rows, cols = fin.shape
    months = prey.shape[0]
    c = Cfg(rows=rows, cols=cols, ages=ages, months=months, month=months - 1, sizes=sizes, n_fleet=len(fleet_blocks))
    operands = [pos, par, par, fin, *own, *got, sea, prey, heat, fish]
    at = len(operands)
    operands += [block for block, _ in fleet_blocks]

    def kernel(*refs):
        refs = list(refs)
        for k, (block, start) in enumerate(fleet_blocks):
            if start:
                refs[at + k] = refs[at + k].at[start : block.shape[0]]
        first_kernel(c, *refs)

    plane = jax.ShapeDtypeStruct((rows, cols), f32)
    stack = jax.ShapeDtypeStruct((months, rows, cols), f32)
    out_shape = [jax.ShapeDtypeStruct((1, rows + SUB, cols), f32), plane, plane, stack, stack]
    out_shape += edge_shapes(ages, rows, cols)
    out_shape.append(jax.ShapeDtypeStruct((months, rows // BY, cols // LANES, ages, LANES), f32))
    return pl.pallas_call(
        kernel,
        in_specs=[whole(SMEM), whole(SMEM)] + [whole()] * (len(operands) - 2),
        out_specs=[whole()] * len(out_shape),
        out_shape=out_shape,
        cost_estimate=cost(4, rows, cols),
        compiler_params=params_of(8),
        name="first_cohort",
    )(*operands)


def month_step(sizes, par, fin, nxt, fish, fields, edges, catch):
    ages, rows, cols = fin.shape
    months = catch.shape[0]
    c = Cfg(rows=rows, cols=cols, ages=ages, months=months, month=months - 1, sizes=sizes)
    operands = [par, fin, nxt, fish, *fields, *edges, catch]
    line = jax.ShapeDtypeStruct((cols // LANES, ages, LANES), f32)
    column = jax.ShapeDtypeStruct((rows, LANES), f32)
    return pl.pallas_call(
        functools.partial(month_kernel, c),
        in_specs=[whole(SMEM)] + [whole()] * (len(operands) - 1),
        out_specs=[whole()] * 5,
        out_shape=[jax.ShapeDtypeStruct((ages, rows, cols), f32), line, line, column, column],
        cost_estimate=cost(ages, rows, cols),
        compiler_params=params_of(16),
        name="month_step",
    )(*operands)


def month_last(sizes, pos, par, later, nxt, recruit, sea, fish, yields, fields, catch, own, got, msgs, terms, bcasts):
    ages, rows, cols = later.shape
    months = catch.shape[0]
    c = Cfg(
        rows=rows, cols=cols, ages=ages, months=months, month=0, sizes=sizes, n_terms=len(terms), n_bcast=len(bcasts)
    )
    operands = [pos, par, par, later, nxt, recruit, sea, fish, yields, *fields, catch, *own, *got, *msgs]
    operands += [*terms, *bcasts]
    scratch = [pltpu.VMEM(x.shape, f32) for x in edge_shapes(ages, rows, cols)]
    return pl.pallas_call(
        functools.partial(last_kernel, c),
        grid=(ages // GROUP,),
        in_specs=[whole(SMEM), whole(SMEM)] + [whole()] * (len(operands) - 2),
        out_specs=[pl.BlockSpec((GROUP, rows, cols), lambda i: (i, 0, 0)), whole()],
        out_shape=[jax.ShapeDtypeStruct((ages, rows, cols), f32), jax.ShapeDtypeStruct((rows, cols), f32)],
        scratch_shapes=scratch + [pltpu.VMEM((rows, cols), f32)],
        cost_estimate=cost(ages, rows, cols),
        compiler_params=params_of(16),
        name="month_last",
    )(*operands)


def habitat_of(forage, heat, ideal, tau):
    off = heat - ideal
    return forage * (tau / (1.0 + off * off))


def shards(
    saved,
    fin,
    prey,
    heat,
    sea,
    fish,
    yields,
    death,
    gear,
    kappa,
    tau,
    ideal,
    breeding,
    landing,
    east_piece,
    north_piece,
    patch,
    bounds,
):
    months, ages, rows, cols = saved.shape
    n_coh, n_lat, n_lon = sizes = tuple(lax.axis_size(axis) for axis in ("coh", "lat", "lon"))
    at_coh, at_lat, at_lon = (lax.axis_index(axis) for axis in ("coh", "lat", "lon"))
    pos = jnp.stack([at_coh, at_lat, at_lon]).astype(jnp.int32)
    cohort_age = at_coh * ages + jnp.arange(ages)
    nblocks = (rows // BY) * (cols // BX)
    inside = (cohort_age[None, :] >= bounds[:, 0:1]) & (cohort_age[None, :] < bounds[:, 1:2])
    masked = (landing * inside[:, None, :].astype(f32)).reshape(landing.shape[0], months * ages)
    names = ((north_piece * n_lon + east_piece[:, 0]) * nblocks + patch).astype(f32)
    fleet = jnp.concatenate([masked, names[:, None]], axis=1)
    fleet = jnp.pad(fleet, ((0, 0), (0, LANES - fleet.shape[1])))

    first = fin[0].astype(f32)
    nxt = shift(first, "coh", -1)
    fleet_lon = [fleet] + [shift(fleet, "lon", d) for d in range(1, n_lon)]
    terms = first_terms(spawn_parts(pos, breeding, ages * n_coh, saved, first, first), "coh")

    ahead, back, east, west, both, fleet_pack, later_last, par = pack_edges(
        sizes, pos, fin, nxt, sea, prey, heat, fleet_lon, (death, gear, kappa, tau, ideal, breeding)
    )
    from_west, from_east = swap_edges(east, west, both, "lon")
    from_before, from_after = shift(ahead, "lat", 1), shift(back, "lat", -1)
    start = ahead.shape[0] - fleet_pack.shape[0]
    terms = other_terms(terms, "coh", both)
    fleet_blocks = [(ahead, start), (from_before, start)]
    if n_lat > 2:
        fleet_blocks.append((from_after, start))
    fleet_blocks += [(shift(fleet_pack, "lat", d), 0) for d in range(2, n_lat - 1)]

    own = (ahead, back, east, west)
    msgs = (from_before, from_after, from_west, from_east)
    plane, openv, openh, forage, heat4, *edges, catch = first_cohort(
        sizes, pos, par, fin, own, msgs, sea, prey, heat, fish, fleet_blocks
    )
    plane = plane.reshape(rows + SUB, cols)
    fields = (openv, openh, forage, heat4)
    down = shift(plane, "coh", -1)
    bcasts = [plane, down] + [lax.ppermute(plane, "coh", [(0, j)]) for j in range(1, n_coh - 1)]
    later, *edges = month_step(sizes, par, fin, later_last, fish, fields, edges, catch)
    ahead, back, east, west, both, recruit, nxt = recruit_edges(
        sizes, months - 1, pos, par, sea, yields, down, terms, edges
    )
    own = (ahead, back, east, west)
    got = (shift(ahead, "lat", 1), shift(back, "lat", -1), *swap_edges(east, west, both, "lon"))
    return tuple(
        month_last(
            sizes, pos, par, later, nxt, recruit, sea, fish, yields, fields, catch, own, got, msgs, terms, bcasts
        )
    )


def solution(mesh):
    in_specs = (
        P(None, "coh", "lat", "lon"),
        P("coh", "lat", "lon"),
        P(None, "lat", "lon"),
        P(None, "lat", "lon"),
        P("lat", "lon"),
        P("lat", "lon"),
        P("lat", "lon"),
        P("coh"),
        P("coh"),
        P("coh"),
        P("coh"),
        P("coh"),
        P("coh"),
        P(("lat", "lon"), None, "coh"),
        P(("lat", "lon"), None),
        P(("lat", "lon")),
        P(("lat", "lon")),
        P(("lat", "lon"), None),
    )
    out_specs = (P("coh", "lat", "lon"), P("lat", "lon"))

    return jax.shard_map(shards, mesh=mesh, in_specs=in_specs, out_specs=out_specs, check_vma=False)
```

time: 57.9 us -> 49.8 us (0.86)
  Pallas kernels: 23.8 us -> 16.5 us
  other arithmetic: 3.14 us -> 1.11 us
  waiting for transfers between devices: 6.78 us -> 8.52 us
    pallas_call x4 -> x5, Pallas kernels: 22 us -> 14.7 us  [the longest x1 6.3 us: month_last(): pl.pallas_call(functools.partial(last_kernel, c), grid=(ages // GROUP,),...]
    ppermute x10, starting transfers between devices: 14.6 us -> 17.2 us  [shift(): return lax.ppermute(x, axis, [(i, (i + distance) % n) for i in range(n)])]
    ppermute x2, starting transfers between devices: 5.04 us -> 2.58 us  [shards(): lax.ppermute(plane, 'coh', [(0, j)])]
    another operation x3 -> x0, other arithmetic: 1.99 us -> none  [shards(): jnp.stack([death * -LOG2E, gear * LOG2E, kappa, tau, ideal * 0.25, maturi...]
    ppermute x2, waiting for transfers between devices: 0.01 us -> 1.3 us  [flipped(): lax.ppermute(x, axis, [(i, i ^ reach) for i in range(lax.axis_size(axis))])]
    another operation x1 -> x0, local copies, waits for them, and re-layouts: 0.75 us -> none  [shards(): jnp.stack([death * -LOG2E, gear * LOG2E, kappa, tau, ideal * 0.25, maturi...]
    ppermute x2, starting transfers between devices: 0.84 us -> 0.14 us  [flipped(): lax.ppermute(x, axis, [(i, i ^ reach) for i in range(lax.axis_size(axis))])]
    unnamed x26 -> x38, local copies, waits for them, and re-layouts: 1.65 us -> 2.34 us
  transfers between devices with their start and end apart: 14 -> 14, of which waited for: 5 -> 7; matrix products, arithmetic and copies ran while one was open for 6% -> 1% of each run, Pallas kernels for 26% -> 20%
where the time goes in v2:
time: 49.8 us; the launch traced here: 49.5 us
  starting transfers between devices  19.9 us (40%)
  Pallas kernels  16.5 us (33%)
  waiting for transfers between devices  8.52 us (17%)
  local copies, waits for them, and re-layouts  2.52 us (5%)
  other arithmetic  1.11 us (2%)
  between operations  0.99 us (2%)
    ppermute x10, starting transfers between devices, shift(): return lax.ppermute(x, axis, [(i, (i + distance) % n) for i in range(n)])  17.2 us
    ppermute x10, waiting for transfers between devices, shift(): return lax.ppermute(x, axis, [(i, (i + distance) % n) for i in range(n)])  7.22 us
    pallas_call x1, Pallas kernels, month_last(): pl.pallas_call(functools.partial(last_kernel, c), grid=(ages // GROUP,),...  6.3 us
    pallas_call x1, Pallas kernels, month_step(): pl.pallas_call(functools.partial(month_kernel, c), in_specs=[whole(SMEM)]...  5.52 us
    ppermute x2, starting transfers between devices, shards(): lax.ppermute(plane, 'coh', [(0, j)])  2.58 us
    unnamed x38, local copies, waits for them, and re-layouts  2.34 us
    pallas_call x1, Pallas kernels, first_cohort(): pl.pallas_call(kernel, in_specs=[whole(SMEM), whole(SMEM)] + [whole()] *...  1.58 us
    ppermute x2, waiting for transfers between devices, flipped(): lax.ppermute(x, axis, [(i, i ^ reach) for i in range(lax.axis_size(axis))])  1.3 us
  transfers between devices with their start and end apart: 14, of which 7 were waited for; matrix products, arithmetic and copies ran while one was open for 1% of the time, Pallas kernels for 20%

profile of v2, /device:TPU:1, one launch (start us, length us, event | category | flops | bytes accessed | tf_op | source)
XLA Modules:
  0.0 49.5 jit_solution(4016041279455363256)
XLA Ops:
  0.6 0.9 %bitcast_convert_fusion.first_ref._ = f32[64,256]{1,0:T(8,128)S(1)} fusion(bf16[32,64,256]{2,1,0:T(8,128)(2,1)} %refs_1_.3), kind=kLoop, calls=%fused_computation | loop fusion | flops 16384 | bytes 98304 | tf_op jit(solution)/shard_map/convert_element_type | solution.py:683
  1.5 4.2 %collective-permute-start = (f32[64,256]{1,0:T(8,128)S(1)}, f32[64,256]{1,0:T(8,128)S(1)}, u32[]{:S(2)}, u32[]{:S(2)}) collective-permute-start(f32[64,256]{1,0:T(8,128)S(1)} %bitcast_convert_fusion.first_ref._), channel_id=1, source_target_pairs={{0,24},{8,0},{16,8},{24,16},{1,25},{9,1},{17,9},{25,17},{2,26},{10... | collective-permute-start | bytes 196616 | tf_op jit(solution)/shard_map/ppermute | solution.py:41
  5.6 0.1 pad_add_fusion.refs_0_.pos_ref
  5.7 1.6 %copy-done.1 = bf16[2,32,64,256]{3,2,1,0:T(8,128)(2,1)S(1)} copy-done((bf16[2,32,64,256]{3,2,1,0:T(8,128)(2,1)S(1)}, bf16[2,32,64,256]{3,2,1,0:T(8,128)(2,1)}, u32[]{:S(2)}) %copy-start.1) | copy-done | bytes 2097176
  7.3 0.7 %copy-done.7 = f32[32]{0:T(128)S(1)} copy-done((f32[32]{0:T(128)S(1)}, f32[32]{0:T(128)}, u32[]{:S(2)}) %copy-start.7) | copy-done | bytes 152
  8.1 1.3 %spawn_parts.1.a_ref = f32[3,64,256]{2,1,0:T(8,128)S(1)} custom-call(s32[3]{0:T(128)S(1)} %pad_add_fusion.refs_0_.pos_ref, f32[32]{0:T(128)S(1)} %copy-done.7, bf16[2,32,64,256]{3,2,1,0:T(8,128)(2,1)S(1)} %copy-done.1, f32[64,256]{1,0:T(8,128)S(1)} %bitcast_convert_fusion.first_ref._, f32[64,256]{1,0:T(8,128)S(1)} %bitcast_convert_fusion.first_ref._), custom_call_target="tpu_custom_call" | custom-call | tf_op jit(solution)/shard_map/spawn_parts/pallas_call | solution.py:68
  9.4 0.1 collective-permute-start.7
  9.5 0.1 and_convert_fusion
  9.7 0.1 copy.20
  9.8 0.1 reshape.85
  9.8 0.1 select_maximum_fusion.refs_6_
  9.9 1.2 %collective-permute-start.1 = (f32[32,128]{1,0:T(8,128)S(1)}, f32[32,128]{1,0:T(8,128)S(1)}, u32[]{:S(2)}, u32[]{:S(2)}) collective-permute-start(f32[32,128]{1,0:T(8,128)S(1)} %select_maximum_fusion.refs_6_), channel_id=1, source_target_pairs={{0,1},{1,0},{2,3},{3,2},{4,5},{5,4},{6,7},{7,6},{8,9},{9,8},{10,11... | collective-permute-start | bytes 49160 | tf_op jit(solution)/shard_map/ppermute | solution.py:41
  11.2 1.3 %collective-permute-done.1.refs_7_ = f32[32,128]{1,0:T(8,128)S(1)} collective-permute-done((f32[32,128]{1,0:T(8,128)S(1)}, f32[32,128]{1,0:T(8,128)S(1)}, u32[]{:S(2)}, u32[]{:S(2)}) %collective-permute-start.1) | collective-permute-done | bytes 16416 | tf_op jit(solution)/shard_map/ppermute | solution.py:41
  12.6 1.0 %pack_edges.1 = (f32[72,256]{1,0:T(8,128)S(1)}, f32[72,256]{1,0:T(8,128)S(1)}, f32[64,128]{1,0:T(8,128)S(1)}, f32[64,128]{1,0:T(8,128)S(1)}, f32[64,128]{1,0:T(8...) custom-call(s32[3]{0:T(128)S(1)} %pad_add_fusion.refs_0_.pos_ref, ...), custom_call_target="tpu_custom_call" | custom-call | tf_op jit(solution)/shard_map/pack_edges/pallas_call | solution.py:201
  13.6 1.3 %collective-permute-done.7.b_ref = f32[3,64,256]{2,1,0:T(8,128)S(1)} collective-permute-done((f32[3,64,256]{2,1,0:T(8,128)S(1)}, f32[3,64,256]{2,1,0:T(8,128)S(1)}, u32[]{:S(2)}, u32[]{:S(2)}) %collective-permute-start.7) | collective-permute-done | bytes 196640 | tf_op jit(solution)/shard_map/ppermute | solution.py:101
  15.0 3.0 %collective-permute-start.2 = (f32[72,256]{1,0:T(8,128)S(1)}, f32[72,256]{1,0:T(8,128)S(1)}, u32[]{:S(2)}, u32[]{:S(2)}) collective-permute-start(f32[72,256]{1,0:T(8,128)S(1)} %get-tuple-element.33.refs_4_.refs_16_), channel_id=1, source_target_pairs={{0,2},{2,4},{4,6},{6,0},{1,3},{3,5},{5,7},{7,1},{8,10},{10,12},{12... | collective-permute-start | bytes 221192 | tf_op jit(solution)/shard_map/ppermute | solution.py:41
  18.0 0.3 collective-permute-start.5
  18.3 1.2 %collective-permute-start.4 = (f32[64,128]{1,0:T(8,128)S(1)}, f32[64,128]{1,0:T(8,128)S(1)}, u32[]{:S(2)}, u32[]{:S(2)}) collective-permute-start(f32[64,128]{1,0:T(8,128)S(1)} %get-tuple-element.37._), channel_id=1, source_target_pairs={{0,1},{1,0},{2,3},{3,2},{4,5},{5,4},{6,7},{7,6},{8,9},{9,8},{10,11... | collective-permute-start | bytes 98312 | tf_op jit(solution)/shard_map/ppermute | solution.py:41
  19.6 1.6 %collective-permute-done.5.refs_19_ = f32[32,256]{1,0:T(8,128)S(1)} collective-permute-done((f32[32,256]{1,0:T(8,128)S(1)}, f32[32,256]{1,0:T(8,128)S(1)}, u32[]{:S(2)}, u32[]{:S(2)}) %collective-permute-start.5) | collective-permute-done | bytes 32800 | tf_op jit(solution)/shard_map/ppermute | solution.py:41
  21.1 0.3 collective-permute-done.4.refs_10_.refs_11_.refs_24_.refs_25_
  21.4 0.7 %collective-permute-done.3.refs_9_.refs_18_.refs_23_ = f32[72,256]{1,0:T(8,128)S(1)} collective-permute-done((f32[72,256]{1,0:T(8,128)S(1)}, f32[72,256]{1,0:T(8,128)S(1)}, u32[]{:S(2)}, u32[]{:S(2)}) %collective-permute-start.3) | collective-permute-done | bytes 73760 | tf_op jit(solution)/shard_map/ppermute | solution.py:41
  22.1 1.6 %first_cohort.1 = (f32[1,72,256]{2,1,0:T(8,128)S(1)}, f32[64,256]{1,0:T(8,128)S(1)}, f32[64,256]{1,0:T(8,128)S(1)}, f32[2,64,256]{2,1,0:T(8,128)S(1)}, f32[2,64,...) custom-call(s32[3]{0:T(128)S(1)} %pad_add_fusion.refs_0_.pos_ref, ...), custom_call_target="tpu_custom_call" | custom-call | flops 3932160 | bytes 524288 | tf_op jit(solution)/shard_map/first_cohort/pallas_call | solution.py:595
  23.7 3.0 %collective-permute-start.6 = (f32[72,256]{1,0:T(8,128)S(1)}, f32[72,256]{1,0:T(8,128)S(1)}, u32[]{:S(2)}, u32[]{:S(2)}) collective-permute-start(f32[72,256]{1,0:T(8,128)S(1)} %bitcast.27), channel_id=1, source_target_pairs={{0,24},{8,0},{16,8},{24,16},{1,25},{9,1},{17,9},{25,17},{2,26},{10... | collective-permute-start | bytes 221192 | tf_op jit(solution)/shard_map/ppermute | solution.py:41
  26.7 1.3 %collective-permute-start.13 = (f32[72,256]{1,0:T(8,128)S(1)}, f32[72,256]{1,0:T(8,128)S(1)}, u32[]{:S(2)}, u32[]{:S(2)}) collective-permute-start(f32[72,256]{1,0:T(8,128)S(1)} %bitcast.28), channel_id=1, source_target_pairs={{0,16},{1,17},{2,18},{3,19},{4,20},{5,21},{6,22},{7,23}} | collective-permute-start | bytes 221192 | tf_op jit(solution)/shard_map/ppermute | solution.py:708
  28.0 1.3 %collective-permute-start.12 = (f32[72,256]{1,0:T(8,128)S(1)}, f32[72,256]{1,0:T(8,128)S(1)}, u32[]{:S(2)}, u32[]{:S(2)}) collective-permute-start(f32[72,256]{1,0:T(8,128)S(1)} %bitcast.29), channel_id=1, source_target_pairs={{0,8},{1,9},{2,10},{3,11},{4,12},{5,13},{6,14},{7,15}} | collective-permute-start | bytes 221192 | tf_op jit(solution)/shard_map/ppermute | solution.py:708
  29.3 5.5 %month_step.1 = (f32[32,64,256]{2,1,0:T(8,128)S(1)}, f32[2,32,128]{2,1,0:T(8,128)S(1)}, f32[2,32,128]{2,1,0:T(8,128)S(1)}, f32[64,128]{1,0:T(8,128)S(1)}, f32[64,128]{1,0:T(8,128)S(1)}) custom-call(f32[8,128]{1,0:T(8,128)S(1)} %get-tuple-element.31.refs_1_.refs_2_.refs_0_, bf16[32,64,256]{2,1,0:T(8,128)(2,1)S(1)} %copy-done, ...), custom_call_target="tpu_custom_call" | custom-call | flops 31457280 | bytes 4194304 | tf_op jit(solution)/shard_map/month_step/pallas_call | solution.py:613
  34.9 0.7 %recruit_edges.1 = (f32[32,256]{1,0:T(8,128)S(1)}, f32[32,256]{1,0:T(8,128)S(1)}, f32[64,128]{1,0:T(8,128)S(1)}, f32[64,128]{1,0:T(8,128)S(1)}, f32[64,128]{1,0:...) custom-call(s32[3]{0:T(128)S(1)} %pad_add_fusion.refs_0_.pos_ref, ...), custom_call_target="tpu_custom_call" | custom-call | tf_op jit(solution)/shard_map/recruit_edges/pallas_call | solution.py:266
  35.6 1.3 %collective-permute-start.11 = (f32[64,128]{1,0:T(8,128)S(1)}, f32[64,128]{1,0:T(8,128)S(1)}, u32[]{:S(2)}, u32[]{:S(2)}) collective-permute-start(f32[64,128]{1,0:T(8,128)S(1)} %get-tuple-element.59), channel_id=1, source_target_pairs={{0,1},{1,0},{2,3},{3,2},{4,5},{5,4},{6,7},{7,6},{8,9},{9,8},{10,11... | collective-permute-start | bytes 98312 | tf_op jit(solution)/shard_map/ppermute | solution.py:41
  36.9 3.0 %collective-permute-start.9 = (f32[32,256]{1,0:T(8,128)S(1)}, f32[32,256]{1,0:T(8,128)S(1)}, u32[]{:S(2)}, u32[]{:S(2)}) collective-permute-start(f32[32,256]{1,0:T(8,128)S(1)} %get-tuple-element.55.refs_14_), channel_id=1, source_target_pairs={{0,2},{2,4},{4,6},{6,0},{1,3},{3,5},{5,7},{7,1},{8,10},{10,12},{12... | collective-permute-start | bytes 98312 | tf_op jit(solution)/shard_map/ppermute | solution.py:41
  39.9 1.0 %collective-permute-done.9.refs_18_ = f32[32,256]{1,0:T(8,128)S(1)} collective-permute-done((f32[32,256]{1,0:T(8,128)S(1)}, f32[32,256]{1,0:T(8,128)S(1)}, u32[]{:S(2)}, u32[]{:S(2)}) %collective-permute-start.9) | collective-permute-done | bytes 32800 | tf_op jit(solution)/shard_map/ppermute | solution.py:41
  40.9 2.3 %collective-permute-done.10.refs_19_ = f32[32,256]{1,0:T(8,128)S(1)} collective-permute-done((f32[32,256]{1,0:T(8,128)S(1)}, f32[32,256]{1,0:T(8,128)S(1)}, u32[]{:S(2)}, u32[]{:S(2)}) %collective-permute-start.10) | collective-permute-done | bytes 32800 | tf_op jit(solution)/shard_map/ppermute | solution.py:41
  43.2 6.3 %month_last.1 = (f32[32,64,256]{2,1,0:T(8,128)}, f32[64,256]{1,0:T(8,128)}) custom-call(s32[3]{0:T(128)S(1)} %pad_add_fusion.refs_0_.pos_ref, f32[8,128]{1,0:T(8,128)S(1)} %get-tuple-element.31.refs_1_.refs_2_.refs_0_, f32[8,128]{1,0:T(8,128)S(1)} %get-tuple-element.31.refs_1_.refs_2_.refs_0_, f32[32,64,256]{2,1,0:T(8,128)S(1)} %get-tuple-element.47.refs_3_, ...), custom_call_target="tpu_custom_call" | custom-call | flops 31457280 | bytes 4194304 | tf_op jit(solution)/shard_map/month_last/pallas_call | solution.py:633
  (51 shorter events, 0.2 us)
Async XLA Ops:
  0.6 11.9 %copy-start = (bf16[32,64,256]{2,1,0:T(8,128)(2,1)S(1)}, bf16[32,64,256]{2,1,0:T(8,128)(2,1)}, u32[]{:S(2)}) copy-start(bf16[32,64,256]{2,1,0:T(8,128)(2,1)} %refs_1_.3) | copy-start | bytes 3145732
  1.5 11.0 %collective-permute-start = (f32[64,256]{1,0:T(8,128)S(1)}, f32[64,256]{1,0:T(8,128)S(1)}, u32[]{:S(2)}, u32[]{:S(2)}) collective-permute-start(f32[64,256]{1,0:T(8,128)S(1)} %bitcast_convert_fusion.first_ref._), channel_id=1, source_target_pairs={{0,24},{8,0},{16,8},{24,16},{1,25},{9,1},{17,9},{25,17},{2,26},{10... | collective-permute-start | bytes 196616 | tf_op jit(solution)/shard_map/ppermute | solution.py:41
  5.7 1.6 %copy-start.1 = (bf16[2,32,64,256]{3,2,1,0:T(8,128)(2,1)S(1)}, bf16[2,32,64,256]{3,2,1,0:T(8,128)(2,1)}, u32[]{:S(2)}) copy-start(bf16[2,32,64,256]{3,2,1,0:T(8,128)(2,1)} %saved_ref.1) | copy-start | bytes 6291460
  8.0 1.5 %copy-start.15 = (s32[32,2]{0,1:T(2,128)S(1)}, s32[32,2]{0,1:T(2,128)}, u32[]{:S(2)}) copy-start(s32[32,2]{0,1:T(2,128)} %param.35) | copy-start | bytes 772
  8.0 1.6 %copy-start.14 = (f32[32,2,32]{2,1,0:T(2,128)S(1)}, f32[32,2,32]{2,1,0:T(2,128)}, u32[]{:S(2)}) copy-start(f32[32,2,32]{2,1,0:T(2,128)} %param.31) | copy-start | bytes 24580
  8.0 1.7 %copy-start.16 = (s32[32]{0:T(128)S(1)}, s32[32]{0:T(128)}, u32[]{:S(2)}) copy-start(s32[32]{0:T(128)} %param.34) | copy-start | bytes 388
  8.0 1.7 %copy-start.17 = (s32[32,1]{0,1:T(1,128)S(1)}, s32[32,1]{0,1:T(1,128)}, u32[]{:S(2)}) copy-start(s32[32,1]{0,1:T(1,128)} %param.32) | copy-start | bytes 388
  8.0 1.7 %copy-start.18 = (s32[32]{0:T(128)S(1)}, s32[32]{0:T(128)}, u32[]{:S(2)}) copy-start(s32[32]{0:T(128)} %param.33) | copy-start | bytes 388
  8.0 4.5 %copy-start.2 = (s32[64,256]{1,0:T(8,128)S(1)}, s32[64,256]{1,0:T(8,128)}, u32[]{:S(2)}) copy-start(s32[64,256]{1,0:T(8,128)} %refs_6_.1) | copy-start | bytes 196612
  8.0 4.5 %copy-start.3 = (f32[2,64,256]{2,1,0:T(8,128)S(1)}, f32[2,64,256]{2,1,0:T(8,128)}, u32[]{:S(2)}) copy-start(f32[2,64,256]{2,1,0:T(8,128)} %refs_13_.1) | copy-start | bytes 393220
  8.0 4.5 %copy-start.4 = (f32[2,64,256]{2,1,0:T(8,128)S(1)}, f32[2,64,256]{2,1,0:T(8,128)}, u32[]{:S(2)}) copy-start(f32[2,64,256]{2,1,0:T(8,128)} %refs_14_.1) | copy-start | bytes 393220
  8.0 4.5 %copy-start.8 = (f32[32]{0:T(128)S(1)}, f32[32]{0:T(128)}, u32[]{:S(2)}) copy-start(f32[32]{0:T(128)} %breed_ref.1) | copy-start | bytes 388
  8.0 4.5 %copy-start.9 = (f32[32]{0:T(128)S(1)}, f32[32]{0:T(128)}, u32[]{:S(2)}) copy-start(f32[32]{0:T(128)} %param.25) | copy-start | bytes 388
  8.0 4.5 %copy-start.10 = (f32[32]{0:T(128)S(1)}, f32[32]{0:T(128)}, u32[]{:S(2)}) copy-start(f32[32]{0:T(128)} %param.26) | copy-start | bytes 388
  8.1 4.5 %copy-start.11 = (f32[32]{0:T(128)S(1)}, f32[32]{0:T(128)}, u32[]{:S(2)}) copy-start(f32[32]{0:T(128)} %param.27) | copy-start | bytes 388
  8.1 4.5 %copy-start.12 = (f32[32]{0:T(128)S(1)}, f32[32]{0:T(128)}, u32[]{:S(2)}) copy-start(f32[32]{0:T(128)} %param.28) | copy-start | bytes 388
  8.1 4.5 %copy-start.13 = (f32[32]{0:T(128)S(1)}, f32[32]{0:T(128)}, u32[]{:S(2)}) copy-start(f32[32]{0:T(128)} %param.29) | copy-start | bytes 388
  8.1 14.0 %copy-start.5 = (f32[64,256]{1,0:T(8,128)S(1)}, f32[64,256]{1,0:T(8,128)}, u32[]{:S(2)}) copy-start(f32[64,256]{1,0:T(8,128)} %refs_7_.1) | copy-start | bytes 196612
  9.4 5.5 %collective-permute-start.7 = (f32[3,64,256]{2,1,0:T(8,128)S(1)}, f32[3,64,256]{2,1,0:T(8,128)S(1)}, u32[]{:S(2)}, u32[]{:S(2)}) collective-permute-start(f32[3,64,256]{2,1,0:T(8,128)S(1)} %spawn_parts.1.a_ref), channel_id=1, source_target_pairs={{0,8},{8,0},{16,24},{24,16},{1,9},{9,1},{17,25},{25,17},{2,10},{10... | collective-permute-start | bytes 589832 | tf_op jit(solution)/shard_map/ppermute | solution.py:101
  9.9 2.6 %collective-permute-start.1 = (f32[32,128]{1,0:T(8,128)S(1)}, f32[32,128]{1,0:T(8,128)S(1)}, u32[]{:S(2)}, u32[]{:S(2)}) collective-permute-start(f32[32,128]{1,0:T(8,128)S(1)} %select_maximum_fusion.refs_6_), channel_id=1, source_target_pairs={{0,1},{1,0},{2,3},{3,2},{4,5},{5,4},{6,7},{7,6},{8,9},{9,8},{10,11... | collective-permute-start | bytes 49160 | tf_op jit(solution)/shard_map/ppermute | solution.py:41
  14.9 19.9 %copy-start.6 = (f32[64,256]{1,0:T(8,128)S(1)}, f32[64,256]{1,0:T(8,128)}, u32[]{:S(2)}) copy-start(f32[64,256]{1,0:T(8,128)} %refs_8_.1) | copy-start | bytes 196612
  14.9 19.9 %collective-permute-start.8 = (f32[3,64,256]{2,1,0:T(8,128)S(1)}, f32[3,64,256]{2,1,0:T(8,128)S(1)}, u32[]{:S(2)}, u32[]{:S(2)}) collective-permute-start(f32[3,64,256]{2,1,0:T(8,128)S(1)} %add_after.1.refs_5_.refs_26_), channel_id=1, source_target_pairs={{0,16},{8,24},{16,0},{24,8},{1,17},{9,25},{17,1},{25,9},{2,18},{10... | collective-permute-start | bytes 589832 | tf_op jit(solution)/shard_map/ppermute | solution.py:101
  15.0 6.4 %collective-permute-start.2 = (f32[72,256]{1,0:T(8,128)S(1)}, f32[72,256]{1,0:T(8,128)S(1)}, u32[]{:S(2)}, u32[]{:S(2)}) collective-permute-start(f32[72,256]{1,0:T(8,128)S(1)} %get-tuple-element.33.refs_4_.refs_16_), channel_id=1, source_target_pairs={{0,2},{2,4},{4,6},{6,0},{1,3},{3,5},{5,7},{7,1},{8,10},{10,12},{12... | collective-permute-start | bytes 221192 | tf_op jit(solution)/shard_map/ppermute | solution.py:41
  18.0 4.1 %collective-permute-start.3 = (f32[72,256]{1,0:T(8,128)S(1)}, f32[72,256]{1,0:T(8,128)S(1)}, u32[]{:S(2)}, u32[]{:S(2)}) collective-permute-start(f32[72,256]{1,0:T(8,128)S(1)} %get-tuple-element.34.refs_5_), channel_id=1, source_target_pairs={{0,6},{2,0},{4,2},{6,4},{1,7},{3,1},{5,3},{7,5},{8,14},{10,8},{12,... | collective-permute-start | bytes 221192 | tf_op jit(solution)/shard_map/ppermute | solution.py:41
  18.0 3.1 %collective-permute-start.5 = (f32[32,256]{1,0:T(8,128)S(1)}, f32[32,256]{1,0:T(8,128)S(1)}, u32[]{:S(2)}, u32[]{:S(2)}) collective-permute-start(f32[32,256]{1,0:T(8,128)S(1)} %get-tuple-element.38), channel_id=1, source_target_pairs={{0,4},{2,6},{4,0},{6,2},{1,5},{3,7},{5,1},{7,3},{8,12},{10,14},{12... | collective-permute-start | bytes 98312 | tf_op jit(solution)/shard_map/ppermute | solution.py:41
  18.3 3.1 %collective-permute-start.4 = (f32[64,128]{1,0:T(8,128)S(1)}, f32[64,128]{1,0:T(8,128)S(1)}, u32[]{:S(2)}, u32[]{:S(2)}) collective-permute-start(f32[64,128]{1,0:T(8,128)S(1)} %get-tuple-element.37._), channel_id=1, source_target_pairs={{0,1},{1,0},{2,3},{3,2},{4,5},{5,4},{6,7},{7,6},{8,9},{9,8},{10,11... | collective-permute-start | bytes 98312 | tf_op jit(solution)/shard_map/ppermute | solution.py:41
  23.7 11.1 %collective-permute-start.6 = (f32[72,256]{1,0:T(8,128)S(1)}, f32[72,256]{1,0:T(8,128)S(1)}, u32[]{:S(2)}, u32[]{:S(2)}) collective-permute-start(f32[72,256]{1,0:T(8,128)S(1)} %bitcast.27), channel_id=1, source_target_pairs={{0,24},{8,0},{16,8},{24,16},{1,25},{9,1},{17,9},{25,17},{2,26},{10... | collective-permute-start | bytes 221192 | tf_op jit(solution)/shard_map/ppermute | solution.py:41
  26.7 13.2 %collective-permute-start.13 = (f32[72,256]{1,0:T(8,128)S(1)}, f32[72,256]{1,0:T(8,128)S(1)}, u32[]{:S(2)}, u32[]{:S(2)}) collective-permute-start(f32[72,256]{1,0:T(8,128)S(1)} %bitcast.28), channel_id=1, source_target_pairs={{0,16},{1,17},{2,18},{3,19},{4,20},{5,21},{6,22},{7,23}} | collective-permute-start | bytes 221192 | tf_op jit(solution)/shard_map/ppermute | solution.py:708
  28.0 11.9 %collective-permute-start.12 = (f32[72,256]{1,0:T(8,128)S(1)}, f32[72,256]{1,0:T(8,128)S(1)}, u32[]{:S(2)}, u32[]{:S(2)}) collective-permute-start(f32[72,256]{1,0:T(8,128)S(1)} %bitcast.29), channel_id=1, source_target_pairs={{0,8},{1,9},{2,10},{3,11},{4,12},{5,13},{6,14},{7,15}} | collective-permute-start | bytes 221192 | tf_op jit(solution)/shard_map/ppermute | solution.py:708
  35.6 4.3 %collective-permute-start.11 = (f32[64,128]{1,0:T(8,128)S(1)}, f32[64,128]{1,0:T(8,128)S(1)}, u32[]{:S(2)}, u32[]{:S(2)}) collective-permute-start(f32[64,128]{1,0:T(8,128)S(1)} %get-tuple-element.59), channel_id=1, source_target_pairs={{0,1},{1,0},{2,3},{3,2},{4,5},{5,4},{6,7},{7,6},{8,9},{9,8},{10,11... | collective-permute-start | bytes 98312 | tf_op jit(solution)/shard_map/ppermute | solution.py:41
  36.9 4.0 %collective-permute-start.9 = (f32[32,256]{1,0:T(8,128)S(1)}, f32[32,256]{1,0:T(8,128)S(1)}, u32[]{:S(2)}, u32[]{:S(2)}) collective-permute-start(f32[32,256]{1,0:T(8,128)S(1)} %get-tuple-element.55.refs_14_), channel_id=1, source_target_pairs={{0,2},{2,4},{4,6},{6,0},{1,3},{3,5},{5,7},{7,1},{8,10},{10,12},{12... | collective-permute-start | bytes 98312 | tf_op jit(solution)/shard_map/ppermute | solution.py:41
  39.9 3.3 %collective-permute-start.10 = (f32[32,256]{1,0:T(8,128)S(1)}, f32[32,256]{1,0:T(8,128)S(1)}, u32[]{:S(2)}, u32[]{:S(2)}) collective-permute-start(f32[32,256]{1,0:T(8,128)S(1)} %get-tuple-element.56.refs_15_), channel_id=1, source_target_pairs={{0,6},{2,0},{4,2},{6,4},{1,7},{3,1},{5,3},{7,5},{8,14},{10,8},{12,... | collective-permute-start | bytes 98312 | tf_op jit(solution)/shard_map/ppermute | solution.py:41
  (1 other events, 0.7 us)

commit v3 on v2

--- a/solution.py
+++ b/solution.py
@@ -14,6 +14,7 @@
 SUB = 8
 GROUP = 8
 PAIR = 2
+PARTS = 2
 SPAWN_MB = 24
 
 f32 = jnp.float32
@@ -124,7 +125,7 @@
     pos_ref, fin_ref, next_ref, sea_ref, prey_ref, heat_ref = refs[:6]
     fleet_refs = refs[6 : 6 + fleets]
     death_ref, gear_ref, kappa_ref, tau_ref, ideal_ref, breed_ref = refs[6 + fleets : 12 + fleets]
-    ahead_ref, back_ref, east_ref, west_ref, both_ref, fleet_out, later_ref, table_ref = refs[12 + fleets :]
+    ahead_ref, back_ref, east_ref, west_ref, fleet_out, later_ref, table_ref, openv, openh, forage, heat4 = refs[12 + fleets :]
     n_coh, n_lat, n_lon = sizes
     age = lax.broadcasted_iota(jnp.int32, (1, ages), 1) + (pos_ref[0] * ages + 1)
     table_ref[...] = jnp.zeros_like(table_ref)
@@ -188,7 +189,40 @@
         east = jnp.where(lane == k, pltpu.roll(right, k + 1, 1), east)
     east_ref[...] = east
     west_ref[...] = west
-    both_ref[...] = jnp.where(pos_ref[2] == 0, east, west)
+
+    sea = fields[0]
+    line = lax.broadcasted_iota(jnp.int32, (rows, cols), 0)
+    column = lax.broadcasted_iota(jnp.int32, (rows, cols), 1)
+    openv[...] = jnp.where(line == rows - 1, 0.0, sea * pltpu.roll(sea, rows - 1, 0))
+    openh[...] = jnp.where(column == cols - 1, 0.0, sea * pltpu.roll(sea, cols - 1, 1))
+    for t in range(months):
+        heat4[t] = heat_ref[t] * 0.25
+        forage[t] = sea * prey_ref[t]
+
+
+def relay_kernel(side, pos_ref, east_ref, west_ref, _, *refs):
+    *block_refs, both_ref, gathered_ref = refs
+    rows = east_ref.shape[0]
+    at = 0
+    for ref in block_refs:
+        for half in range(2):
+            gathered_ref[at : at + side, :] = ref[ref.shape[0] - side :, half * LANES : (half + 1) * LANES]
+            at += side
+    both_ref[0:rows, :] = jnp.where(pos_ref[2] == 0, east_ref[...], west_ref[...])
+    both_ref[rows:, :] = gathered_ref[...]
+
+
+def relay(pos, east, west, ahead_of, blocks, side):
+    rows = east.shape[0]
+    tall = 2 * side * len(blocks)
+    return pl.pallas_call(
+        functools.partial(relay_kernel, side),
+        in_specs=[whole(SMEM), whole(), whole(), pl.BlockSpec(memory_space=pl.ANY)] + [whole()] * len(blocks),
+        out_specs=[whole()] * 2,
+        out_shape=[jax.ShapeDtypeStruct((rows + tall, LANES), f32), jax.ShapeDtypeStruct((tall, LANES), f32)],
+        compiler_params=params_of(8),
+        name="relay",
+    )(pos, east, west, ahead_of, *blocks)
 
 
 def pack_edges(sizes, pos, fin, nxt, sea, prey, heat, fleet_blocks, rates):
@@ -201,76 +235,94 @@
     return pl.pallas_call(
         functools.partial(pack_kernel, months, ages, sizes, len(fleet_blocks)),
         in_specs=[whole(SMEM)] + [whole()] * (5 + len(fleet_blocks) + len(rates)),
-        out_specs=[whole()] * 8,
+        out_specs=[whole()] * 11,
         out_shape=[
             line,
             line,
             column,
             column,
-            column,
             jax.ShapeDtypeStruct((half, 2 * LANES), f32),
             jax.ShapeDtypeStruct((rows, cols), f32),
             jax.ShapeDtypeStruct((SUB, LANES), f32),
+            jax.ShapeDtypeStruct((rows, cols), f32),
+            jax.ShapeDtypeStruct((rows, cols), f32),
+            jax.ShapeDtypeStruct((months, rows, cols), f32),
+            jax.ShapeDtypeStruct((months, rows, cols), f32),
         ],
         compiler_params=params_of(16),
         name="pack_edges",
     )(pos, fin, nxt, sea, prey, heat, *fleet_blocks, *[rate.reshape(1, ages) for rate in rates])
 
 
-def recruit_kernel(months, month, ages, sizes, terms, *refs):
-    pos_ref, parv_ref, sea_ref, yield_ref, nxt_ref = refs[:5]
-    term_refs = refs[5 : 5 + terms]
-    rest = refs[5 + terms :]
-    top_ref, bottom_ref, west_ref, east_ref = rest[:4]
-    ahead_out, back_out, east_out, west_out, both_out, recruit_out, last_out = rest[4:]
-    n_coh = sizes[0]
-    rows, cols = sea_ref.shape
-    keep = (pos_ref[0] < n_coh - 1).astype(f32)
-    spawning = functools.reduce(jnp.add, [r[month] for r in term_refs])
+def recruit_kernel(c, terms, *refs):
+    pos_ref, par_ref, parv_ref, sea_ref, yield_ref, fish_ref, nxt_ref = refs[:7]
+    term_refs = refs[7 : 7 + terms]
+    rowc, colw, cole, catch, _ = refs[7 + terms : 12 + terms]
+    all_ref, ahead_out, back_out, east_out, west_out, both_out, recruit_out, last_out, top, bottom = refs[12 + terms :]
+    rows, cols, ages, months = c.rows, c.cols, c.ages, c.months
+    n_i, n_j = rows // SUB, cols // LANES
+    keep = (pos_ref[0] < c.sizes[0] - 1).astype(f32)
+    spawning = functools.reduce(jnp.add, [r[c.month] for r in term_refs])
     first = functools.reduce(jnp.add, [r[months] for r in term_refs])
     ratio = 1.0 / (1.0 + spawning)
-    recruit = first * sea_ref[...].astype(f32) * yield_ref[...] * ratio * ratio
-    recruit_out[...] = recruit
-    mat_next = nxt_ref[rows : rows + 1, :]
-    last = (nxt_ref[0:rows, :] + recruit * mat_next) * keep
+    recruit_out[...] = first * sea_ref[...].astype(f32) * yield_ref[...] * ratio * ratio
+    last = (nxt_ref[0:rows, :] + recruit_out[...] * nxt_ref[rows : rows + 1, :]) * keep
     last_out[...] = last
 
-    mat_row = parv_ref[MAT : MAT + 1, :]
-    down = lax.broadcasted_iota(jnp.int32, (ages, LANES), 0)
-    across = lax.broadcasted_iota(jnp.int32, (ages, LANES), 1)
-    mat_col = jnp.sum(
-        jnp.where(down == across, jnp.broadcast_to(mat_row, (ages, LANES)), 0.0), axis=1, keepdims=True
-    )
-    for src, dst, row in ((top_ref, back_out, 0), (bottom_ref, ahead_out, rows - 1)):
-        full = jnp.concatenate([src[j] for j in range(src.shape[0])], axis=1)
-        full = full + recruit[row : row + 1, :] * mat_col
-        up = pltpu.roll(full, ages - 1, 0)
-        place = lax.broadcasted_iota(jnp.int32, (ages, cols), 0)
-        dst[...] = jnp.where(place == ages - 1, last[row : row + 1, :], up)
-    lane = lax.broadcasted_iota(jnp.int32, (rows, LANES), 1)
-    sides = []
-    for src, dst, col in ((west_ref, west_out, 0), (east_ref, east_out, cols - 1)):
-        full = src[...] + recruit[:, col : col + 1] * mat_row
-        up = pltpu.roll(full, LANES - 1, 1)
-        sides.append(jnp.where(lane == ages - 1, last[:, col : col + 1], up))
-        dst[...] = sides[-1]
-    both_out[...] = jnp.where(pos_ref[2] == 0, sides[1], sides[0])
-
-
-def recruit_edges(sizes, month, pos, parv, sea, yields, nxt, terms, edges):
-    rows, cols = sea.shape
-    ages = edges[0].shape[1]
+    def body(h, carry):
+        for k in range(PAIR):
+            a = h * PAIR + k
+            mat = par_ref[MAT, a]
+            for i in range(n_i):
+                for j in range(n_j):
+                    ys, xs = slice(i * SUB, (i + 1) * SUB), slice(j * LANES, (j + 1) * LANES)
+                    value = at_edges(
+                        c, i, j, a, all_ref[a, ys, xs], fish_ref, rowc, colw, cole, catch.at[c.month]
+                    )
+                    value = value + recruit_out[ys, xs] * mat
+                    all_ref[a, ys, xs] = value
+                    if i == 0:
+                        top[j, pl.ds(a, 1), :] = value[0:1]
+                    if i == n_i - 1:
+                        bottom[j, pl.ds(a, 1), :] = value[SUB - 1 : SUB]
+        return carry
+
+    lax.fori_loop(0, ages // PAIR, body, 0)
+    place = lax.broadcasted_iota(jnp.int32, (ages, cols), 0)
+    for src, dst, row in ((top, back_out, 0), (bottom, ahead_out, rows - 1)):
+        full = jnp.concatenate([src[j] for j in range(n_j)], axis=1)
+        dst[...] = jnp.where(place == ages - 1, last[row : row + 1, :], pltpu.roll(full, ages - 1, 0))
+    lane = lax.broadcasted_iota(jnp.int32, (SUB, LANES), 1)
+    for i in range(n_i):
+        rs = slice(i * SUB, (i + 1) * SUB)
+        for dst, lo, by, col in ((west_out, 0, 0, 0), (east_out, cols - LANES, 1, cols - 1)):
+            found = jnp.where(lane == ages - 1, last_out[rs, col : col + 1], 0.0)
+            for k in range(1, ages):
+                value = all_ref[k, rs, lo : lo + LANES]
+                found = jnp.where(lane == k - 1, pltpu.roll(value, k - 1 + by, 1) if k - 1 + by else value, found)
+            dst[rs, :] = found
+    both_out[...] = jnp.where(pos_ref[2] == 0, east_out[...], west_out[...])
+
+
+def recruit_edges(sizes, pos, par, sea, yields, fish, nxt, terms, edges, catch, inner):
+    ages, rows, cols = inner.shape
     months = terms[0].shape[0] - 1
+    c = Cfg(rows=rows, cols=cols, ages=ages, months=months, month=months - 1, sizes=sizes)
     line = jax.ShapeDtypeStruct((ages, cols), f32)
     column = jax.ShapeDtypeStruct((rows, LANES), f32)
+    operands = [pos, par, par, sea, yields, fish, nxt, *terms, *edges, catch, inner]
     return pl.pallas_call(
-        functools.partial(recruit_kernel, months, month, ages, sizes, len(terms)),
-        in_specs=[whole(SMEM)] + [whole()] * (4 + len(terms) + 4),
-        out_specs=[whole()] * 7,
-        out_shape=[line, line, column, column, column] + [jax.ShapeDtypeStruct((rows, cols), f32)] * 2,
+        functools.partial(recruit_kernel, c, len(terms)),
+        in_specs=[whole(SMEM), whole(SMEM)] + [whole()] * (len(operands) - 2),
+        out_specs=[whole()] * 8,
+        out_shape=[jax.ShapeDtypeStruct(inner.shape, f32), line, line, column, column, column]
+        + [jax.ShapeDtypeStruct((rows, cols), f32)] * 2,
+        scratch_shapes=[pltpu.VMEM((cols // LANES, ages, LANES), f32)] * 2,
+        input_output_aliases={len(operands) - 1: 0},
+        cost_estimate=pl.CostEstimate(flops=16 * inner.size, bytes_accessed=8 * inner.size, transcendentals=0),
         compiler_params=params_of(8),
         name="recruit_edges",
-    )(pos, parv, sea, yields, nxt, *terms, *edges)
+    )(*operands)
 
 
 class Cfg:
@@ -285,14 +337,14 @@
     return jnp.sum(jnp.where(down == across, row, 0.0), axis=1, keepdims=True)
 
 
-def edge_flux(c, pos_ref, parv_ref, sea_ref, forage_ref, heat4_ref, own, got, msgs, rowc, colw, cole):
+def edge_flux(c, pos_ref, parv_ref, sea_ref, forage_ref, heat4_ref, own, got, msgs, rowc, colw, cole, fish_ref=None):
     rows, cols, ages = c.rows, c.cols, c.ages
     n_coh, n_lat, n_lon = c.sizes
     own_ahead, own_back, own_east, own_west = own
     from_before, from_after, from_west, from_east = got
     msg_before, msg_after, msg_west, msg_east = msgs
     sea_line, prey_line, heat_line = ages, ages + 1 + 2 * c.month, ages + 2 + 2 * c.month
-    kappa, tau, ideal = (column_of(parv_ref, k, ages) for k in (KAPPA, TAU, IDEAL))
+    kappa, tau, ideal, death, gear2 = (column_of(parv_ref, k, ages) for k in (KAPPA, TAU, IDEAL, DEATH, GEAR2))
     has = [
         (pos_ref[1] > 0).astype(f32),
         (pos_ref[1] < n_lat - 1).astype(f32),
@@ -309,23 +361,31 @@
         )
         both = sea_ref[row : row + 1, :].astype(f32) * sea_there * has[k]
         flux = both * (kappa + jnp.maximum(there - here, 0.0)) * (own[0:ages, :] - got[0:ages, :])
+        if fish_ref is not None:
+            flux = flux * jnp.exp2(death - gear2 * fish_ref[row : row + 1, :])
         for j in range(cols // LANES):
             rowc[k, j] = flux[:, j * LANES : (j + 1) * LANES]
-    kappa, tau, ideal = (parv_ref[k : k + 1, :] for k in (KAPPA, TAU, IDEAL))
+    kappa, tau, ideal, death, gear2 = (parv_ref[k : k + 1, :] for k in (KAPPA, TAU, IDEAL, DEATH, GEAR2))
     for k, (col, own, got, msg, dst) in enumerate(
         ((0, own_west, from_west, msg_west, colw), (cols - 1, own_east, from_east, msg_east, cole))
     ):
         here = habitat_of(forage_ref[:, col : col + 1], heat4_ref[:, col : col + 1], ideal, tau)
+        msg = msg.at[0:rows]
         sea_there = msg[:, sea_line : sea_line + 1]
         there = habitat_of(
             sea_there * msg[:, prey_line : prey_line + 1], msg[:, heat_line : heat_line + 1] * 0.25, ideal, tau
         )
         both = sea_ref[:, col : col + 1].astype(f32) * sea_there * has[2 + k]
-        dst[...] = both * (kappa + jnp.maximum(there - here, 0.0)) * (own[...] - got[...])
-
-
-def advance(c, k, a, par_ref, load, tables, out_ref, recruit=None, lines=None):
-    openv, openh, forage, heat4, fish_ref, rowc, colw, cole, catch = tables
+        flux = both * (kappa + jnp.maximum(there - here, 0.0)) * (own[0:rows, :] - got[0:rows, :])
+        if fish_ref is not None:
+            flux = flux * jnp.exp2(death - gear2 * fish_ref[:, col : col + 1])
+        dst[...] = flux
+
+
+def advance(c, k, a, par_ref, load, tables, out_ref, recruit=None):
+    openv, openh, forage, heat4, fish_ref, *edges = tables
+    if edges:
+        rowc, colw, cole, catch = edges
     n_i, n_j = c.rows // SUB, c.cols // LANES
     lane = lax.broadcasted_iota(jnp.int32, (SUB, LANES), 1)
     sub = lax.broadcasted_iota(jnp.int32, (SUB, LANES), 0)
@@ -347,8 +407,10 @@
         return adj, hab, [pltpu.roll(v, SUB - 1, 0) for v in adj], [pltpu.roll(v, SUB - 1, 0) for v in hab]
 
     now = strip(0)
-    above = [jnp.broadcast_to(-rowc[0, j, pl.ds(a, 1), :], (SUB, LANES)) for j in range(n_j)]
-    below = [jnp.broadcast_to(rowc[1, j, pl.ds(a, 1), :], (SUB, LANES)) for j in range(n_j)]
+    above = [jnp.zeros((SUB, LANES), f32)] * n_j
+    if edges:
+        above = [jnp.broadcast_to(-rowc[0, j, pl.ds(a, 1), :], (SUB, LANES)) for j in range(n_j)]
+        below = [jnp.broadcast_to(rowc[1, j, pl.ds(a, 1), :], (SUB, LANES)) for j in range(n_j)]
     for i in range(n_i):
         after = strip(i + 1) if i + 1 < n_i else now
         adj, hab, adj_up, hab_up = now
@@ -361,7 +423,7 @@
             d = openv[at] * (adj[j] - adj_d)
             p = jnp.maximum(g, 0.0) + kappa
             f = p * d
-            if i == n_i - 1:
+            if edges and i == n_i - 1:
                 f = jnp.where(sub == SUB - 1, below[j], f)
             turned = pltpu.roll((p - g) * d, 1, 0)
             out[j] = f - jnp.where(sub == 0, above[j], turned)
@@ -382,25 +444,42 @@
             flows.append(p * d)
             backs.append(pltpu.roll((p - g) * d, 1, 1))
         rs = slice(i * SUB, (i + 1) * SUB)
-        edge_e = pltpu.roll(cole[rs, :], (2 * LANES - 1) - a, 1)
-        edge_w = pltpu.roll(-colw[rs, :], LANES - a, 1)
-        flows[-1] = jnp.where(lane == LANES - 1, edge_e, flows[-1])
+        if edges:
+            edge_e = pltpu.roll(cole[rs, :], (2 * LANES - 1) - a, 1)
+            edge_w = pltpu.roll(-colw[rs, :], LANES - a, 1)
+            flows[-1] = jnp.where(lane == LANES - 1, edge_e, flows[-1])
+        else:
+            edge_w = jnp.zeros((SUB, LANES), f32)
         for j in range(n_j):
             at = tile(i, j)
             came = jnp.where(lane == 0, backs[j - 1] if j else edge_w, backs[j])
             moved = adj[j] - (out[j] + flows[j] - came)
             fish = fish_ref[at]
             survive = jnp.exp2(death - gear2 * fish)
-            caught = catch[i * SUB // BY, j, pl.ds(a, 1), :]
-            value = survive * moved + fish * caught
+            value = survive * moved
+            if edges:
+                value = value + fish * catch[i * SUB // BY, j, pl.ds(a, 1), :]
             if recruit is not None:
                 value = value + recruit[at] * mat
             out_ref[(k,) + at] = value
-            if lines is not None and i == 0:
-                lines[0][j, pl.ds(a, 1), :] = value[0:1]
-            if lines is not None and i == n_i - 1:
-                lines[1][j, pl.ds(a, 1), :] = value[SUB - 1 : SUB]
         now = after
+
+
+def at_edges(c, i, j, a, value, fish_ref, rowc, colw, cole, catch):
+    lane = lax.broadcasted_iota(jnp.int32, (SUB, LANES), 1)
+    sub = lax.broadcasted_iota(jnp.int32, (SUB, LANES), 0)
+    rs = slice(i * SUB, (i + 1) * SUB)
+    n_i, n_j = c.rows // SUB, c.cols // LANES
+    value = value + fish_ref[rs, j * LANES : (j + 1) * LANES] * catch[i * SUB // BY, j, pl.ds(a, 1), :]
+    if i == 0:
+        value = value - jnp.where(sub == 0, rowc[0, j, pl.ds(a, 1), :], 0.0)
+    if i == n_i - 1:
+        value = value - jnp.where(sub == SUB - 1, rowc[1, j, pl.ds(a, 1), :], 0.0)
+    if j == 0:
+        value = value - jnp.where(lane == 0, pltpu.roll(colw[rs, :], LANES - a, 1), 0.0)
+    if j == n_j - 1:
+        value = value - jnp.where(lane == LANES - 1, pltpu.roll(cole[rs, :], (2 * LANES - 1) - a, 1), 0.0)
+    return value
 
 
 def read_plane(ref, k, ys, xs):
@@ -428,16 +507,20 @@
 
     final = step == c.ages // count - 1
     turns = count // PAIR
-    lax.fori_loop(0, jnp.where(final, turns - 1, turns) if c.ages > count else turns - 1, body, 0)
+    fixed = isinstance(step, int)
+    if fixed:
+        lax.fori_loop(0, turns - 1 if final else turns, body, 0)
+    else:
+        lax.fori_loop(0, jnp.where(final, turns - 1, turns), body, 0)
 
     def rest():
         for k in range(count - PAIR, count):
             a = c.ages - count + k
             go(k, a, loader(a) if a + 1 < c.ages else lambda ys, xs: next_ref[ys, xs])
 
-    if c.ages > count:
+    if not fixed:
         pl.when(final)(rest)
-    else:
+    elif final:
         rest()
 
 
@@ -449,27 +532,17 @@
         del refs[:n]
         return out
 
-    pos_ref, par_ref, parv_ref, later_ref = take(4)
+    pos_ref, parv_ref, inner_ref = take(3)
     own, got = take(4), take(4)
-    sea_ref, prey_ref, heat_ref, fish_ref = take(4)
+    sea_ref, fish_ref = take(2)
     fleet_refs = take(c.n_fleet)
-    plane_out, openv, openh, forage, heat4, rowc, colw, cole, catch = take(9)
+    forage, heat4 = take(2)
+    plane_out, rowc, colw, cole, catch = take(5)
     rows, cols, ages, months = c.rows, c.cols, c.ages, c.months
     blocks_y, blocks_x = rows // BY, cols // BX
-    sea = sea_ref[...].astype(f32)
-    line = lax.broadcasted_iota(jnp.int32, (rows, cols), 0)
-    column = lax.broadcasted_iota(jnp.int32, (rows, cols), 1)
-    openv[...] = jnp.where(line == rows - 1, 0.0, sea * pltpu.roll(sea, rows - 1, 0))
-    openh[...] = jnp.where(column == cols - 1, 0.0, sea * pltpu.roll(sea, cols - 1, 1))
-    for t in range(months):
-        heat4[t] = heat_ref[t] * 0.25
-        forage[t] = sea * prey_ref[t]
-    edge_flux(c, pos_ref, parv_ref, sea_ref, forage.at[c.month], heat4.at[c.month], own, got, got, rowc, colw, cole)
-
-    flat = []
-    for ref in fleet_refs:
-        flat += [ref[:, 0:LANES], ref[:, LANES : 2 * LANES]]
-    flat = jnp.concatenate(flat, axis=0)
+    edge_flux(c, pos_ref, parv_ref, sea_ref, forage.at[c.month], heat4.at[c.month], own, got, got, rowc, colw, cole, fish_ref)
+
+    flat = jnp.concatenate([ref[...] for ref in fleet_refs], axis=0)
     names = flat[:, months * ages : months * ages + 1]
     turned = flat.T[0 : months * ages]
     base = ((pos_ref[1] * c.sizes[2] + pos_ref[2]) * (blocks_y * blocks_x)).astype(f32)
@@ -482,39 +555,26 @@
             for j in range(cols // LANES):
                 catch[t, by, j] = gear * sums[t * ages : (t + 1) * ages, j * LANES : (j + 1) * LANES]
 
-    tables = (openv, openh, forage.at[c.month], heat4.at[c.month], fish_ref, rowc, colw, cole, catch.at[c.month])
-    advance(c, 0, 0, par_ref, lambda ys, xs: read_plane(later_ref, 1, ys, xs), tables, plane_out)
+    for i in range(rows // SUB):
+        for j in range(cols // LANES):
+            ys, xs = slice(i * SUB, (i + 1) * SUB), slice(j * LANES, (j + 1) * LANES)
+            plane_out[0, ys, xs] = at_edges(
+                c, i, j, 0, inner_ref[0, ys, xs], fish_ref, rowc, colw, cole, catch.at[c.month]
+            )
     plane_out[0, rows : rows + SUB, :] = jnp.broadcast_to(
         jnp.broadcast_to(parv_ref[MAT : MAT + 1, 0:1], (1, cols)), (SUB, cols)
     )
 
 
 def month_kernel(c, *refs):
-    refs = list(refs)
-
-    def take(n):
-        out = refs[:n]
-        del refs[:n]
-        return out
-
-    par_ref, later_ref, next_ref, fish_ref = take(4)
-    openv, openh, forage, heat4, rowc, colw, cole, catch = take(8)
-    out_ref, top_out, bottom_out, west_out, east_out = take(5)
-    tables = (openv, openh, forage.at[c.month], heat4.at[c.month], fish_ref, rowc, colw, cole, catch.at[c.month])
+    par_ref, later_ref, next_ref, fish_ref, openv, openh, forage, heat4 = refs[:8]
+    out_ref = refs[-1]
+    tables = (openv, openh, forage.at[c.month], heat4.at[c.month], fish_ref)
 
     def go(k, a, load):
-        advance(c, k, a, par_ref, load, tables, out_ref, lines=(top_out, bottom_out))
-
-    all_cohorts(c, 0, c.ages, par_ref, later_ref, next_ref, None, go)
-    lane = lax.broadcasted_iota(jnp.int32, (SUB, LANES), 1)
-    for i in range(c.rows // SUB):
-        rs = slice(i * SUB, (i + 1) * SUB)
-        for dst, lo, by in ((west_out, 0, 0), (east_out, c.cols - LANES, 1)):
-            found = jnp.zeros((SUB, LANES), f32)
-            for k in range(c.ages):
-                value = out_ref[k, rs, lo : lo + LANES]
-                found = jnp.where(lane == k, pltpu.roll(value, k + by, 1) if k + by else value, found)
-            dst[rs, :] = found
+        advance(c, a, a, par_ref, load, tables, out_ref)
+
+    all_cohorts(c, c.part, c.ages // PARTS, par_ref, later_ref, next_ref, None, go)
 
 
 def last_kernel(c, *refs):
@@ -556,7 +616,7 @@
     def go(k, a, load):
         advance(c, k, a, par_ref, load, tables, out_ref, recruit=final_recruit)
 
-    all_cohorts(c, step, GROUP, par_ref, later_ref, next_ref, recruit_ref, go)
+    all_cohorts(c, step, GROUP, par_ref, later_ref, next_ref, None, go)
 
 
 def cost(planes, rows, cols):
@@ -572,13 +632,13 @@
     ]
 
 
-def first_cohort(sizes, pos, par, fin, own, got, sea, prey, heat, fish, fleet_blocks):
-    ages, rows, cols = fin.shape
-    months = prey.shape[0]
+def first_cohort(sizes, pos, par, inner, own, got, sea, fish, fleet_blocks, forage, heat4):
+    ages, rows, cols = inner.shape
+    months = forage.shape[0]
     c = Cfg(rows=rows, cols=cols, ages=ages, months=months, month=months - 1, sizes=sizes, n_fleet=len(fleet_blocks))
-    operands = [pos, par, par, fin, *own, *got, sea, prey, heat, fish]
+    operands = [pos, par, inner, *own, *got, sea, fish]
     at = len(operands)
-    operands += [block for block, _ in fleet_blocks]
+    operands += [block for block, _ in fleet_blocks] + [forage, heat4]
 
     def kernel(*refs):
         refs = list(refs)
@@ -587,14 +647,12 @@
                 refs[at + k] = refs[at + k].at[start : block.shape[0]]
         first_kernel(c, *refs)
 
-    plane = jax.ShapeDtypeStruct((rows, cols), f32)
-    stack = jax.ShapeDtypeStruct((months, rows, cols), f32)
-    out_shape = [jax.ShapeDtypeStruct((1, rows + SUB, cols), f32), plane, plane, stack, stack]
+    out_shape = [jax.ShapeDtypeStruct((1, rows + SUB, cols), f32)]
     out_shape += edge_shapes(ages, rows, cols)
     out_shape.append(jax.ShapeDtypeStruct((months, rows // BY, cols // LANES, ages, LANES), f32))
     return pl.pallas_call(
         kernel,
-        in_specs=[whole(SMEM), whole(SMEM)] + [whole()] * (len(operands) - 2),
+        in_specs=[whole(SMEM)] + [whole()] * (len(operands) - 1),
         out_specs=[whole()] * len(out_shape),
         out_shape=out_shape,
         cost_estimate=cost(4, rows, cols),
@@ -603,21 +661,26 @@
     )(*operands)
 
 
-def month_step(sizes, par, fin, nxt, fish, fields, edges, catch):
+def month_inner(sizes, part, par, fin, nxt, fish, fields, before, ahead_of):
     ages, rows, cols = fin.shape
-    months = catch.shape[0]
-    c = Cfg(rows=rows, cols=cols, ages=ages, months=months, month=months - 1, sizes=sizes)
-    operands = [par, fin, nxt, fish, *fields, *edges, catch]
-    line = jax.ShapeDtypeStruct((cols // LANES, ages, LANES), f32)
-    column = jax.ShapeDtypeStruct((rows, LANES), f32)
+    months = fields[2].shape[0]
+    c = Cfg(rows=rows, cols=cols, ages=ages, months=months, month=months - 1, sizes=sizes, part=part)
+    operands = [par, fin, nxt, fish, *fields, ahead_of]
+    specs = [whole(SMEM)] + [whole()] * (len(operands) - 2) + [pl.BlockSpec(memory_space=pl.ANY)]
+    alias = {}
+    if before is not None:
+        alias = {len(operands): 0}
+        operands.append(before)
+        specs.append(whole())
     return pl.pallas_call(
         functools.partial(month_kernel, c),
-        in_specs=[whole(SMEM)] + [whole()] * (len(operands) - 1),
-        out_specs=[whole()] * 5,
-        out_shape=[jax.ShapeDtypeStruct((ages, rows, cols), f32), line, line, column, column],
-        cost_estimate=cost(ages, rows, cols),
+        in_specs=specs,
+        out_specs=whole(),
+        out_shape=jax.ShapeDtypeStruct((ages, rows, cols), f32),
+        input_output_aliases=alias,
+        cost_estimate=cost(ages // PARTS, rows, cols),
         compiler_params=params_of(16),
-        name="month_step",
+        name="month_inner",
     )(*operands)
 
 
@@ -682,33 +745,34 @@
 
     first = fin[0].astype(f32)
     nxt = shift(first, "coh", -1)
-    fleet_lon = [fleet] + [shift(fleet, "lon", d) for d in range(1, n_lon)]
     terms = first_terms(spawn_parts(pos, breeding, ages * n_coh, saved, first, first), "coh")
 
-    ahead, back, east, west, both, fleet_pack, later_last, par = pack_edges(
-        sizes, pos, fin, nxt, sea, prey, heat, fleet_lon, (death, gear, kappa, tau, ideal, breeding)
+    ahead, back, east, west, fleet_pack, later_last, par, *fields = pack_edges(
+        sizes, pos, fin, nxt, sea, prey, heat, [fleet], (death, gear, kappa, tau, ideal, breeding)
     )
+    from_before, from_after = shift(ahead, "lat", 1), shift(back, "lat", -1)
+    blocks = [ahead, from_before] + ([from_after] if n_lat > 2 else [])
+    blocks += [shift(fleet_pack, "lat", d) for d in range(2, n_lat - 1)]
+    inner = month_inner(sizes, 0, par, fin, later_last, fish, fields, None, ahead)
+    both, gathered = relay(pos, east, west, inner, blocks, fleet_pack.shape[0])
+    terms = other_terms(terms, "coh", both)
+    inner = month_inner(sizes, 1, par, fin, later_last, fish, fields, inner, both)
     from_west, from_east = swap_edges(east, west, both, "lon")
-    from_before, from_after = shift(ahead, "lat", 1), shift(back, "lat", -1)
-    start = ahead.shape[0] - fleet_pack.shape[0]
-    terms = other_terms(terms, "coh", both)
-    fleet_blocks = [(ahead, start), (from_before, start)]
-    if n_lat > 2:
-        fleet_blocks.append((from_after, start))
-    fleet_blocks += [(shift(fleet_pack, "lat", d), 0) for d in range(2, n_lat - 1)]
-
+    fleet_blocks = [(gathered, 0)]
+    if n_lon == 2:
+        fleet_blocks.append((from_west, rows))
+    else:
+        fleet_blocks += [(shift(gathered, "lon", d), 0) for d in range(1, n_lon)]
     own = (ahead, back, east, west)
     msgs = (from_before, from_after, from_west, from_east)
-    plane, openv, openh, forage, heat4, *edges, catch = first_cohort(
-        sizes, pos, par, fin, own, msgs, sea, prey, heat, fish, fleet_blocks
+    plane, *edges, catch = first_cohort(
+        sizes, pos, par, inner, own, msgs, sea, fish, fleet_blocks, fields[2], fields[3]
     )
     plane = plane.reshape(rows + SUB, cols)
-    fields = (openv, openh, forage, heat4)
     down = shift(plane, "coh", -1)
     bcasts = [plane, down] + [lax.ppermute(plane, "coh", [(0, j)]) for j in range(1, n_coh - 1)]
-    later, *edges = month_step(sizes, par, fin, later_last, fish, fields, edges, catch)
-    ahead, back, east, west, both, recruit, nxt = recruit_edges(
-        sizes, months - 1, pos, par, sea, yields, down, terms, edges
+    later, ahead, back, east, west, both, recruit, nxt = recruit_edges(
+        sizes, pos, par, sea, yields, fish, down, terms, edges, catch, inner
     )
     own = (ahead, back, east, west)
     got = (shift(ahead, "lat", 1), shift(back, "lat", -1), *swap_edges(east, west, both, "lon"))

time: 49.8 us -> 45.8 us (0.920)
  waiting for transfers between devices: 8.52 us -> 4.08 us
  Pallas kernels: 16.5 us -> 18.6 us
  starting transfers between devices: 19.9 us -> 18.2 us
    ppermute x10 -> x9, waiting for transfers between devices: 7.22 us -> 4.07 us  [shift(): return lax.ppermute(x, axis, [(i, (i + distance) % n) for i in range(n)])]
    ppermute x10 -> x9, starting transfers between devices: 17.2 us -> 15.1 us  [shift(): return lax.ppermute(x, axis, [(i, (i + distance) % n) for i in range(n)])]
    pallas_call x3 -> x5, Pallas kernels: 7.85 us -> 9.94 us  [the longest x2 4.89 us: month_inner(): pl.pallas_call(functools.partial(month_kernel, c), in_specs=specs, out_sp...]
    ppermute x2, waiting for transfers between devices: 1.3 us -> 0.01 us  [flipped(): lax.ppermute(x, axis, [(i, i ^ reach) for i in range(lax.axis_size(axis))])]
  transfers between devices with their start and end apart: 14 -> 13, of which waited for: 7 -> 4; matrix products, arithmetic and copies ran while one was open for 1% -> 1% of each run, Pallas kernels for 20% -> 27%
where the time goes in v3:
time: 45.8 us; the launch traced here: 45.6 us
  Pallas kernels  18.6 us (41%)
  starting transfers between devices  18.2 us (40%)
  waiting for transfers between devices  4.08 us (9%)
  local copies, waits for them, and re-layouts  2.52 us (6%)
  other arithmetic  1.11 us (2%)
  between operations  1.01 us (2%)
    ppermute x9, starting transfers between devices, shift(): return lax.ppermute(x, axis, [(i, (i + distance) % n) for i in range(n)])  15.1 us
    pallas_call x1, Pallas kernels, month_last(): pl.pallas_call(functools.partial(last_kernel, c), grid=(ages // GROUP,),...  6.33 us
    pallas_call x2, Pallas kernels, month_inner(): pl.pallas_call(functools.partial(month_kernel, c), in_specs=specs, out_sp...  4.89 us
    ppermute x9, waiting for transfers between devices, shift(): return lax.ppermute(x, axis, [(i, (i + distance) % n) for i in range(n)])  4.07 us
    pallas_call x1, Pallas kernels, recruit_edges(): pl.pallas_call(functools.partial(recruit_kernel, c, len(terms)), in_specs...  2.96 us
    ppermute x2, starting transfers between devices, shards(): lax.ppermute(plane, 'coh', [(0, j)])  2.58 us
    unnamed x38, local copies, waits for them, and re-layouts  2.34 us
    pallas_call x1, Pallas kernels, first_cohort(): pl.pallas_call(kernel, in_specs=[whole(SMEM)] + [whole()] * (len(operands...  1.53 us
  transfers between devices with their start and end apart: 13, of which 4 were waited for; matrix products, arithmetic and copies ran while one was open for 1% of the time, Pallas kernels for 27%

profile of v3, /device:TPU:1, one launch (start us, length us, event | category | flops | bytes accessed | tf_op | source)
XLA Modules:
  0.0 45.6 jit_solution(109197783932083668)
XLA Ops:
  0.6 0.9 %bitcast_convert_fusion.first_ref._ = f32[64,256]{1,0:T(8,128)S(1)} fusion(bf16[32,64,256]{2,1,0:T(8,128)(2,1)} %refs_1_.5), kind=kLoop, calls=%fused_computation | loop fusion | flops 16384 | bytes 98304 | tf_op jit(solution)/shard_map/convert_element_type | solution.py:746
  1.5 4.2 %collective-permute-start = (f32[64,256]{1,0:T(8,128)S(1)}, f32[64,256]{1,0:T(8,128)S(1)}, u32[]{:S(2)}, u32[]{:S(2)}) collective-permute-start(f32[64,256]{1,0:T(8,128)S(1)} %bitcast_convert_fusion.first_ref._), channel_id=1, source_target_pairs={{0,24},{8,0},{16,8},{24,16},{1,25},{9,1},{17,9},{25,17},{2,26},{10... | collective-permute-start | bytes 196616 | tf_op jit(solution)/shard_map/ppermute | solution.py:42
  5.6 0.1 pad_add_fusion.refs_0_.pos_ref
  5.7 1.6 %copy-done.1 = bf16[2,32,64,256]{3,2,1,0:T(8,128)(2,1)S(1)} copy-done((bf16[2,32,64,256]{3,2,1,0:T(8,128)(2,1)S(1)}, bf16[2,32,64,256]{3,2,1,0:T(8,128)(2,1)}, u32[]{:S(2)}) %copy-start.1) | copy-done | bytes 2097176
  7.3 0.7 %copy-done.7 = f32[32]{0:T(128)S(1)} copy-done((f32[32]{0:T(128)S(1)}, f32[32]{0:T(128)}, u32[]{:S(2)}) %copy-start.7) | copy-done | bytes 152
  8.1 1.3 %spawn_parts.1.a_ref = f32[3,64,256]{2,1,0:T(8,128)S(1)} custom-call(s32[3]{0:T(128)S(1)} %pad_add_fusion.refs_0_.pos_ref, f32[32]{0:T(128)S(1)} %copy-done.7, bf16[2,32,64,256]{3,2,1,0:T(8,128)(2,1)S(1)} %copy-done.1, f32[64,256]{1,0:T(8,128)S(1)} %bitcast_convert_fusion.first_ref._, f32[64,256]{1,0:T(8,128)S(1)} %bitcast_convert_fusion.first_ref._), custom_call_target="tpu_custom_call" | custom-call | tf_op jit(solution)/shard_map/spawn_parts/pallas_call | solution.py:69
  9.4 0.1 collective-permute-start.6
  9.5 0.1 and_convert_fusion
  9.7 0.1 copy.22
  9.8 0.1 reshape.85
  9.8 0.1 select_maximum_fusion.refs_6_
  10.0 1.0 %pack_edges.1 = (f32[56,256]{1,0:T(8,128)S(1)}, f32[56,256]{1,0:T(8,128)S(1)}, f32[64,128]{1,0:T(8,128)S(1)}, f32[64,128]{1,0:T(8,128)S(1)}, f32[16,256]{1,0:T(8...) custom-call(s32[3]{0:T(128)S(1)} %pad_add_fusion.refs_0_.pos_ref, ...), custom_call_target="tpu_custom_call" | custom-call | tf_op jit(solution)/shard_map/pack_edges/pallas_call | solution.py:235
  11.0 1.0 %collective-permute-start.2 = (f32[56,256]{1,0:T(8,128)S(1)}, f32[56,256]{1,0:T(8,128)S(1)}, u32[]{:S(2)}, u32[]{:S(2)}) collective-permute-start(f32[56,256]{1,0:T(8,128)S(1)} %get-tuple-element.37.refs_4_), channel_id=1, source_target_pairs={{0,6},{2,0},{4,2},{6,4},{1,7},{3,1},{5,3},{7,5},{8,14},{10,8},{12,... | collective-permute-start | bytes 172040 | tf_op jit(solution)/shard_map/ppermute | solution.py:42
  12.1 1.2 %collective-permute-start.1 = (f32[56,256]{1,0:T(8,128)S(1)}, f32[56,256]{1,0:T(8,128)S(1)}, u32[]{:S(2)}, u32[]{:S(2)}) collective-permute-start(f32[56,256]{1,0:T(8,128)S(1)} %get-tuple-element.36.refs_8_.refs_0_.refs_3_), channel_id=1, source_target_pairs={{0,2},{2,4},{4,6},{6,0},{1,3},{3,5},{5,7},{7,1},{8,10},{10,12},{12... | collective-permute-start | bytes 172040 | tf_op jit(solution)/shard_map/ppermute | solution.py:42
  13.2 0.8 %collective-permute-start.3 = (f32[16,256]{1,0:T(8,128)S(1)}, f32[16,256]{1,0:T(8,128)S(1)}, u32[]{:S(2)}, u32[]{:S(2)}) collective-permute-start(f32[16,256]{1,0:T(8,128)S(1)} %get-tuple-element.38), channel_id=1, source_target_pairs={{0,4},{2,6},{4,0},{6,2},{1,5},{3,7},{5,1},{7,3},{8,12},{10,14},{12... | collective-permute-start | bytes 49160 | tf_op jit(solution)/shard_map/ppermute | solution.py:42
  14.1 2.4 %month_inner.2._.refs_9_ = f32[32,64,256]{2,1,0:T(8,128)S(1)} custom-call(f32[8,128]{1,0:T(8,128)S(1)} %get-tuple-element.28.refs_0_.refs_1_.refs_2_, bf16[32,64,256]{2,1,0:T(8,128)(2,1)S(1)} %copy-done, f32[64,256]{1,0:T(8,128)S(1)} %get-tuple-element.29.refs_2_, f32[64,256]{1,0:T(8,128)S(1)} %copy-done.2, f32[64,256]{1,0:T(8,128)S(1)} %get-tuple-element.30.refs_4_.refs_9_, ...), custom_call_target="tpu_custom_call" | custom-call | flops 15728640 | bytes 2097152 | tf_op jit(solution)/shard_map/month_inner/pallas_call | solution.py:675
  16.5 0.6 %relay.1 = (f32[192,128]{1,0:T(8,128)S(1)}, f32[128,128]{1,0:T(8,128)S(1)}) custom-call(s32[3]{0:T(128)S(1)} %pad_add_fusion.refs_0_.pos_ref, f32[64,128]{1,0:T(8,128)S(1)} %get-tuple-element.34.east_ref.refs_5_, f32[64,128]{1,0:T(8,128)S(1)} %get-tuple-element.35.west_ref.refs_6_, f32[32,64,256]{2,1,0:T(8,128)S(1)} %month_inner.2._.refs_9_, ...), custom_call_target="tpu_custom_call" | custom-call | tf_op jit(solution)/shard_map/relay/pallas_call | solution.py:218
  17.2 0.5 %collective-permute-start.7 = (f32[3,64,256]{2,1,0:T(8,128)S(1)}, f32[3,64,256]{2,1,0:T(8,128)S(1)}, u32[]{:S(2)}, u32[]{:S(2)}) collective-permute-start(f32[3,64,256]{2,1,0:T(8,128)S(1)} %add_after.1.refs_7_.refs_26_), channel_id=1, source_target_pairs={{0,16},{8,24},{16,0},{24,8},{1,17},{9,25},{17,1},{25,9},{2,18},{10... | collective-permute-start | bytes 589832 | tf_op jit(solution)/shard_map/ppermute | solution.py:102
  17.6 1.2 %collective-permute-start.4 = (f32[192,128]{1,0:T(8,128)S(1)}, f32[192,128]{1,0:T(8,128)S(1)}, u32[]{:S(2)}, u32[]{:S(2)}) collective-permute-start(f32[192,128]{1,0:T(8,128)S(1)} %get-tuple-element.39.refs_8_._), channel_id=1, source_target_pairs={{0,1},{1,0},{2,3},{3,2},{4,5},{5,4},{6,7},{7,6},{8,9},{9,8},{10,11... | collective-permute-start | bytes 294920 | tf_op jit(solution)/shard_map/ppermute | solution.py:42
  18.9 2.4 %month_inner.3.refs_2_.refs_13_ = f32[32,64,256]{2,1,0:T(8,128)S(1)} custom-call(f32[8,128]{1,0:T(8,128)S(1)} %get-tuple-element.28.refs_0_.refs_1_.refs_2_, bf16[32,64,256]{2,1,0:T(8,128)(2,1)S(1)} %copy-done, f32[64,256]{1,0:T(8,128)S(1)} %get-tuple-element.29.refs_2_, f32[64,256]{1,0:T(8,128)S(1)} %copy-done.2, ...), custom_call_target="tpu_custom_call", output_to_operand_aliasing={{}: (9, {})} | custom-call | flops 15728640 | bytes 2097152 | tf_op jit(solution)/shard_map/month_inner/pallas_call | solution.py:675
  21.3 0.1 collective-permute-done.4.refs_9_.refs_10_.refs_14_.refs_24_.refs_25_
  21.4 1.5 %first_cohort.1 = (f32[1,72,256]{2,1,0:T(8,128)S(1)}, f32[2,2,32,128]{3,2,1,0:T(8,128)S(1)}, f32[64,128]{1,0:T(8,128)S(1)}, f32[64,128]{1,0:T(8,128)S(1)}, f32[2,4,2,32,128]{4,3,2,1,0:T(8,128)S(1)}) custom-call(s32[3]{0:T(128)S(1)} %pad_add_fusion.refs_0_.pos_ref, f32[8,128]{1,0:T(8,128)S(1)} %get-tuple-element.28.refs_0_.refs_1_.refs_2_, ...), custom_call_target="tpu_custom_call" | custom-call | flops 3932160 | bytes 524288 | tf_op jit(solution)/shard_map/first_cohort/pallas_call | solution.py:653
  23.0 3.1 %collective-permute-start.5 = (f32[72,256]{1,0:T(8,128)S(1)}, f32[72,256]{1,0:T(8,128)S(1)}, u32[]{:S(2)}, u32[]{:S(2)}) collective-permute-start(f32[72,256]{1,0:T(8,128)S(1)} %bitcast.27), channel_id=1, source_target_pairs={{0,24},{8,0},{16,8},{24,16},{1,25},{9,1},{17,9},{25,17},{2,26},{10... | collective-permute-start | bytes 221192 | tf_op jit(solution)/shard_map/ppermute | solution.py:42
  26.1 1.3 %collective-permute-start.12 = (f32[72,256]{1,0:T(8,128)S(1)}, f32[72,256]{1,0:T(8,128)S(1)}, u32[]{:S(2)}, u32[]{:S(2)}) collective-permute-start(f32[72,256]{1,0:T(8,128)S(1)} %bitcast.28), channel_id=1, source_target_pairs={{0,16},{1,17},{2,18},{3,19},{4,20},{5,21},{6,22},{7,23}} | collective-permute-start | bytes 221192 | tf_op jit(solution)/shard_map/ppermute | solution.py:773
  27.4 1.3 %collective-permute-start.11 = (f32[72,256]{1,0:T(8,128)S(1)}, f32[72,256]{1,0:T(8,128)S(1)}, u32[]{:S(2)}, u32[]{:S(2)}) collective-permute-start(f32[72,256]{1,0:T(8,128)S(1)} %bitcast.29), channel_id=1, source_target_pairs={{0,8},{1,9},{2,10},{3,11},{4,12},{5,13},{6,14},{7,15}} | collective-permute-start | bytes 221192 | tf_op jit(solution)/shard_map/ppermute | solution.py:773
  28.7 0.7 %collective-permute-done.5.refs_6_.refs_29_ = f32[72,256]{1,0:T(8,128)S(1)} collective-permute-done((f32[72,256]{1,0:T(8,128)S(1)}, f32[72,256]{1,0:T(8,128)S(1)}, u32[]{:S(2)}, u32[]{:S(2)}) %collective-permute-start.5) | collective-permute-done | bytes 73760 | tf_op jit(solution)/shard_map/ppermute | solution.py:42
  29.4 3.0 %recruit_edges.1 = (f32[32,64,256]{2,1,0:T(8,128)S(1)}, f32[32,256]{1,0:T(8,128)S(1)}, f32[32,256]{1,0:T(8,128)S(1)}, f32[64,128]{1,0:T(8,128)S(1)}, f32[64,128]...) custom-call(s32[3]{0:T(128)S(1)} %pad_add_fusion.refs_0_.pos_ref, ...), custom_call_target="tpu_custom_call", output_to_operand_aliasing={{0}: (13, {})} | custom-call | flops 8388608 | bytes 4194304 | tf_op jit(solution)/shard_map/recruit_edges/pallas_call | solution.py:314
  32.3 1.3 %collective-permute-start.10 = (f32[64,128]{1,0:T(8,128)S(1)}, f32[64,128]{1,0:T(8,128)S(1)}, u32[]{:S(2)}, u32[]{:S(2)}) collective-permute-start(f32[64,128]{1,0:T(8,128)S(1)} %get-tuple-element.53), channel_id=1, source_target_pairs={{0,1},{1,0},{2,3},{3,2},{4,5},{5,4},{6,7},{7,6},{8,9},{9,8},{10,11... | collective-permute-start | bytes 98312 | tf_op jit(solution)/shard_map/ppermute | solution.py:42
  33.6 2.2 %collective-permute-start.8 = (f32[32,256]{1,0:T(8,128)S(1)}, f32[32,256]{1,0:T(8,128)S(1)}, u32[]{:S(2)}, u32[]{:S(2)}) collective-permute-start(f32[32,256]{1,0:T(8,128)S(1)} %get-tuple-element.49.refs_14_), channel_id=1, source_target_pairs={{0,2},{2,4},{4,6},{6,0},{1,3},{3,5},{5,7},{7,1},{8,10},{10,12},{12... | collective-permute-start | bytes 98312 | tf_op jit(solution)/shard_map/ppermute | solution.py:42
  35.9 1.0 %collective-permute-done.8.refs_18_ = f32[32,256]{1,0:T(8,128)S(1)} collective-permute-done((f32[32,256]{1,0:T(8,128)S(1)}, f32[32,256]{1,0:T(8,128)S(1)}, u32[]{:S(2)}, u32[]{:S(2)}) %collective-permute-start.8) | collective-permute-done | bytes 32800 | tf_op jit(solution)/shard_map/ppermute | solution.py:42
  36.9 2.3 %collective-permute-done.9.refs_19_ = f32[32,256]{1,0:T(8,128)S(1)} collective-permute-done((f32[32,256]{1,0:T(8,128)S(1)}, f32[32,256]{1,0:T(8,128)S(1)}, u32[]{:S(2)}, u32[]{:S(2)}) %collective-permute-start.9) | collective-permute-done | bytes 32800 | tf_op jit(solution)/shard_map/ppermute | solution.py:42
  39.2 6.3 %month_last.1 = (f32[32,64,256]{2,1,0:T(8,128)}, f32[64,256]{1,0:T(8,128)}) custom-call(s32[3]{0:T(128)S(1)} %pad_add_fusion.refs_0_.pos_ref, f32[8,128]{1,0:T(8,128)S(1)} %get-tuple-element.28.refs_0_.refs_1_.refs_2_, f32[8,128]{1,0:T(8,128)S(1)} %get-tuple-element.28.refs_0_.refs_1_.refs_2_, f32[32,64,256]{2,1,0:T(8,128)S(1)} %get-tuple-element.46.refs_3_, ...), custom_call_target="tpu_custom_call" | custom-call | flops 31457280 | bytes 4194304 | tf_op jit(solution)/shard_map/month_last/pallas_call | solution.py:696
  (51 shorter events, 0.2 us)
Async XLA Ops:
  0.6 9.3 %copy-start = (bf16[32,64,256]{2,1,0:T(8,128)(2,1)S(1)}, bf16[32,64,256]{2,1,0:T(8,128)(2,1)}, u32[]{:S(2)}) copy-start(bf16[32,64,256]{2,1,0:T(8,128)(2,1)} %refs_1_.5) | copy-start | bytes 3145732
  1.5 8.4 %collective-permute-start = (f32[64,256]{1,0:T(8,128)S(1)}, f32[64,256]{1,0:T(8,128)S(1)}, u32[]{:S(2)}, u32[]{:S(2)}) collective-permute-start(f32[64,256]{1,0:T(8,128)S(1)} %bitcast_convert_fusion.first_ref._), channel_id=1, source_target_pairs={{0,24},{8,0},{16,8},{24,16},{1,25},{9,1},{17,9},{25,17},{2,26},{10... | collective-permute-start | bytes 196616 | tf_op jit(solution)/shard_map/ppermute | solution.py:42
  5.7 1.6 %copy-start.1 = (bf16[2,32,64,256]{3,2,1,0:T(8,128)(2,1)S(1)}, bf16[2,32,64,256]{3,2,1,0:T(8,128)(2,1)}, u32[]{:S(2)}) copy-start(bf16[2,32,64,256]{3,2,1,0:T(8,128)(2,1)} %saved_ref.1) | copy-start | bytes 6291460
  7.3 0.7 %copy-start.7 = (f32[32]{0:T(128)S(1)}, f32[32]{0:T(128)}, u32[]{:S(2)}) copy-start(f32[32]{0:T(128)} %breed_ref.1) | copy-start | bytes 388
  8.0 1.5 %copy-start.15 = (s32[32,2]{0,1:T(2,128)S(1)}, s32[32,2]{0,1:T(2,128)}, u32[]{:S(2)}) copy-start(s32[32,2]{0,1:T(2,128)} %param.35) | copy-start | bytes 772
  8.0 1.6 %copy-start.14 = (f32[32,2,32]{2,1,0:T(2,128)S(1)}, f32[32,2,32]{2,1,0:T(2,128)}, u32[]{:S(2)}) copy-start(f32[32,2,32]{2,1,0:T(2,128)} %param.31) | copy-start | bytes 24580
  8.0 1.7 %copy-start.16 = (s32[32]{0:T(128)S(1)}, s32[32]{0:T(128)}, u32[]{:S(2)}) copy-start(s32[32]{0:T(128)} %param.34) | copy-start | bytes 388
  8.0 1.7 %copy-start.17 = (s32[32,1]{0,1:T(1,128)S(1)}, s32[32,1]{0,1:T(1,128)}, u32[]{:S(2)}) copy-start(s32[32,1]{0,1:T(1,128)} %param.32) | copy-start | bytes 388
  8.0 1.7 %copy-start.18 = (s32[32]{0:T(128)S(1)}, s32[32]{0:T(128)}, u32[]{:S(2)}) copy-start(s32[32]{0:T(128)} %param.33) | copy-start | bytes 388
  8.0 1.9 %copy-start.3 = (s32[64,256]{1,0:T(8,128)S(1)}, s32[64,256]{1,0:T(8,128)}, u32[]{:S(2)}) copy-start(s32[64,256]{1,0:T(8,128)} %refs_6_.1) | copy-start | bytes 196612
  8.0 1.9 %copy-start.5 = (f32[2,64,256]{2,1,0:T(8,128)S(1)}, f32[2,64,256]{2,1,0:T(8,128)}, u32[]{:S(2)}) copy-start(f32[2,64,256]{2,1,0:T(8,128)} %refs_4_.2) | copy-start | bytes 393220
  8.0 1.9 %copy-start.6 = (f32[2,64,256]{2,1,0:T(8,128)S(1)}, f32[2,64,256]{2,1,0:T(8,128)}, u32[]{:S(2)}) copy-start(f32[2,64,256]{2,1,0:T(8,128)} %refs_5_.2) | copy-start | bytes 393220
  8.0 1.9 %copy-start.8 = (f32[32]{0:T(128)S(1)}, f32[32]{0:T(128)}, u32[]{:S(2)}) copy-start(f32[32]{0:T(128)} %breed_ref.1) | copy-start | bytes 388
  8.0 1.9 %copy-start.9 = (f32[32]{0:T(128)S(1)}, f32[32]{0:T(128)}, u32[]{:S(2)}) copy-start(f32[32]{0:T(128)} %param.25) | copy-start | bytes 388
  8.0 1.9 %copy-start.10 = (f32[32]{0:T(128)S(1)}, f32[32]{0:T(128)}, u32[]{:S(2)}) copy-start(f32[32]{0:T(128)} %param.26) | copy-start | bytes 388
  8.1 1.9 %copy-start.11 = (f32[32]{0:T(128)S(1)}, f32[32]{0:T(128)}, u32[]{:S(2)}) copy-start(f32[32]{0:T(128)} %param.27) | copy-start | bytes 388
  8.1 1.9 %copy-start.12 = (f32[32]{0:T(128)S(1)}, f32[32]{0:T(128)}, u32[]{:S(2)}) copy-start(f32[32]{0:T(128)} %param.28) | copy-start | bytes 388
  8.1 1.9 %copy-start.13 = (f32[32]{0:T(128)S(1)}, f32[32]{0:T(128)}, u32[]{:S(2)}) copy-start(f32[32]{0:T(128)} %param.29) | copy-start | bytes 388
  8.1 6.0 %copy-start.2 = (f32[64,256]{1,0:T(8,128)S(1)}, f32[64,256]{1,0:T(8,128)}, u32[]{:S(2)}) copy-start(f32[64,256]{1,0:T(8,128)} %refs_7_.1) | copy-start | bytes 196612
  9.4 7.7 %collective-permute-start.6 = (f32[3,64,256]{2,1,0:T(8,128)S(1)}, f32[3,64,256]{2,1,0:T(8,128)S(1)}, u32[]{:S(2)}, u32[]{:S(2)}) collective-permute-start(f32[3,64,256]{2,1,0:T(8,128)S(1)} %spawn_parts.1.a_ref), channel_id=1, source_target_pairs={{0,8},{8,0},{16,24},{24,16},{1,9},{9,1},{17,25},{25,17},{2,10},{10... | collective-permute-start | bytes 589832 | tf_op jit(solution)/shard_map/ppermute | solution.py:102
  11.0 5.5 %collective-permute-start.2 = (f32[56,256]{1,0:T(8,128)S(1)}, f32[56,256]{1,0:T(8,128)S(1)}, u32[]{:S(2)}, u32[]{:S(2)}) collective-permute-start(f32[56,256]{1,0:T(8,128)S(1)} %get-tuple-element.37.refs_4_), channel_id=1, source_target_pairs={{0,6},{2,0},{4,2},{6,4},{1,7},{3,1},{5,3},{7,5},{8,14},{10,8},{12,... | collective-permute-start | bytes 172040 | tf_op jit(solution)/shard_map/ppermute | solution.py:42
  12.1 4.5 %collective-permute-start.1 = (f32[56,256]{1,0:T(8,128)S(1)}, f32[56,256]{1,0:T(8,128)S(1)}, u32[]{:S(2)}, u32[]{:S(2)}) collective-permute-start(f32[56,256]{1,0:T(8,128)S(1)} %get-tuple-element.36.refs_8_.refs_0_.refs_3_), channel_id=1, source_target_pairs={{0,2},{2,4},{4,6},{6,0},{1,3},{3,5},{5,7},{7,1},{8,10},{10,12},{12... | collective-permute-start | bytes 172040 | tf_op jit(solution)/shard_map/ppermute | solution.py:42
  13.2 3.3 %collective-permute-start.3 = (f32[16,256]{1,0:T(8,128)S(1)}, f32[16,256]{1,0:T(8,128)S(1)}, u32[]{:S(2)}, u32[]{:S(2)}) collective-permute-start(f32[16,256]{1,0:T(8,128)S(1)} %get-tuple-element.38), channel_id=1, source_target_pairs={{0,4},{2,6},{4,0},{6,2},{1,5},{3,7},{5,1},{7,3},{8,12},{10,14},{12... | collective-permute-start | bytes 49160 | tf_op jit(solution)/shard_map/ppermute | solution.py:42
  17.2 12.2 %collective-permute-start.7 = (f32[3,64,256]{2,1,0:T(8,128)S(1)}, f32[3,64,256]{2,1,0:T(8,128)S(1)}, u32[]{:S(2)}, u32[]{:S(2)}) collective-permute-start(f32[3,64,256]{2,1,0:T(8,128)S(1)} %add_after.1.refs_7_.refs_26_), channel_id=1, source_target_pairs={{0,16},{8,24},{16,0},{24,8},{1,17},{9,25},{17,1},{25,9},{2,18},{10... | collective-permute-start | bytes 589832 | tf_op jit(solution)/shard_map/ppermute | solution.py:102
  17.6 3.8 %collective-permute-start.4 = (f32[192,128]{1,0:T(8,128)S(1)}, f32[192,128]{1,0:T(8,128)S(1)}, u32[]{:S(2)}, u32[]{:S(2)}) collective-permute-start(f32[192,128]{1,0:T(8,128)S(1)} %get-tuple-element.39.refs_8_._), channel_id=1, source_target_pairs={{0,1},{1,0},{2,3},{3,2},{4,5},{5,4},{6,7},{7,6},{8,9},{9,8},{10,11... | collective-permute-start | bytes 294920 | tf_op jit(solution)/shard_map/ppermute | solution.py:42
  21.3 8.0 %copy-start.4 = (f32[64,256]{1,0:T(8,128)S(1)}, f32[64,256]{1,0:T(8,128)}, u32[]{:S(2)}) copy-start(f32[64,256]{1,0:T(8,128)} %refs_8_.1) | copy-start | bytes 196612
  23.0 6.4 %collective-permute-start.5 = (f32[72,256]{1,0:T(8,128)S(1)}, f32[72,256]{1,0:T(8,128)S(1)}, u32[]{:S(2)}, u32[]{:S(2)}) collective-permute-start(f32[72,256]{1,0:T(8,128)S(1)} %bitcast.27), channel_id=1, source_target_pairs={{0,24},{8,0},{16,8},{24,16},{1,25},{9,1},{17,9},{25,17},{2,26},{10... | collective-permute-start | bytes 221192 | tf_op jit(solution)/shard_map/ppermute | solution.py:42
  26.1 9.8 %collective-permute-start.12 = (f32[72,256]{1,0:T(8,128)S(1)}, f32[72,256]{1,0:T(8,128)S(1)}, u32[]{:S(2)}, u32[]{:S(2)}) collective-permute-start(f32[72,256]{1,0:T(8,128)S(1)} %bitcast.28), channel_id=1, source_target_pairs={{0,16},{1,17},{2,18},{3,19},{4,20},{5,21},{6,22},{7,23}} | collective-permute-start | bytes 221192 | tf_op jit(solution)/shard_map/ppermute | solution.py:773
  27.4 8.5 %collective-permute-start.11 = (f32[72,256]{1,0:T(8,128)S(1)}, f32[72,256]{1,0:T(8,128)S(1)}, u32[]{:S(2)}, u32[]{:S(2)}) collective-permute-start(f32[72,256]{1,0:T(8,128)S(1)} %bitcast.29), channel_id=1, source_target_pairs={{0,8},{1,9},{2,10},{3,11},{4,12},{5,13},{6,14},{7,15}} | collective-permute-start | bytes 221192 | tf_op jit(solution)/shard_map/ppermute | solution.py:773
  32.3 3.6 %collective-permute-start.10 = (f32[64,128]{1,0:T(8,128)S(1)}, f32[64,128]{1,0:T(8,128)S(1)}, u32[]{:S(2)}, u32[]{:S(2)}) collective-permute-start(f32[64,128]{1,0:T(8,128)S(1)} %get-tuple-element.53), channel_id=1, source_target_pairs={{0,1},{1,0},{2,3},{3,2},{4,5},{5,4},{6,7},{7,6},{8,9},{9,8},{10,11... | collective-permute-start | bytes 98312 | tf_op jit(solution)/shard_map/ppermute | solution.py:42
  33.6 3.3 %collective-permute-start.8 = (f32[32,256]{1,0:T(8,128)S(1)}, f32[32,256]{1,0:T(8,128)S(1)}, u32[]{:S(2)}, u32[]{:S(2)}) collective-permute-start(f32[32,256]{1,0:T(8,128)S(1)} %get-tuple-element.49.refs_14_), channel_id=1, source_target_pairs={{0,2},{2,4},{4,6},{6,0},{1,3},{3,5},{5,7},{7,1},{8,10},{10,12},{12... | collective-permute-start | bytes 98312 | tf_op jit(solution)/shard_map/ppermute | solution.py:42
  35.9 3.3 %collective-permute-start.9 = (f32[32,256]{1,0:T(8,128)S(1)}, f32[32,256]{1,0:T(8,128)S(1)}, u32[]{:S(2)}, u32[]{:S(2)}) collective-permute-start(f32[32,256]{1,0:T(8,128)S(1)} %get-tuple-element.50.refs_15_), channel_id=1, source_target_pairs={{0,6},{2,0},{4,2},{6,4},{1,7},{3,1},{5,3},{7,5},{8,14},{10,8},{12,... | collective-permute-start | bytes 98312 | tf_op jit(solution)/shard_map/ppermute | solution.py:42

commit v4 on v3

--- a/solution.py
+++ b/solution.py
@@ -15,6 +15,7 @@
 GROUP = 8
 PAIR = 2
 PARTS = 2
+BATCH = 8
 SPAWN_MB = 24
 
 f32 = jnp.float32
@@ -270,8 +271,8 @@
     last_out[...] = last
 
     def body(h, carry):
-        for k in range(PAIR):
-            a = h * PAIR + k
+        for k in range(BATCH):
+            a = h * BATCH + k
             mat = par_ref[MAT, a]
             for i in range(n_i):
                 for j in range(n_j):
@@ -287,7 +288,7 @@
                         bottom[j, pl.ds(a, 1), :] = value[SUB - 1 : SUB]
         return carry
 
-    lax.fori_loop(0, ages // PAIR, body, 0)
+    lax.fori_loop(0, ages // BATCH, body, 0)
     place = lax.broadcasted_iota(jnp.int32, (ages, cols), 0)
     for src, dst, row in ((top, back_out, 0), (bottom, ahead_out, rows - 1)):
         full = jnp.concatenate([src[j] for j in range(n_j)], axis=1)

time: 45.8 us -> 45 us (0.983)
  Pallas kernels: 18.6 us -> 17.8 us
    pallas_call x1, Pallas kernels: 2.96 us -> 2.15 us  [recruit_edges(): pl.pallas_call(functools.partial(recruit_kernel, c, len(terms)), in_specs...]
  transfers between devices with their start and end apart: 13 -> 13, of which waited for: 4 -> 4; matrix products, arithmetic and copies ran while one was open for 1% -> 1% of each run, Pallas kernels for 27% -> 26%
where the time goes in v4:
time: 45 us; the launch traced here: 44.7 us
  starting transfers between devices  18.2 us (40%)
  Pallas kernels  17.8 us (40%)
  waiting for transfers between devices  4.08 us (9%)
  local copies, waits for them, and re-layouts  2.52 us (6%)
  other arithmetic  1.11 us (2%)
  between operations  1.01 us (2%)
    ppermute x9, starting transfers between devices, shift(): return lax.ppermute(x, axis, [(i, (i + distance) % n) for i in range(n)])  15.1 us
    pallas_call x1, Pallas kernels, month_last(): pl.pallas_call(functools.partial(last_kernel, c), grid=(ages // GROUP,),...  6.33 us
    pallas_call x2, Pallas kernels, month_inner(): pl.pallas_call(functools.partial(month_kernel, c), in_specs=specs, out_sp...  4.89 us
    ppermute x9, waiting for transfers between devices, shift(): return lax.ppermute(x, axis, [(i, (i + distance) % n) for i in range(n)])  4.07 us
    ppermute x2, starting transfers between devices, shards(): lax.ppermute(plane, 'coh', [(0, j)])  2.58 us
    unnamed x38, local copies, waits for them, and re-layouts  2.34 us
    pallas_call x1, Pallas kernels, recruit_edges(): pl.pallas_call(functools.partial(recruit_kernel, c, len(terms)), in_specs...  2.15 us
    pallas_call x1, Pallas kernels, first_cohort(): pl.pallas_call(kernel, in_specs=[whole(SMEM)] + [whole()] * (len(operands...  1.53 us
  transfers between devices with their start and end apart: 13, of which 4 were waited for; matrix products, arithmetic and copies ran while one was open for 1% of the time, Pallas kernels for 26%

profile of v4, /device:TPU:1, one launch (start us, length us, event | category | flops | bytes accessed | tf_op | source)
XLA Modules:
  0.0 44.7 jit_solution(880616984425104661)
XLA Ops:
  0.6 0.9 %bitcast_convert_fusion.first_ref._ = f32[64,256]{1,0:T(8,128)S(1)} fusion(bf16[32,64,256]{2,1,0:T(8,128)(2,1)} %refs_1_.5), kind=kLoop, calls=%fused_computation | loop fusion | flops 16384 | bytes 98304 | tf_op jit(solution)/shard_map/convert_element_type | solution.py:747
  1.5 4.2 %collective-permute-start = (f32[64,256]{1,0:T(8,128)S(1)}, f32[64,256]{1,0:T(8,128)S(1)}, u32[]{:S(2)}, u32[]{:S(2)}) collective-permute-start(f32[64,256]{1,0:T(8,128)S(1)} %bitcast_convert_fusion.first_ref._), channel_id=1, source_target_pairs={{0,24},{8,0},{16,8},{24,16},{1,25},{9,1},{17,9},{25,17},{2,26},{10... | collective-permute-start | bytes 196616 | tf_op jit(solution)/shard_map/ppermute | solution.py:43
  5.6 0.1 pad_add_fusion.refs_0_.pos_ref
  5.7 1.6 %copy-done.1 = bf16[2,32,64,256]{3,2,1,0:T(8,128)(2,1)S(1)} copy-done((bf16[2,32,64,256]{3,2,1,0:T(8,128)(2,1)S(1)}, bf16[2,32,64,256]{3,2,1,0:T(8,128)(2,1)}, u32[]{:S(2)}) %copy-start.1) | copy-done | bytes 2097176
  7.3 0.7 %copy-done.7 = f32[32]{0:T(128)S(1)} copy-done((f32[32]{0:T(128)S(1)}, f32[32]{0:T(128)}, u32[]{:S(2)}) %copy-start.7) | copy-done | bytes 152
  8.1 1.3 %spawn_parts.1.a_ref = f32[3,64,256]{2,1,0:T(8,128)S(1)} custom-call(s32[3]{0:T(128)S(1)} %pad_add_fusion.refs_0_.pos_ref, f32[32]{0:T(128)S(1)} %copy-done.7, bf16[2,32,64,256]{3,2,1,0:T(8,128)(2,1)S(1)} %copy-done.1, f32[64,256]{1,0:T(8,128)S(1)} %bitcast_convert_fusion.first_ref._, f32[64,256]{1,0:T(8,128)S(1)} %bitcast_convert_fusion.first_ref._), custom_call_target="tpu_custom_call" | custom-call | tf_op jit(solution)/shard_map/spawn_parts/pallas_call | solution.py:70
  9.4 0.1 collective-permute-start.6
  9.5 0.1 and_convert_fusion
  9.7 0.1 copy.22
  9.8 0.1 reshape.85
  9.8 0.1 select_maximum_fusion.refs_6_
  10.0 1.0 %pack_edges.1 = (f32[56,256]{1,0:T(8,128)S(1)}, f32[56,256]{1,0:T(8,128)S(1)}, f32[64,128]{1,0:T(8,128)S(1)}, f32[64,128]{1,0:T(8,128)S(1)}, f32[16,256]{1,0:T(8...) custom-call(s32[3]{0:T(128)S(1)} %pad_add_fusion.refs_0_.pos_ref, ...), custom_call_target="tpu_custom_call" | custom-call | tf_op jit(solution)/shard_map/pack_edges/pallas_call | solution.py:236
  11.0 1.0 %collective-permute-start.2 = (f32[56,256]{1,0:T(8,128)S(1)}, f32[56,256]{1,0:T(8,128)S(1)}, u32[]{:S(2)}, u32[]{:S(2)}) collective-permute-start(f32[56,256]{1,0:T(8,128)S(1)} %get-tuple-element.37.refs_4_), channel_id=1, source_target_pairs={{0,6},{2,0},{4,2},{6,4},{1,7},{3,1},{5,3},{7,5},{8,14},{10,8},{12,... | collective-permute-start | bytes 172040 | tf_op jit(solution)/shard_map/ppermute | solution.py:43
  12.1 1.2 %collective-permute-start.1 = (f32[56,256]{1,0:T(8,128)S(1)}, f32[56,256]{1,0:T(8,128)S(1)}, u32[]{:S(2)}, u32[]{:S(2)}) collective-permute-start(f32[56,256]{1,0:T(8,128)S(1)} %get-tuple-element.36.refs_8_.refs_0_.refs_3_), channel_id=1, source_target_pairs={{0,2},{2,4},{4,6},{6,0},{1,3},{3,5},{5,7},{7,1},{8,10},{10,12},{12... | collective-permute-start | bytes 172040 | tf_op jit(solution)/shard_map/ppermute | solution.py:43
  13.2 0.8 %collective-permute-start.3 = (f32[16,256]{1,0:T(8,128)S(1)}, f32[16,256]{1,0:T(8,128)S(1)}, u32[]{:S(2)}, u32[]{:S(2)}) collective-permute-start(f32[16,256]{1,0:T(8,128)S(1)} %get-tuple-element.38), channel_id=1, source_target_pairs={{0,4},{2,6},{4,0},{6,2},{1,5},{3,7},{5,1},{7,3},{8,12},{10,14},{12... | collective-permute-start | bytes 49160 | tf_op jit(solution)/shard_map/ppermute | solution.py:43
  14.1 2.4 %month_inner.2._.refs_9_ = f32[32,64,256]{2,1,0:T(8,128)S(1)} custom-call(f32[8,128]{1,0:T(8,128)S(1)} %get-tuple-element.28.refs_0_.refs_1_.refs_2_, bf16[32,64,256]{2,1,0:T(8,128)(2,1)S(1)} %copy-done, f32[64,256]{1,0:T(8,128)S(1)} %get-tuple-element.29.refs_2_, f32[64,256]{1,0:T(8,128)S(1)} %copy-done.2, f32[64,256]{1,0:T(8,128)S(1)} %get-tuple-element.30.refs_4_.refs_9_, ...), custom_call_target="tpu_custom_call" | custom-call | flops 15728640 | bytes 2097152 | tf_op jit(solution)/shard_map/month_inner/pallas_call | solution.py:676
  16.5 0.6 %relay.1 = (f32[192,128]{1,0:T(8,128)S(1)}, f32[128,128]{1,0:T(8,128)S(1)}) custom-call(s32[3]{0:T(128)S(1)} %pad_add_fusion.refs_0_.pos_ref, f32[64,128]{1,0:T(8,128)S(1)} %get-tuple-element.34.east_ref.refs_5_, f32[64,128]{1,0:T(8,128)S(1)} %get-tuple-element.35.west_ref.refs_6_, f32[32,64,256]{2,1,0:T(8,128)S(1)} %month_inner.2._.refs_9_, ...), custom_call_target="tpu_custom_call" | custom-call | tf_op jit(solution)/shard_map/relay/pallas_call | solution.py:219
  17.2 0.5 %collective-permute-start.7 = (f32[3,64,256]{2,1,0:T(8,128)S(1)}, f32[3,64,256]{2,1,0:T(8,128)S(1)}, u32[]{:S(2)}, u32[]{:S(2)}) collective-permute-start(f32[3,64,256]{2,1,0:T(8,128)S(1)} %add_after.1.refs_7_.refs_26_), channel_id=1, source_target_pairs={{0,16},{8,24},{16,0},{24,8},{1,17},{9,25},{17,1},{25,9},{2,18},{10... | collective-permute-start | bytes 589832 | tf_op jit(solution)/shard_map/ppermute | solution.py:103
  17.6 1.2 %collective-permute-start.4 = (f32[192,128]{1,0:T(8,128)S(1)}, f32[192,128]{1,0:T(8,128)S(1)}, u32[]{:S(2)}, u32[]{:S(2)}) collective-permute-start(f32[192,128]{1,0:T(8,128)S(1)} %get-tuple-element.39.refs_8_._), channel_id=1, source_target_pairs={{0,1},{1,0},{2,3},{3,2},{4,5},{5,4},{6,7},{7,6},{8,9},{9,8},{10,11... | collective-permute-start | bytes 294920 | tf_op jit(solution)/shard_map/ppermute | solution.py:43
  18.9 2.4 %month_inner.3.refs_2_.refs_13_ = f32[32,64,256]{2,1,0:T(8,128)S(1)} custom-call(f32[8,128]{1,0:T(8,128)S(1)} %get-tuple-element.28.refs_0_.refs_1_.refs_2_, bf16[32,64,256]{2,1,0:T(8,128)(2,1)S(1)} %copy-done, f32[64,256]{1,0:T(8,128)S(1)} %get-tuple-element.29.refs_2_, f32[64,256]{1,0:T(8,128)S(1)} %copy-done.2, ...), custom_call_target="tpu_custom_call", output_to_operand_aliasing={{}: (9, {})} | custom-call | flops 15728640 | bytes 2097152 | tf_op jit(solution)/shard_map/month_inner/pallas_call | solution.py:676
  21.3 0.1 collective-permute-done.4.refs_9_.refs_10_.refs_14_.refs_24_.refs_25_
  21.4 1.5 %first_cohort.1 = (f32[1,72,256]{2,1,0:T(8,128)S(1)}, f32[2,2,32,128]{3,2,1,0:T(8,128)S(1)}, f32[64,128]{1,0:T(8,128)S(1)}, f32[64,128]{1,0:T(8,128)S(1)}, f32[2,4,2,32,128]{4,3,2,1,0:T(8,128)S(1)}) custom-call(s32[3]{0:T(128)S(1)} %pad_add_fusion.refs_0_.pos_ref, f32[8,128]{1,0:T(8,128)S(1)} %get-tuple-element.28.refs_0_.refs_1_.refs_2_, ...), custom_call_target="tpu_custom_call" | custom-call | flops 3932160 | bytes 524288 | tf_op jit(solution)/shard_map/first_cohort/pallas_call | solution.py:654
  23.0 3.1 %collective-permute-start.5 = (f32[72,256]{1,0:T(8,128)S(1)}, f32[72,256]{1,0:T(8,128)S(1)}, u32[]{:S(2)}, u32[]{:S(2)}) collective-permute-start(f32[72,256]{1,0:T(8,128)S(1)} %bitcast.27), channel_id=1, source_target_pairs={{0,24},{8,0},{16,8},{24,16},{1,25},{9,1},{17,9},{25,17},{2,26},{10... | collective-permute-start | bytes 221192 | tf_op jit(solution)/shard_map/ppermute | solution.py:43
  26.1 1.3 %collective-permute-start.12 = (f32[72,256]{1,0:T(8,128)S(1)}, f32[72,256]{1,0:T(8,128)S(1)}, u32[]{:S(2)}, u32[]{:S(2)}) collective-permute-start(f32[72,256]{1,0:T(8,128)S(1)} %bitcast.28), channel_id=1, source_target_pairs={{0,16},{1,17},{2,18},{3,19},{4,20},{5,21},{6,22},{7,23}} | collective-permute-start | bytes 221192 | tf_op jit(solution)/shard_map/ppermute | solution.py:774
  27.4 1.3 %collective-permute-start.11 = (f32[72,256]{1,0:T(8,128)S(1)}, f32[72,256]{1,0:T(8,128)S(1)}, u32[]{:S(2)}, u32[]{:S(2)}) collective-permute-start(f32[72,256]{1,0:T(8,128)S(1)} %bitcast.29), channel_id=1, source_target_pairs={{0,8},{1,9},{2,10},{3,11},{4,12},{5,13},{6,14},{7,15}} | collective-permute-start | bytes 221192 | tf_op jit(solution)/shard_map/ppermute | solution.py:774
  28.7 0.7 %collective-permute-done.5.refs_6_.refs_29_ = f32[72,256]{1,0:T(8,128)S(1)} collective-permute-done((f32[72,256]{1,0:T(8,128)S(1)}, f32[72,256]{1,0:T(8,128)S(1)}, u32[]{:S(2)}, u32[]{:S(2)}) %collective-permute-start.5) | collective-permute-done | bytes 73760 | tf_op jit(solution)/shard_map/ppermute | solution.py:43
  29.4 2.1 %recruit_edges.1 = (f32[32,64,256]{2,1,0:T(8,128)S(1)}, f32[32,256]{1,0:T(8,128)S(1)}, f32[32,256]{1,0:T(8,128)S(1)}, f32[64,128]{1,0:T(8,128)S(1)}, f32[64,128]...) custom-call(s32[3]{0:T(128)S(1)} %pad_add_fusion.refs_0_.pos_ref, ...), custom_call_target="tpu_custom_call", output_to_operand_aliasing={{0}: (13, {})} | custom-call | flops 8388608 | bytes 4194304 | tf_op jit(solution)/shard_map/recruit_edges/pallas_call | solution.py:315
  31.5 1.3 %collective-permute-start.10 = (f32[64,128]{1,0:T(8,128)S(1)}, f32[64,128]{1,0:T(8,128)S(1)}, u32[]{:S(2)}, u32[]{:S(2)}) collective-permute-start(f32[64,128]{1,0:T(8,128)S(1)} %get-tuple-element.53), channel_id=1, source_target_pairs={{0,1},{1,0},{2,3},{3,2},{4,5},{5,4},{6,7},{7,6},{8,9},{9,8},{10,11... | collective-permute-start | bytes 98312 | tf_op jit(solution)/shard_map/ppermute | solution.py:43
  32.8 2.2 %collective-permute-start.8 = (f32[32,256]{1,0:T(8,128)S(1)}, f32[32,256]{1,0:T(8,128)S(1)}, u32[]{:S(2)}, u32[]{:S(2)}) collective-permute-start(f32[32,256]{1,0:T(8,128)S(1)} %get-tuple-element.49.refs_14_), channel_id=1, source_target_pairs={{0,2},{2,4},{4,6},{6,0},{1,3},{3,5},{5,7},{7,1},{8,10},{10,12},{12... | collective-permute-start | bytes 98312 | tf_op jit(solution)/shard_map/ppermute | solution.py:43
  35.1 1.0 %collective-permute-done.8.refs_18_ = f32[32,256]{1,0:T(8,128)S(1)} collective-permute-done((f32[32,256]{1,0:T(8,128)S(1)}, f32[32,256]{1,0:T(8,128)S(1)}, u32[]{:S(2)}, u32[]{:S(2)}) %collective-permute-start.8) | collective-permute-done | bytes 32800 | tf_op jit(solution)/shard_map/ppermute | solution.py:43
  36.1 2.3 %collective-permute-done.9.refs_19_ = f32[32,256]{1,0:T(8,128)S(1)} collective-permute-done((f32[32,256]{1,0:T(8,128)S(1)}, f32[32,256]{1,0:T(8,128)S(1)}, u32[]{:S(2)}, u32[]{:S(2)}) %collective-permute-start.9) | collective-permute-done | bytes 32800 | tf_op jit(solution)/shard_map/ppermute | solution.py:43
  38.4 6.3 %month_last.1 = (f32[32,64,256]{2,1,0:T(8,128)}, f32[64,256]{1,0:T(8,128)}) custom-call(s32[3]{0:T(128)S(1)} %pad_add_fusion.refs_0_.pos_ref, f32[8,128]{1,0:T(8,128)S(1)} %get-tuple-element.28.refs_0_.refs_1_.refs_2_, f32[8,128]{1,0:T(8,128)S(1)} %get-tuple-element.28.refs_0_.refs_1_.refs_2_, f32[32,64,256]{2,1,0:T(8,128)S(1)} %get-tuple-element.46.refs_3_, ...), custom_call_target="tpu_custom_call" | custom-call | flops 31457280 | bytes 4194304 | tf_op jit(solution)/shard_map/month_last/pallas_call | solution.py:697
  (51 shorter events, 0.2 us)
Async XLA Ops:
  0.6 9.3 %copy-start = (bf16[32,64,256]{2,1,0:T(8,128)(2,1)S(1)}, bf16[32,64,256]{2,1,0:T(8,128)(2,1)}, u32[]{:S(2)}) copy-start(bf16[32,64,256]{2,1,0:T(8,128)(2,1)} %refs_1_.5) | copy-start | bytes 3145732
  1.5 8.4 %collective-permute-start = (f32[64,256]{1,0:T(8,128)S(1)}, f32[64,256]{1,0:T(8,128)S(1)}, u32[]{:S(2)}, u32[]{:S(2)}) collective-permute-start(f32[64,256]{1,0:T(8,128)S(1)} %bitcast_convert_fusion.first_ref._), channel_id=1, source_target_pairs={{0,24},{8,0},{16,8},{24,16},{1,25},{9,1},{17,9},{25,17},{2,26},{10... | collective-permute-start | bytes 196616 | tf_op jit(solution)/shard_map/ppermute | solution.py:43
  5.7 1.6 %copy-start.1 = (bf16[2,32,64,256]{3,2,1,0:T(8,128)(2,1)S(1)}, bf16[2,32,64,256]{3,2,1,0:T(8,128)(2,1)}, u32[]{:S(2)}) copy-start(bf16[2,32,64,256]{3,2,1,0:T(8,128)(2,1)} %saved_ref.1) | copy-start | bytes 6291460
  7.3 0.7 %copy-start.7 = (f32[32]{0:T(128)S(1)}, f32[32]{0:T(128)}, u32[]{:S(2)}) copy-start(f32[32]{0:T(128)} %breed_ref.1) | copy-start | bytes 388
  8.0 1.5 %copy-start.15 = (s32[32,2]{0,1:T(2,128)S(1)}, s32[32,2]{0,1:T(2,128)}, u32[]{:S(2)}) copy-start(s32[32,2]{0,1:T(2,128)} %param.35) | copy-start | bytes 772
  8.0 1.6 %copy-start.14 = (f32[32,2,32]{2,1,0:T(2,128)S(1)}, f32[32,2,32]{2,1,0:T(2,128)}, u32[]{:S(2)}) copy-start(f32[32,2,32]{2,1,0:T(2,128)} %param.31) | copy-start | bytes 24580
  8.0 1.7 %copy-start.16 = (s32[32]{0:T(128)S(1)}, s32[32]{0:T(128)}, u32[]{:S(2)}) copy-start(s32[32]{0:T(128)} %param.34) | copy-start | bytes 388
  8.0 1.7 %copy-start.17 = (s32[32,1]{0,1:T(1,128)S(1)}, s32[32,1]{0,1:T(1,128)}, u32[]{:S(2)}) copy-start(s32[32,1]{0,1:T(1,128)} %param.32) | copy-start | bytes 388
  8.0 1.7 %copy-start.18 = (s32[32]{0:T(128)S(1)}, s32[32]{0:T(128)}, u32[]{:S(2)}) copy-start(s32[32]{0:T(128)} %param.33) | copy-start | bytes 388
  8.0 1.9 %copy-start.3 = (s32[64,256]{1,0:T(8,128)S(1)}, s32[64,256]{1,0:T(8,128)}, u32[]{:S(2)}) copy-start(s32[64,256]{1,0:T(8,128)} %refs_6_.1) | copy-start | bytes 196612
  8.0 1.9 %copy-start.5 = (f32[2,64,256]{2,1,0:T(8,128)S(1)}, f32[2,64,256]{2,1,0:T(8,128)}, u32[]{:S(2)}) copy-start(f32[2,64,256]{2,1,0:T(8,128)} %refs_4_.2) | copy-start | bytes 393220
  8.0 1.9 %copy-start.6 = (f32[2,64,256]{2,1,0:T(8,128)S(1)}, f32[2,64,256]{2,1,0:T(8,128)}, u32[]{:S(2)}) copy-start(f32[2,64,256]{2,1,0:T(8,128)} %refs_5_.2) | copy-start | bytes 393220
  8.0 1.9 %copy-start.8 = (f32[32]{0:T(128)S(1)}, f32[32]{0:T(128)}, u32[]{:S(2)}) copy-start(f32[32]{0:T(128)} %breed_ref.1) | copy-start | bytes 388
  8.0 1.9 %copy-start.9 = (f32[32]{0:T(128)S(1)}, f32[32]{0:T(128)}, u32[]{:S(2)}) copy-start(f32[32]{0:T(128)} %param.25) | copy-start | bytes 388
  8.0 1.9 %copy-start.10 = (f32[32]{0:T(128)S(1)}, f32[32]{0:T(128)}, u32[]{:S(2)}) copy-start(f32[32]{0:T(128)} %param.26) | copy-start | bytes 388
  8.1 1.9 %copy-start.11 = (f32[32]{0:T(128)S(1)}, f32[32]{0:T(128)}, u32[]{:S(2)}) copy-start(f32[32]{0:T(128)} %param.27) | copy-start | bytes 388
  8.1 1.9 %copy-start.12 = (f32[32]{0:T(128)S(1)}, f32[32]{0:T(128)}, u32[]{:S(2)}) copy-start(f32[32]{0:T(128)} %param.28) | copy-start | bytes 388
  8.1 1.9 %copy-start.13 = (f32[32]{0:T(128)S(1)}, f32[32]{0:T(128)}, u32[]{:S(2)}) copy-start(f32[32]{0:T(128)} %param.29) | copy-start | bytes 388
  8.1 6.0 %copy-start.2 = (f32[64,256]{1,0:T(8,128)S(1)}, f32[64,256]{1,0:T(8,128)}, u32[]{:S(2)}) copy-start(f32[64,256]{1,0:T(8,128)} %refs_7_.1) | copy-start | bytes 196612
  9.4 7.7 %collective-permute-start.6 = (f32[3,64,256]{2,1,0:T(8,128)S(1)}, f32[3,64,256]{2,1,0:T(8,128)S(1)}, u32[]{:S(2)}, u32[]{:S(2)}) collective-permute-start(f32[3,64,256]{2,1,0:T(8,128)S(1)} %spawn_parts.1.a_ref), channel_id=1, source_target_pairs={{0,8},{8,0},{16,24},{24,16},{1,9},{9,1},{17,25},{25,17},{2,10},{10... | collective-permute-start | bytes 589832 | tf_op jit(solution)/shard_map/ppermute | solution.py:103
  11.0 5.5 %collective-permute-start.2 = (f32[56,256]{1,0:T(8,128)S(1)}, f32[56,256]{1,0:T(8,128)S(1)}, u32[]{:S(2)}, u32[]{:S(2)}) collective-permute-start(f32[56,256]{1,0:T(8,128)S(1)} %get-tuple-element.37.refs_4_), channel_id=1, source_target_pairs={{0,6},{2,0},{4,2},{6,4},{1,7},{3,1},{5,3},{7,5},{8,14},{10,8},{12,... | collective-permute-start | bytes 172040 | tf_op jit(solution)/shard_map/ppermute | solution.py:43
  12.1 4.5 %collective-permute-start.1 = (f32[56,256]{1,0:T(8,128)S(1)}, f32[56,256]{1,0:T(8,128)S(1)}, u32[]{:S(2)}, u32[]{:S(2)}) collective-permute-start(f32[56,256]{1,0:T(8,128)S(1)} %get-tuple-element.36.refs_8_.refs_0_.refs_3_), channel_id=1, source_target_pairs={{0,2},{2,4},{4,6},{6,0},{1,3},{3,5},{5,7},{7,1},{8,10},{10,12},{12... | collective-permute-start | bytes 172040 | tf_op jit(solution)/shard_map/ppermute | solution.py:43
  13.2 3.3 %collective-permute-start.3 = (f32[16,256]{1,0:T(8,128)S(1)}, f32[16,256]{1,0:T(8,128)S(1)}, u32[]{:S(2)}, u32[]{:S(2)}) collective-permute-start(f32[16,256]{1,0:T(8,128)S(1)} %get-tuple-element.38), channel_id=1, source_target_pairs={{0,4},{2,6},{4,0},{6,2},{1,5},{3,7},{5,1},{7,3},{8,12},{10,14},{12... | collective-permute-start | bytes 49160 | tf_op jit(solution)/shard_map/ppermute | solution.py:43
  17.2 12.2 %collective-permute-start.7 = (f32[3,64,256]{2,1,0:T(8,128)S(1)}, f32[3,64,256]{2,1,0:T(8,128)S(1)}, u32[]{:S(2)}, u32[]{:S(2)}) collective-permute-start(f32[3,64,256]{2,1,0:T(8,128)S(1)} %add_after.1.refs_7_.refs_26_), channel_id=1, source_target_pairs={{0,16},{8,24},{16,0},{24,8},{1,17},{9,25},{17,1},{25,9},{2,18},{10... | collective-permute-start | bytes 589832 | tf_op jit(solution)/shard_map/ppermute | solution.py:103
  17.6 3.8 %collective-permute-start.4 = (f32[192,128]{1,0:T(8,128)S(1)}, f32[192,128]{1,0:T(8,128)S(1)}, u32[]{:S(2)}, u32[]{:S(2)}) collective-permute-start(f32[192,128]{1,0:T(8,128)S(1)} %get-tuple-element.39.refs_8_._), channel_id=1, source_target_pairs={{0,1},{1,0},{2,3},{3,2},{4,5},{5,4},{6,7},{7,6},{8,9},{9,8},{10,11... | collective-permute-start | bytes 294920 | tf_op jit(solution)/shard_map/ppermute | solution.py:43
  21.3 8.0 %copy-start.4 = (f32[64,256]{1,0:T(8,128)S(1)}, f32[64,256]{1,0:T(8,128)}, u32[]{:S(2)}) copy-start(f32[64,256]{1,0:T(8,128)} %refs_8_.1) | copy-start | bytes 196612
  23.0 6.4 %collective-permute-start.5 = (f32[72,256]{1,0:T(8,128)S(1)}, f32[72,256]{1,0:T(8,128)S(1)}, u32[]{:S(2)}, u32[]{:S(2)}) collective-permute-start(f32[72,256]{1,0:T(8,128)S(1)} %bitcast.27), channel_id=1, source_target_pairs={{0,24},{8,0},{16,8},{24,16},{1,25},{9,1},{17,9},{25,17},{2,26},{10... | collective-permute-start | bytes 221192 | tf_op jit(solution)/shard_map/ppermute | solution.py:43
  26.1 9.0 %collective-permute-start.12 = (f32[72,256]{1,0:T(8,128)S(1)}, f32[72,256]{1,0:T(8,128)S(1)}, u32[]{:S(2)}, u32[]{:S(2)}) collective-permute-start(f32[72,256]{1,0:T(8,128)S(1)} %bitcast.28), channel_id=1, source_target_pairs={{0,16},{1,17},{2,18},{3,19},{4,20},{5,21},{6,22},{7,23}} | collective-permute-start | bytes 221192 | tf_op jit(solution)/shard_map/ppermute | solution.py:774
  27.4 7.7 %collective-permute-start.11 = (f32[72,256]{1,0:T(8,128)S(1)}, f32[72,256]{1,0:T(8,128)S(1)}, u32[]{:S(2)}, u32[]{:S(2)}) collective-permute-start(f32[72,256]{1,0:T(8,128)S(1)} %bitcast.29), channel_id=1, source_target_pairs={{0,8},{1,9},{2,10},{3,11},{4,12},{5,13},{6,14},{7,15}} | collective-permute-start | bytes 221192 | tf_op jit(solution)/shard_map/ppermute | solution.py:774
  31.5 3.6 %collective-permute-start.10 = (f32[64,128]{1,0:T(8,128)S(1)}, f32[64,128]{1,0:T(8,128)S(1)}, u32[]{:S(2)}, u32[]{:S(2)}) collective-permute-start(f32[64,128]{1,0:T(8,128)S(1)} %get-tuple-element.53), channel_id=1, source_target_pairs={{0,1},{1,0},{2,3},{3,2},{4,5},{5,4},{6,7},{7,6},{8,9},{9,8},{10,11... | collective-permute-start | bytes 98312 | tf_op jit(solution)/shard_map/ppermute | solution.py:43
  32.8 3.3 %collective-permute-start.8 = (f32[32,256]{1,0:T(8,128)S(1)}, f32[32,256]{1,0:T(8,128)S(1)}, u32[]{:S(2)}, u32[]{:S(2)}) collective-permute-start(f32[32,256]{1,0:T(8,128)S(1)} %get-tuple-element.49.refs_14_), channel_id=1, source_target_pairs={{0,2},{2,4},{4,6},{6,0},{1,3},{3,5},{5,7},{7,1},{8,10},{10,12},{12... | collective-permute-start | bytes 98312 | tf_op jit(solution)/shard_map/ppermute | solution.py:43
  35.1 3.3 %collective-permute-start.9 = (f32[32,256]{1,0:T(8,128)S(1)}, f32[32,256]{1,0:T(8,128)S(1)}, u32[]{:S(2)}, u32[]{:S(2)}) collective-permute-start(f32[32,256]{1,0:T(8,128)S(1)} %get-tuple-element.50.refs_15_), channel_id=1, source_target_pairs={{0,6},{2,0},{4,2},{6,4},{1,7},{3,1},{5,3},{7,5},{8,14},{10,8},{12,... | collective-permute-start | bytes 98312 | tf_op jit(solution)/shard_map/ppermute | solution.py:43

commit v5 on v4

--- a/solution.py
+++ b/solution.py
@@ -15,7 +15,7 @@
 GROUP = 8
 PAIR = 2
 PARTS = 2
-BATCH = 8
+BATCH = 16
 SPAWN_MB = 24
 
 f32 = jnp.float32

time: 45 us -> 44.8 us (level)
  transfers between devices with their start and end apart: 13 -> 13, of which waited for: 4 -> 4; matrix products, arithmetic and copies ran while one was open for 1% -> 1% of each run, Pallas kernels for 26% -> 25%
where the time goes in v5:
time: 44.8 us; the launch traced here: 44.6 us
  starting transfers between devices  18.2 us (41%)
  Pallas kernels  17.7 us (40%)
  waiting for transfers between devices  4.08 us (9%)
  local copies, waits for them, and re-layouts  2.52 us (6%)
  other arithmetic  1.11 us (2%)
  between operations  1.01 us (2%)
    ppermute x9, starting transfers between devices, shift(): return lax.ppermute(x, axis, [(i, (i + distance) % n) for i in range(n)])  15.1 us
    pallas_call x1, Pallas kernels, month_last(): pl.pallas_call(functools.partial(last_kernel, c), grid=(ages // GROUP,),...  6.33 us
    pallas_call x2, Pallas kernels, month_inner(): pl.pallas_call(functools.partial(month_kernel, c), in_specs=specs, out_sp...  4.89 us
    ppermute x9, waiting for transfers between devices, shift(): return lax.ppermute(x, axis, [(i, (i + distance) % n) for i in range(n)])  4.07 us
    ppermute x2, starting transfers between devices, shards(): lax.ppermute(plane, 'coh', [(0, j)])  2.58 us
    unnamed x38, local copies, waits for them, and re-layouts  2.34 us
    pallas_call x1, Pallas kernels, recruit_edges(): pl.pallas_call(functools.partial(recruit_kernel, c, len(terms)), in_specs...  2.01 us
    pallas_call x1, Pallas kernels, first_cohort(): pl.pallas_call(kernel, in_specs=[whole(SMEM)] + [whole()] * (len(operands...  1.53 us
  transfers between devices with their start and end apart: 13, of which 4 were waited for; matrix products, arithmetic and copies ran while one was open for 1% of the time, Pallas kernels for 25%

profile of v5, /device:TPU:1, one launch (start us, length us, event | category | flops | bytes accessed | tf_op | source)
XLA Modules:
  0.0 44.6 jit_solution(12960397922619082526)
XLA Ops:
  0.6 0.9 %bitcast_convert_fusion.first_ref._ = f32[64,256]{1,0:T(8,128)S(1)} fusion(bf16[32,64,256]{2,1,0:T(8,128)(2,1)} %refs_1_.5), kind=kLoop, calls=%fused_computation | loop fusion | flops 16384 | bytes 98304 | tf_op jit(solution)/shard_map/convert_element_type | solution.py:747
  1.5 4.2 %collective-permute-start = (f32[64,256]{1,0:T(8,128)S(1)}, f32[64,256]{1,0:T(8,128)S(1)}, u32[]{:S(2)}, u32[]{:S(2)}) collective-permute-start(f32[64,256]{1,0:T(8,128)S(1)} %bitcast_convert_fusion.first_ref._), channel_id=1, source_target_pairs={{0,24},{8,0},{16,8},{24,16},{1,25},{9,1},{17,9},{25,17},{2,26},{10... | collective-permute-start | bytes 196616 | tf_op jit(solution)/shard_map/ppermute | solution.py:43
  5.6 0.1 pad_add_fusion.refs_0_.pos_ref
  5.7 1.6 %copy-done.1 = bf16[2,32,64,256]{3,2,1,0:T(8,128)(2,1)S(1)} copy-done((bf16[2,32,64,256]{3,2,1,0:T(8,128)(2,1)S(1)}, bf16[2,32,64,256]{3,2,1,0:T(8,128)(2,1)}, u32[]{:S(2)}) %copy-start.1) | copy-done | bytes 2097176
  7.3 0.7 %copy-done.7 = f32[32]{0:T(128)S(1)} copy-done((f32[32]{0:T(128)S(1)}, f32[32]{0:T(128)}, u32[]{:S(2)}) %copy-start.7) | copy-done | bytes 152
  8.1 1.3 %spawn_parts.1.a_ref = f32[3,64,256]{2,1,0:T(8,128)S(1)} custom-call(s32[3]{0:T(128)S(1)} %pad_add_fusion.refs_0_.pos_ref, f32[32]{0:T(128)S(1)} %copy-done.7, bf16[2,32,64,256]{3,2,1,0:T(8,128)(2,1)S(1)} %copy-done.1, f32[64,256]{1,0:T(8,128)S(1)} %bitcast_convert_fusion.first_ref._, f32[64,256]{1,0:T(8,128)S(1)} %bitcast_convert_fusion.first_ref._), custom_call_target="tpu_custom_call" | custom-call | tf_op jit(solution)/shard_map/spawn_parts/pallas_call | solution.py:70
  9.4 0.1 collective-permute-start.6
  9.5 0.1 and_convert_fusion
  9.7 0.1 copy.22
  9.8 0.1 reshape.85
  9.8 0.1 select_maximum_fusion.refs_6_
  10.0 1.0 %pack_edges.1 = (f32[56,256]{1,0:T(8,128)S(1)}, f32[56,256]{1,0:T(8,128)S(1)}, f32[64,128]{1,0:T(8,128)S(1)}, f32[64,128]{1,0:T(8,128)S(1)}, f32[16,256]{1,0:T(8...) custom-call(s32[3]{0:T(128)S(1)} %pad_add_fusion.refs_0_.pos_ref, ...), custom_call_target="tpu_custom_call" | custom-call | tf_op jit(solution)/shard_map/pack_edges/pallas_call | solution.py:236
  11.0 1.0 %collective-permute-start.2 = (f32[56,256]{1,0:T(8,128)S(1)}, f32[56,256]{1,0:T(8,128)S(1)}, u32[]{:S(2)}, u32[]{:S(2)}) collective-permute-start(f32[56,256]{1,0:T(8,128)S(1)} %get-tuple-element.37.refs_4_), channel_id=1, source_target_pairs={{0,6},{2,0},{4,2},{6,4},{1,7},{3,1},{5,3},{7,5},{8,14},{10,8},{12,... | collective-permute-start | bytes 172040 | tf_op jit(solution)/shard_map/ppermute | solution.py:43
  12.1 1.2 %collective-permute-start.1 = (f32[56,256]{1,0:T(8,128)S(1)}, f32[56,256]{1,0:T(8,128)S(1)}, u32[]{:S(2)}, u32[]{:S(2)}) collective-permute-start(f32[56,256]{1,0:T(8,128)S(1)} %get-tuple-element.36.refs_8_.refs_0_.refs_3_), channel_id=1, source_target_pairs={{0,2},{2,4},{4,6},{6,0},{1,3},{3,5},{5,7},{7,1},{8,10},{10,12},{12... | collective-permute-start | bytes 172040 | tf_op jit(solution)/shard_map/ppermute | solution.py:43
  13.2 0.8 %collective-permute-start.3 = (f32[16,256]{1,0:T(8,128)S(1)}, f32[16,256]{1,0:T(8,128)S(1)}, u32[]{:S(2)}, u32[]{:S(2)}) collective-permute-start(f32[16,256]{1,0:T(8,128)S(1)} %get-tuple-element.38), channel_id=1, source_target_pairs={{0,4},{2,6},{4,0},{6,2},{1,5},{3,7},{5,1},{7,3},{8,12},{10,14},{12... | collective-permute-start | bytes 49160 | tf_op jit(solution)/shard_map/ppermute | solution.py:43
  14.1 2.4 %month_inner.2._.refs_9_ = f32[32,64,256]{2,1,0:T(8,128)S(1)} custom-call(f32[8,128]{1,0:T(8,128)S(1)} %get-tuple-element.28.refs_0_.refs_1_.refs_2_, bf16[32,64,256]{2,1,0:T(8,128)(2,1)S(1)} %copy-done, f32[64,256]{1,0:T(8,128)S(1)} %get-tuple-element.29.refs_2_, f32[64,256]{1,0:T(8,128)S(1)} %copy-done.2, f32[64,256]{1,0:T(8,128)S(1)} %get-tuple-element.30.refs_4_.refs_9_, ...), custom_call_target="tpu_custom_call" | custom-call | flops 15728640 | bytes 2097152 | tf_op jit(solution)/shard_map/month_inner/pallas_call | solution.py:676
  16.5 0.6 %relay.1 = (f32[192,128]{1,0:T(8,128)S(1)}, f32[128,128]{1,0:T(8,128)S(1)}) custom-call(s32[3]{0:T(128)S(1)} %pad_add_fusion.refs_0_.pos_ref, f32[64,128]{1,0:T(8,128)S(1)} %get-tuple-element.34.east_ref.refs_5_, f32[64,128]{1,0:T(8,128)S(1)} %get-tuple-element.35.west_ref.refs_6_, f32[32,64,256]{2,1,0:T(8,128)S(1)} %month_inner.2._.refs_9_, ...), custom_call_target="tpu_custom_call" | custom-call | tf_op jit(solution)/shard_map/relay/pallas_call | solution.py:219
  17.2 0.5 %collective-permute-start.7 = (f32[3,64,256]{2,1,0:T(8,128)S(1)}, f32[3,64,256]{2,1,0:T(8,128)S(1)}, u32[]{:S(2)}, u32[]{:S(2)}) collective-permute-start(f32[3,64,256]{2,1,0:T(8,128)S(1)} %add_after.1.refs_7_.refs_26_), channel_id=1, source_target_pairs={{0,16},{8,24},{16,0},{24,8},{1,17},{9,25},{17,1},{25,9},{2,18},{10... | collective-permute-start | bytes 589832 | tf_op jit(solution)/shard_map/ppermute | solution.py:103
  17.6 1.2 %collective-permute-start.4 = (f32[192,128]{1,0:T(8,128)S(1)}, f32[192,128]{1,0:T(8,128)S(1)}, u32[]{:S(2)}, u32[]{:S(2)}) collective-permute-start(f32[192,128]{1,0:T(8,128)S(1)} %get-tuple-element.39.refs_8_._), channel_id=1, source_target_pairs={{0,1},{1,0},{2,3},{3,2},{4,5},{5,4},{6,7},{7,6},{8,9},{9,8},{10,11... | collective-permute-start | bytes 294920 | tf_op jit(solution)/shard_map/ppermute | solution.py:43
  18.9 2.4 %month_inner.3.refs_2_.refs_13_ = f32[32,64,256]{2,1,0:T(8,128)S(1)} custom-call(f32[8,128]{1,0:T(8,128)S(1)} %get-tuple-element.28.refs_0_.refs_1_.refs_2_, bf16[32,64,256]{2,1,0:T(8,128)(2,1)S(1)} %copy-done, f32[64,256]{1,0:T(8,128)S(1)} %get-tuple-element.29.refs_2_, f32[64,256]{1,0:T(8,128)S(1)} %copy-done.2, ...), custom_call_target="tpu_custom_call", output_to_operand_aliasing={{}: (9, {})} | custom-call | flops 15728640 | bytes 2097152 | tf_op jit(solution)/shard_map/month_inner/pallas_call | solution.py:676
  21.3 0.1 collective-permute-done.4.refs_9_.refs_10_.refs_14_.refs_24_.refs_25_
  21.4 1.5 %first_cohort.1 = (f32[1,72,256]{2,1,0:T(8,128)S(1)}, f32[2,2,32,128]{3,2,1,0:T(8,128)S(1)}, f32[64,128]{1,0:T(8,128)S(1)}, f32[64,128]{1,0:T(8,128)S(1)}, f32[2,4,2,32,128]{4,3,2,1,0:T(8,128)S(1)}) custom-call(s32[3]{0:T(128)S(1)} %pad_add_fusion.refs_0_.pos_ref, f32[8,128]{1,0:T(8,128)S(1)} %get-tuple-element.28.refs_0_.refs_1_.refs_2_, ...), custom_call_target="tpu_custom_call" | custom-call | flops 3932160 | bytes 524288 | tf_op jit(solution)/shard_map/first_cohort/pallas_call | solution.py:654
  23.0 3.1 %collective-permute-start.5 = (f32[72,256]{1,0:T(8,128)S(1)}, f32[72,256]{1,0:T(8,128)S(1)}, u32[]{:S(2)}, u32[]{:S(2)}) collective-permute-start(f32[72,256]{1,0:T(8,128)S(1)} %bitcast.27), channel_id=1, source_target_pairs={{0,24},{8,0},{16,8},{24,16},{1,25},{9,1},{17,9},{25,17},{2,26},{10... | collective-permute-start | bytes 221192 | tf_op jit(solution)/shard_map/ppermute | solution.py:43
  26.1 1.3 %collective-permute-start.12 = (f32[72,256]{1,0:T(8,128)S(1)}, f32[72,256]{1,0:T(8,128)S(1)}, u32[]{:S(2)}, u32[]{:S(2)}) collective-permute-start(f32[72,256]{1,0:T(8,128)S(1)} %bitcast.28), channel_id=1, source_target_pairs={{0,16},{1,17},{2,18},{3,19},{4,20},{5,21},{6,22},{7,23}} | collective-permute-start | bytes 221192 | tf_op jit(solution)/shard_map/ppermute | solution.py:774
  27.4 1.3 %collective-permute-start.11 = (f32[72,256]{1,0:T(8,128)S(1)}, f32[72,256]{1,0:T(8,128)S(1)}, u32[]{:S(2)}, u32[]{:S(2)}) collective-permute-start(f32[72,256]{1,0:T(8,128)S(1)} %bitcast.29), channel_id=1, source_target_pairs={{0,8},{1,9},{2,10},{3,11},{4,12},{5,13},{6,14},{7,15}} | collective-permute-start | bytes 221192 | tf_op jit(solution)/shard_map/ppermute | solution.py:774
  28.7 0.7 %collective-permute-done.5.refs_6_.refs_29_ = f32[72,256]{1,0:T(8,128)S(1)} collective-permute-done((f32[72,256]{1,0:T(8,128)S(1)}, f32[72,256]{1,0:T(8,128)S(1)}, u32[]{:S(2)}, u32[]{:S(2)}) %collective-permute-start.5) | collective-permute-done | bytes 73760 | tf_op jit(solution)/shard_map/ppermute | solution.py:43
  29.4 2.0 %recruit_edges.1 = (f32[32,64,256]{2,1,0:T(8,128)S(1)}, f32[32,256]{1,0:T(8,128)S(1)}, f32[32,256]{1,0:T(8,128)S(1)}, f32[64,128]{1,0:T(8,128)S(1)}, f32[64,128]...) custom-call(s32[3]{0:T(128)S(1)} %pad_add_fusion.refs_0_.pos_ref, ...), custom_call_target="tpu_custom_call", output_to_operand_aliasing={{0}: (13, {})} | custom-call | flops 8388608 | bytes 4194304 | tf_op jit(solution)/shard_map/recruit_edges/pallas_call | solution.py:315
  31.4 1.3 %collective-permute-start.10 = (f32[64,128]{1,0:T(8,128)S(1)}, f32[64,128]{1,0:T(8,128)S(1)}, u32[]{:S(2)}, u32[]{:S(2)}) collective-permute-start(f32[64,128]{1,0:T(8,128)S(1)} %get-tuple-element.53), channel_id=1, source_target_pairs={{0,1},{1,0},{2,3},{3,2},{4,5},{5,4},{6,7},{7,6},{8,9},{9,8},{10,11... | collective-permute-start | bytes 98312 | tf_op jit(solution)/shard_map/ppermute | solution.py:43
  32.7 2.2 %collective-permute-start.8 = (f32[32,256]{1,0:T(8,128)S(1)}, f32[32,256]{1,0:T(8,128)S(1)}, u32[]{:S(2)}, u32[]{:S(2)}) collective-permute-start(f32[32,256]{1,0:T(8,128)S(1)} %get-tuple-element.49.refs_14_), channel_id=1, source_target_pairs={{0,2},{2,4},{4,6},{6,0},{1,3},{3,5},{5,7},{7,1},{8,10},{10,12},{12... | collective-permute-start | bytes 98312 | tf_op jit(solution)/shard_map/ppermute | solution.py:43
  35.0 1.0 %collective-permute-done.8.refs_18_ = f32[32,256]{1,0:T(8,128)S(1)} collective-permute-done((f32[32,256]{1,0:T(8,128)S(1)}, f32[32,256]{1,0:T(8,128)S(1)}, u32[]{:S(2)}, u32[]{:S(2)}) %collective-permute-start.8) | collective-permute-done | bytes 32800 | tf_op jit(solution)/shard_map/ppermute | solution.py:43
  36.0 2.3 %collective-permute-done.9.refs_19_ = f32[32,256]{1,0:T(8,128)S(1)} collective-permute-done((f32[32,256]{1,0:T(8,128)S(1)}, f32[32,256]{1,0:T(8,128)S(1)}, u32[]{:S(2)}, u32[]{:S(2)}) %collective-permute-start.9) | collective-permute-done | bytes 32800 | tf_op jit(solution)/shard_map/ppermute | solution.py:43
  38.3 6.3 %month_last.1 = (f32[32,64,256]{2,1,0:T(8,128)}, f32[64,256]{1,0:T(8,128)}) custom-call(s32[3]{0:T(128)S(1)} %pad_add_fusion.refs_0_.pos_ref, f32[8,128]{1,0:T(8,128)S(1)} %get-tuple-element.28.refs_0_.refs_1_.refs_2_, f32[8,128]{1,0:T(8,128)S(1)} %get-tuple-element.28.refs_0_.refs_1_.refs_2_, f32[32,64,256]{2,1,0:T(8,128)S(1)} %get-tuple-element.46.refs_3_, ...), custom_call_target="tpu_custom_call" | custom-call | flops 31457280 | bytes 4194304 | tf_op jit(solution)/shard_map/month_last/pallas_call | solution.py:697
  (51 shorter events, 0.2 us)
Async XLA Ops:
  0.6 9.3 %copy-start = (bf16[32,64,256]{2,1,0:T(8,128)(2,1)S(1)}, bf16[32,64,256]{2,1,0:T(8,128)(2,1)}, u32[]{:S(2)}) copy-start(bf16[32,64,256]{2,1,0:T(8,128)(2,1)} %refs_1_.5) | copy-start | bytes 3145732
  1.5 8.4 %collective-permute-start = (f32[64,256]{1,0:T(8,128)S(1)}, f32[64,256]{1,0:T(8,128)S(1)}, u32[]{:S(2)}, u32[]{:S(2)}) collective-permute-start(f32[64,256]{1,0:T(8,128)S(1)} %bitcast_convert_fusion.first_ref._), channel_id=1, source_target_pairs={{0,24},{8,0},{16,8},{24,16},{1,25},{9,1},{17,9},{25,17},{2,26},{10... | collective-permute-start | bytes 196616 | tf_op jit(solution)/shard_map/ppermute | solution.py:43
  5.7 1.6 %copy-start.1 = (bf16[2,32,64,256]{3,2,1,0:T(8,128)(2,1)S(1)}, bf16[2,32,64,256]{3,2,1,0:T(8,128)(2,1)}, u32[]{:S(2)}) copy-start(bf16[2,32,64,256]{3,2,1,0:T(8,128)(2,1)} %saved_ref.1) | copy-start | bytes 6291460
  7.3 0.7 %copy-start.7 = (f32[32]{0:T(128)S(1)}, f32[32]{0:T(128)}, u32[]{:S(2)}) copy-start(f32[32]{0:T(128)} %breed_ref.1) | copy-start | bytes 388
  8.0 1.5 %copy-start.15 = (s32[32,2]{0,1:T(2,128)S(1)}, s32[32,2]{0,1:T(2,128)}, u32[]{:S(2)}) copy-start(s32[32,2]{0,1:T(2,128)} %param.35) | copy-start | bytes 772
  8.0 1.6 %copy-start.14 = (f32[32,2,32]{2,1,0:T(2,128)S(1)}, f32[32,2,32]{2,1,0:T(2,128)}, u32[]{:S(2)}) copy-start(f32[32,2,32]{2,1,0:T(2,128)} %param.31) | copy-start | bytes 24580
  8.0 1.7 %copy-start.16 = (s32[32]{0:T(128)S(1)}, s32[32]{0:T(128)}, u32[]{:S(2)}) copy-start(s32[32]{0:T(128)} %param.34) | copy-start | bytes 388
  8.0 1.7 %copy-start.17 = (s32[32,1]{0,1:T(1,128)S(1)}, s32[32,1]{0,1:T(1,128)}, u32[]{:S(2)}) copy-start(s32[32,1]{0,1:T(1,128)} %param.32) | copy-start | bytes 388
  8.0 1.7 %copy-start.18 = (s32[32]{0:T(128)S(1)}, s32[32]{0:T(128)}, u32[]{:S(2)}) copy-start(s32[32]{0:T(128)} %param.33) | copy-start | bytes 388
  8.0 1.9 %copy-start.3 = (s32[64,256]{1,0:T(8,128)S(1)}, s32[64,256]{1,0:T(8,128)}, u32[]{:S(2)}) copy-start(s32[64,256]{1,0:T(8,128)} %refs_6_.1) | copy-start | bytes 196612
  8.0 1.9 %copy-start.5 = (f32[2,64,256]{2,1,0:T(8,128)S(1)}, f32[2,64,256]{2,1,0:T(8,128)}, u32[]{:S(2)}) copy-start(f32[2,64,256]{2,1,0:T(8,128)} %refs_4_.2) | copy-start | bytes 393220
  8.0 1.9 %copy-start.6 = (f32[2,64,256]{2,1,0:T(8,128)S(1)}, f32[2,64,256]{2,1,0:T(8,128)}, u32[]{:S(2)}) copy-start(f32[2,64,256]{2,1,0:T(8,128)} %refs_5_.2) | copy-start | bytes 393220
  8.0 1.9 %copy-start.8 = (f32[32]{0:T(128)S(1)}, f32[32]{0:T(128)}, u32[]{:S(2)}) copy-start(f32[32]{0:T(128)} %breed_ref.1) | copy-start | bytes 388
  8.0 1.9 %copy-start.9 = (f32[32]{0:T(128)S(1)}, f32[32]{0:T(128)}, u32[]{:S(2)}) copy-start(f32[32]{0:T(128)} %param.25) | copy-start | bytes 388
  8.0 1.9 %copy-start.10 = (f32[32]{0:T(128)S(1)}, f32[32]{0:T(128)}, u32[]{:S(2)}) copy-start(f32[32]{0:T(128)} %param.26) | copy-start | bytes 388
  8.1 1.9 %copy-start.11 = (f32[32]{0:T(128)S(1)}, f32[32]{0:T(128)}, u32[]{:S(2)}) copy-start(f32[32]{0:T(128)} %param.27) | copy-start | bytes 388
  8.1 1.9 %copy-start.12 = (f32[32]{0:T(128)S(1)}, f32[32]{0:T(128)}, u32[]{:S(2)}) copy-start(f32[32]{0:T(128)} %param.28) | copy-start | bytes 388
  8.1 1.9 %copy-start.13 = (f32[32]{0:T(128)S(1)}, f32[32]{0:T(128)}, u32[]{:S(2)}) copy-start(f32[32]{0:T(128)} %param.29) | copy-start | bytes 388
  8.1 6.0 %copy-start.2 = (f32[64,256]{1,0:T(8,128)S(1)}, f32[64,256]{1,0:T(8,128)}, u32[]{:S(2)}) copy-start(f32[64,256]{1,0:T(8,128)} %refs_7_.1) | copy-start | bytes 196612
  9.4 7.7 %collective-permute-start.6 = (f32[3,64,256]{2,1,0:T(8,128)S(1)}, f32[3,64,256]{2,1,0:T(8,128)S(1)}, u32[]{:S(2)}, u32[]{:S(2)}) collective-permute-start(f32[3,64,256]{2,1,0:T(8,128)S(1)} %spawn_parts.1.a_ref), channel_id=1, source_target_pairs={{0,8},{8,0},{16,24},{24,16},{1,9},{9,1},{17,25},{25,17},{2,10},{10... | collective-permute-start | bytes 589832 | tf_op jit(solution)/shard_map/ppermute | solution.py:103
  11.0 5.5 %collective-permute-start.2 = (f32[56,256]{1,0:T(8,128)S(1)}, f32[56,256]{1,0:T(8,128)S(1)}, u32[]{:S(2)}, u32[]{:S(2)}) collective-permute-start(f32[56,256]{1,0:T(8,128)S(1)} %get-tuple-element.37.refs_4_), channel_id=1, source_target_pairs={{0,6},{2,0},{4,2},{6,4},{1,7},{3,1},{5,3},{7,5},{8,14},{10,8},{12,... | collective-permute-start | bytes 172040 | tf_op jit(solution)/shard_map/ppermute | solution.py:43
  12.1 4.5 %collective-permute-start.1 = (f32[56,256]{1,0:T(8,128)S(1)}, f32[56,256]{1,0:T(8,128)S(1)}, u32[]{:S(2)}, u32[]{:S(2)}) collective-permute-start(f32[56,256]{1,0:T(8,128)S(1)} %get-tuple-element.36.refs_8_.refs_0_.refs_3_), channel_id=1, source_target_pairs={{0,2},{2,4},{4,6},{6,0},{1,3},{3,5},{5,7},{7,1},{8,10},{10,12},{12... | collective-permute-start | bytes 172040 | tf_op jit(solution)/shard_map/ppermute | solution.py:43
  13.2 3.3 %collective-permute-start.3 = (f32[16,256]{1,0:T(8,128)S(1)}, f32[16,256]{1,0:T(8,128)S(1)}, u32[]{:S(2)}, u32[]{:S(2)}) collective-permute-start(f32[16,256]{1,0:T(8,128)S(1)} %get-tuple-element.38), channel_id=1, source_target_pairs={{0,4},{2,6},{4,0},{6,2},{1,5},{3,7},{5,1},{7,3},{8,12},{10,14},{12... | collective-permute-start | bytes 49160 | tf_op jit(solution)/shard_map/ppermute | solution.py:43
  17.2 12.2 %collective-permute-start.7 = (f32[3,64,256]{2,1,0:T(8,128)S(1)}, f32[3,64,256]{2,1,0:T(8,128)S(1)}, u32[]{:S(2)}, u32[]{:S(2)}) collective-permute-start(f32[3,64,256]{2,1,0:T(8,128)S(1)} %add_after.1.refs_7_.refs_26_), channel_id=1, source_target_pairs={{0,16},{8,24},{16,0},{24,8},{1,17},{9,25},{17,1},{25,9},{2,18},{10... | collective-permute-start | bytes 589832 | tf_op jit(solution)/shard_map/ppermute | solution.py:103
  17.6 3.8 %collective-permute-start.4 = (f32[192,128]{1,0:T(8,128)S(1)}, f32[192,128]{1,0:T(8,128)S(1)}, u32[]{:S(2)}, u32[]{:S(2)}) collective-permute-start(f32[192,128]{1,0:T(8,128)S(1)} %get-tuple-element.39.refs_8_._), channel_id=1, source_target_pairs={{0,1},{1,0},{2,3},{3,2},{4,5},{5,4},{6,7},{7,6},{8,9},{9,8},{10,11... | collective-permute-start | bytes 294920 | tf_op jit(solution)/shard_map/ppermute | solution.py:43
  21.3 8.0 %copy-start.4 = (f32[64,256]{1,0:T(8,128)S(1)}, f32[64,256]{1,0:T(8,128)}, u32[]{:S(2)}) copy-start(f32[64,256]{1,0:T(8,128)} %refs_8_.1) | copy-start | bytes 196612
  23.0 6.4 %collective-permute-start.5 = (f32[72,256]{1,0:T(8,128)S(1)}, f32[72,256]{1,0:T(8,128)S(1)}, u32[]{:S(2)}, u32[]{:S(2)}) collective-permute-start(f32[72,256]{1,0:T(8,128)S(1)} %bitcast.27), channel_id=1, source_target_pairs={{0,24},{8,0},{16,8},{24,16},{1,25},{9,1},{17,9},{25,17},{2,26},{10... | collective-permute-start | bytes 221192 | tf_op jit(solution)/shard_map/ppermute | solution.py:43
  26.1 8.8 %collective-permute-start.12 = (f32[72,256]{1,0:T(8,128)S(1)}, f32[72,256]{1,0:T(8,128)S(1)}, u32[]{:S(2)}, u32[]{:S(2)}) collective-permute-start(f32[72,256]{1,0:T(8,128)S(1)} %bitcast.28), channel_id=1, source_target_pairs={{0,16},{1,17},{2,18},{3,19},{4,20},{5,21},{6,22},{7,23}} | collective-permute-start | bytes 221192 | tf_op jit(solution)/shard_map/ppermute | solution.py:774
  27.4 7.5 %collective-permute-start.11 = (f32[72,256]{1,0:T(8,128)S(1)}, f32[72,256]{1,0:T(8,128)S(1)}, u32[]{:S(2)}, u32[]{:S(2)}) collective-permute-start(f32[72,256]{1,0:T(8,128)S(1)} %bitcast.29), channel_id=1, source_target_pairs={{0,8},{1,9},{2,10},{3,11},{4,12},{5,13},{6,14},{7,15}} | collective-permute-start | bytes 221192 | tf_op jit(solution)/shard_map/ppermute | solution.py:774
  31.4 3.6 %collective-permute-start.10 = (f32[64,128]{1,0:T(8,128)S(1)}, f32[64,128]{1,0:T(8,128)S(1)}, u32[]{:S(2)}, u32[]{:S(2)}) collective-permute-start(f32[64,128]{1,0:T(8,128)S(1)} %get-tuple-element.53), channel_id=1, source_target_pairs={{0,1},{1,0},{2,3},{3,2},{4,5},{5,4},{6,7},{7,6},{8,9},{9,8},{10,11... | collective-permute-start | bytes 98312 | tf_op jit(solution)/shard_map/ppermute | solution.py:43
  32.7 3.3 %collective-permute-start.8 = (f32[32,256]{1,0:T(8,128)S(1)}, f32[32,256]{1,0:T(8,128)S(1)}, u32[]{:S(2)}, u32[]{:S(2)}) collective-permute-start(f32[32,256]{1,0:T(8,128)S(1)} %get-tuple-element.49.refs_14_), channel_id=1, source_target_pairs={{0,2},{2,4},{4,6},{6,0},{1,3},{3,5},{5,7},{7,1},{8,10},{10,12},{12... | collective-permute-start | bytes 98312 | tf_op jit(solution)/shard_map/ppermute | solution.py:43
  34.9 3.3 %collective-permute-start.9 = (f32[32,256]{1,0:T(8,128)S(1)}, f32[32,256]{1,0:T(8,128)S(1)}, u32[]{:S(2)}, u32[]{:S(2)}) collective-permute-start(f32[32,256]{1,0:T(8,128)S(1)} %get-tuple-element.50.refs_15_), channel_id=1, source_target_pairs={{0,6},{2,0},{4,2},{6,4},{1,7},{3,1},{5,3},{7,5},{8,14},{10,8},{12,... | collective-permute-start | bytes 98312 | tf_op jit(solution)/shard_map/ppermute | solution.py:43
